TPU v7x, 256 devices: a whole 4x4x8 slice. The times are simulated.
256 devices in a mesh: pipe: 4 (over x), seq: 32 (over z, y), batch: 2 (over core).
Axes of the slice: x: 4, y: 4, z: 8, core: 2. Of those that a mesh axis runs over, the one named last changes fastest.
Arguments:
- latent_noise: float32 [4, 2, 512, 64], P('pipe', 'batch', 'seq'), may hold values from -6 to 6
- text_rows: bfloat16 [4, 2, 256, 4096], P(None, 'batch', None, 'seq'), may hold values from -6 to 6
- text_lengths: int32 [4, 2], P(None, 'batch'), may hold values from 32 to 256, as said below
- plan: int32 [3], replicated, may hold values from 1 to 1000, as said below
- context_weight: bfloat16 [4096, 1536], P('seq'), may hold values from -0.09375 to 0.09375
- w_embed: bfloat16 [64, 1536], replicated, may hold values from -0.75 to 0.75
- w_attention: bfloat16 [4, 1536, 4608], P('pipe', 'batch'), may hold values from -1 to 1
- w_project: bfloat16 [4, 1536, 1536], P('pipe', 'batch'), may hold values from -0.15625 to 0.15625
- w_modulate: bfloat16 [4, 256, 4608], P('pipe', 'batch'), may hold values from -0.375 to 0.375
- w_final: bfloat16 [1536, 64], replicated, may hold values from -0.15625 to 0.15625
Outputs:
- final_latent: float32 [4, 2, 512, 64], P('pipe', 'batch', 'seq')
Inputs may be any that keep to these rules, and one draw needn't show every extreme that they name: `text_lengths`: at least one prompt has 256 live rows and one has 32. `plan`: strictly falling; the first entry is 1000 and the last is 1.
All inputs are finite; a program needn't handle non-finite values.
Results may differ from a plain program's by a relative error of at most 0.02.
Values may be sent and summed in bfloat16 or wider, within the bound.
No kernel may reach another device: no remote copies, remote signals or barrier semaphores. Data moves between devices by JAX's collectives and lax.ppermute only.
A program may use at most 128 MiB of HBM per device.

v0:
```python
import functools
import math

import jax
import jax.numpy as jnp
from jax import lax
from jax.experimental import pallas as pl
from jax.experimental.pallas import tpu as pltpu
from jax.sharding import Mesh, PartitionSpec as P

HEADS = 16
HEAD = 96
STEPS = 2
BLOCKS = 4
X, Z, Y, C = 4, 8, 4, 2
AXES = ("x", "z", "y", "c")
BF = jnp.bfloat16
F32 = jnp.float32
VMEM = 26 * 1024 * 1024
SPAN = 768
CHUNKS = 4
TOGETHER = 2

epsilon = 1e-06


def layer_norm(hidden):
    values = hidden.astype(F32)
    center = values - jnp.mean(values, axis=-1, keepdims=True)
    spread = jnp.mean(center * center, axis=-1, keepdims=True)
    return center * lax.rsqrt(spread + epsilon)


def time_features(noise_level, feature_count):
    half_count = feature_count // 2
    wave_frequency = jnp.exp(
        -math.log(10000.0) * jnp.arange(half_count, dtype=F32) / half_count
    )
    angles = noise_level * wave_frequency
    return jnp.concatenate([jnp.cos(angles), jnp.sin(angles)]).astype(BF)


def flat(x, z, y, c):
    return ((x * Z + z) * Y + y) * C + c


def move(value, pairs):
    return lax.ppermute(value, AXES, [(flat(*a), flat(*b)) for a, b in pairs])


def homes():
    return [(z // 2, z, z % 2) for z in range(Z)]


def whole():
    return pl.BlockSpec(memory_space=pltpu.VMEM)


def scalar():
    return pl.BlockSpec(memory_space=pltpu.SMEM)


def params():
    return pltpu.CompilerParams(vmem_limit_bytes=VMEM)


def joined_kernel(core_ref, own_ref, other_ref, out_ref, sems):
    half = own_ref.shape[0]
    core = core_ref[0]
    copies = (
        pltpu.make_async_copy(
            own_ref, out_ref.at[pl.ds(pl.multiple_of(core * half, 16), half), :], sems.at[0]
        ),
        pltpu.make_async_copy(
            other_ref, out_ref.at[pl.ds(pl.multiple_of((1 - core) * half, 16), half), :], sems.at[1]
        ),
    )
    for copy in copies:
        copy.start()
    for copy in copies:
        copy.wait()


def joined(core, own, other):
    half, columns = own.shape
    return pl.pallas_call(
        joined_kernel,
        in_specs=[scalar(), pl.BlockSpec(memory_space=pl.ANY), pl.BlockSpec(memory_space=pl.ANY)],
        out_specs=whole(),
        out_shape=jax.ShapeDtypeStruct((2 * half, columns), BF),
        scratch_shapes=[pltpu.SemaphoreType.DMA((2,))],
        compiler_params=params(),
        name="joined",
    )(core, own, other)


def product_kernel(rows_ref, shift_ref, scale_ref, weight_ref, out_ref, normed, *, norm, column):
    count = rows_ref.shape[0]
    step = min(count, 64)
    if norm:

        def body(i, carry):
            there = pl.ds(pl.multiple_of(i * step, step), step)
            values = rows_ref[there, :].astype(F32)
            center = values - jnp.mean(values, axis=-1, keepdims=True)
            spread = jnp.mean(center * center, axis=-1, keepdims=True)
            values = center * lax.rsqrt(spread + epsilon)
            normed[there, :] = (values * (1.0 + scale_ref[...]) + shift_ref[...]).astype(BF)
            return carry

        lax.fori_loop(0, count // step, body, 0, unroll=True)
        source = normed
    else:
        source = rows_ref
    for i in range(out_ref.shape[1] // SPAN):
        there = slice(i * SPAN, (i + 1) * SPAN)
        here = slice(column + i * SPAN, column + (i + 1) * SPAN)
        out_ref[:, there] = jnp.dot(
            source[...], weight_ref[:, here], preferred_element_type=F32
        ).astype(BF)


def product(rows, shift, scale, weight, column, norm):
    count, width = rows.shape
    columns = weight.shape[1] - column
    return pl.pallas_call(
        functools.partial(product_kernel, norm=norm, column=column),
        in_specs=[whole()] * 4,
        out_specs=whole(),
        out_shape=jax.ShapeDtypeStruct((count, columns), BF),
        scratch_shapes=[pltpu.VMEM((count, width), BF)],
        compiler_params=params(),
        name="product",
    )(rows, shift, scale, weight)


def attention_kernel(*refs, queries, blocks):
    projected, refs = refs[:blocks], refs[blocks:]
    text_ref, bias_ref, gate_ref, weight_ref, *refs = refs
    hidden_refs, out_refs, attended = refs[: len(queries)], refs[len(queries) : -1], refs[-1]
    inner = weight_ref.shape[0]
    factor = math.log2(math.e) / math.sqrt(HEAD)
    lanes = lax.broadcasted_iota(jnp.int32, (1, 128), 1)
    wide = lax.broadcasted_iota(jnp.int32, (1, 256), 1)
    bias = bias_ref[...]
    contract = (((1,), (1,)), ((), ()))

    def group(g, carry):
        base = pl.multiple_of(g * 4 * HEAD, 128)
        outs = []
        for h in range(4):
            low, high = h * HEAD, (h + 1) * HEAD
            start, stop = low // 128 * 128, -(-high // 128) * 128
            width = stop - start

            def window(refs, offset):
                there = pl.ds(pl.multiple_of(base + start + offset, 128), width)
                return jnp.concatenate([ref[:, there] for ref in refs], 0)

            index = lanes if width == 128 else wide
            mask = ((index >= low - start) & (index < high - start)).astype(F32).astype(BF)
            q = window([projected[i] for i in queries], 0) * mask
            image = lax.dot_general(
                q, window(projected, inner), contract, preferred_element_type=F32
            )
            text = lax.dot_general(
                q, window([text_ref], 0), contract, preferred_element_type=F32
            )
            text = text + bias
            top = jnp.maximum(
                jnp.max(image, axis=-1, keepdims=True), jnp.max(text, axis=-1, keepdims=True)
            )
            image = jnp.exp2((image - top) * factor)
            text = jnp.exp2((text - top) * factor)
            total = jnp.sum(image, axis=-1, keepdims=True) + jnp.sum(text, axis=-1, keepdims=True)
            value = jnp.dot(
                image.astype(BF), window(projected, 2 * inner), preferred_element_type=F32
            ) + jnp.dot(
                text.astype(BF), window([text_ref], inner), preferred_element_type=F32
            )
            outs.append(value * (1.0 / total))
        tiles = (
            jnp.where(lanes < 96, outs[0], outs[1][:, :128]),
            jnp.where(lanes < 64, outs[1][:, 128:], outs[2][:, :128]),
            jnp.where(lanes < 32, outs[2][:, 128:], outs[3]),
        )
        for j, tile in enumerate(tiles):
            attended[:, pl.ds(pl.multiple_of(base + j * 128, 128), 128)] = tile.astype(BF)
        return carry

    lax.fori_loop(0, inner // (4 * HEAD), group, 0)
    for i in range(weight_ref.shape[1] // SPAN):
        there = slice(i * SPAN, (i + 1) * SPAN)
        update = gate_ref[:, there] * jnp.dot(
            attended[...], weight_ref[:, there], preferred_element_type=F32
        )
        done = 0
        for hidden_ref, out_ref in zip(hidden_refs, out_refs):
            count = hidden_ref.shape[0]
            part = update[done : done + count]
            out_ref[:, there] = (hidden_ref[:, there].astype(F32) + part).astype(BF)
            done += count


def attention(projected, text, bias, gate, weight, hidden, queries):
    hidden = [hidden[i] for i in queries]
    rows = sum(part.shape[0] for part in hidden)
    return pl.pallas_call(
        functools.partial(attention_kernel, queries=queries, blocks=len(projected)),
        in_specs=[whole()] * (len(projected) + 4 + len(hidden)),
        out_specs=[whole()] * len(hidden),
        out_shape=[jax.ShapeDtypeStruct(part.shape, BF) for part in hidden],
        scratch_shapes=[pltpu.VMEM((rows, weight.shape[0]), BF)],
        compiler_params=params(),
        name="attention",
    )(*projected, text, bias, gate, weight, *hidden)


def on_device(
    latent_noise,
    text_rows,
    text_lengths,
    plan,
    context_weight,
    w_embed,
    w_attention,
    w_project,
    w_modulate,
    w_final,
):
    x, z, y, c = (lax.axis_index(name) for name in AXES)
    width = w_embed.shape[1]
    latent_width = latent_noise.shape[3]
    rows_here = latent_noise.shape[2]
    patches = rows_here * Z * Y
    text_total = text_rows.shape[2]
    core = jnp.reshape(c, (1,)).astype(jnp.int32)
    image = z // 2

    def across(value):
        return move(
            value, [((a, b, 0, 1 - b % C), (a, b, 0, b % C)) for a in range(X) for b in range(Z)]
        )

    def hop(value, source, target):
        return move(value, [((source, b, 0, d), (target, b, 0, d)) for _, b, d in homes()])

    attn_weight = joined(core, w_attention[0], across(w_attention[0]))
    proj_weight = joined(core, w_project[0], across(w_project[0]))
    levels = plan.astype(F32)
    mod_rows = w_modulate.shape[1]
    features = jnp.stack([time_features(levels[k], C * mod_rows) for k in range(STEPS)])
    features = lax.dynamic_slice_in_dim(features, c * mod_rows, mod_rows, 1)
    modulation = jnp.dot(features, w_modulate[0], preferred_element_type=F32)
    modulation = modulation + across(modulation)

    text = lax.dynamic_index_in_dim(text_rows[:, 0], x, 0, keepdims=False)
    partial = jnp.dot(text, context_weight, preferred_element_type=F32).astype(BF)
    quarter = text_total // Y
    eighth = quarter // Z
    parts = lax.all_to_all(
        partial.reshape(Y, quarter, width), "y", split_axis=0, concat_axis=0, tiled=True
    )
    summed = jnp.sum(parts.astype(F32), axis=0).astype(BF)
    parts = lax.all_to_all(
        summed.reshape(Z, eighth, width), "z", split_axis=0, concat_axis=0, tiled=True
    )
    summed = jnp.sum(parts.astype(F32), axis=0).astype(BF)

    latent = latent_noise[0, 0].reshape(-1)
    high = latent.astype(BF)
    low = (latent - high.astype(F32)).astype(BF)
    both = jnp.concatenate([high, low])
    tail = -(-both.size // width)
    piece = jnp.concatenate(
        [summed, jnp.pad(both, (0, tail * width - both.size)).reshape(tail, width)], 0
    )
    held = eighth + tail
    shared = lax.all_to_all(
        jnp.broadcast_to(piece[None], (X, held, width)), "x", split_axis=0, concat_axis=0, tiled=True
    )
    shared = jnp.repeat(shared, Z // X, axis=0)
    shared = lax.all_to_all(shared, "z", split_axis=0, concat_axis=0, tiled=True)
    pieces = [shared.reshape(Z * held, width)]
    for k in range(1, Y):
        pieces.append(
            move(
                pieces[0],
                [((a, b, k, b % C), (a, b, 0, b % C)) for a in range(X) for b in range(Z)],
            )
        )
    pieces = jnp.stack(pieces).reshape(Y, Z, held, width)
    context = pieces[:, :, :eighth].reshape(text_total, width)
    latents = pieces[:, :, eighth:].reshape(Y, Z, tail * width)[:, :, : both.size]
    latents = latents.reshape(Y, Z, 2, rows_here, latent_width)
    latents = jnp.transpose(latents, (2, 1, 0, 3, 4)).reshape(2, patches, latent_width)
    latent = latents[0].astype(F32) + latents[1].astype(F32)

    length = jnp.sum(jnp.where(jnp.arange(X) == image, text_lengths[:, 0], 0))
    bias = jnp.where(jnp.arange(text_total) < length, 0.0, -1e30).astype(F32)[None, :]
    nothing = jnp.zeros((1, width), F32)
    keys = product(context, nothing, nothing, attn_weight, width, False)

    rows = patches // CHUNKS

    def embedded(value):
        return [
            jnp.dot(
                value[i * rows : (i + 1) * rows], w_embed, preferred_element_type=F32
            ).astype(BF)
            for i in range(CHUNKS)
        ]

    hidden = embedded(latents[0])
    for turn in range(STEPS * BLOCKS):
        step, block = divmod(turn, BLOCKS)
        shift = modulation[step : step + 1, :width]
        scale = modulation[step : step + 1, width : 2 * width]
        gate = modulation[step : step + 1, 2 * width :]
        projected = [product(part, shift, scale, attn_weight, 0, True) for part in hidden]
        following = []
        for i in range(0, CHUNKS, TOGETHER):
            queries = tuple(range(i, i + TOGETHER))
            if following:
                bound, following = lax.optimization_barrier((gate, following))
            else:
                bound = gate
            following = following + list(
                attention(projected, keys, bias, bound, proj_weight, hidden, queries)
            )
        hidden = following
        if block < BLOCKS - 1:
            hidden = [hop(part, block, block + 1) for part in hidden]
        else:
            final = jnp.concatenate(hidden, 0)
            velocity = jnp.dot(
                layer_norm(final).astype(BF), w_final, preferred_element_type=F32
            )
            latent = latent + (levels[step + 1] - levels[step]) / 1000.0 * velocity
            if step < STEPS - 1:
                hidden = embedded(hop(latent.astype(BF), block, 0))

    last = BLOCKS - 1
    latent = latent.reshape(patches * latent_width // 128, 128)
    moved = move(latent, [((last, b, 0, d), (m, b, 0, d)) for m, b, d in homes() if m != last])
    latent = jnp.where(x == last, latent, moved)
    spread = lax.all_to_all(
        latent.reshape(Z * Y, rows_here * latent_width // 128, 128),
        ("z", "y"),
        split_axis=0,
        concat_axis=0,
        tiled=True,
    )
    mine = lax.dynamic_index_in_dim(spread, (2 * x + c) * Y, 0, keepdims=False)
    return mine.reshape(latent_noise.shape)


def solution(mesh):
    inner = Mesh(mesh.devices.reshape(X, Z, Y, C), AXES)
    seq = ("z", "y")
    placed = (
        P("x", "c", seq, None),
        P(None, "c", None, seq),
        P(None, "c"),
        P(),
        P(seq, None),
        P(),
        P("x", "c", None),
        P("x", "c", None),
        P("x", "c", None),
        P(),
    )
    return jax.shard_map(
        on_device,
        mesh=inner,
        in_specs=placed,
        out_specs=P("x", "c", seq, None),
        check_vma=False,
    )
```

profile of v0, /device:TPU:2, one launch (start us, length us, event | category | flops | bytes accessed | tf_op | source)
XLA Modules:
  0.0 417.9 jit_solution(2554570131222019079)
XLA Ops:
  3.7 6.8 %all-to-all-start = ((bf16[4,64,1536]{2,1,0:T(8,128)(2,1)}), bf16[4,64,1536]{2,1,0:T(8,128)(2,1)S(1)}, u32[]{:S(2)}, u32[]{:S(2)}) async-start(bf16[4,64,1536]{2,1,0:T(8,128)(2,1)} %bitcast.1), calls=%async_computation | async-start | bytes 1572864 | tf_op jit(solution)/shard_map/all_to_all | solution.py:261
  11.9 12.1 %all-to-all-done = bf16[4,64,1536]{2,1,0:T(8,128)(2,1)S(1)} async-done(((bf16[4,64,1536]{2,1,0:T(8,128)(2,1)}), bf16[4,64,1536]{2,1,0:T(8,128)(2,1)S(1)}, u32[]{:S(2)}, u32[]{:S(2)}) %all-to-all-start) | async-done | bytes 786464 | tf_op jit(solution)/shard_map/all_to_all | solution.py:261
  24.8 8.5 %all-to-all-start.1 = ((bf16[8,8,1536]{2,1,0:T(8,128)(2,1)}), bf16[8,8,1536]{2,1,0:T(8,128)(2,1)S(1)}, u32[]{:S(2)}, u32[]{:S(2)}) async-start(bf16[8,8,1536]{2,1,0:T(8,128)(2,1)} %bitcast.2), calls=%async_computation.1 | async-start | bytes 393216 | tf_op jit(solution)/shard_map/all_to_all | solution.py:265
  34.6 9.2 %all-to-all-done.1 = bf16[8,8,1536]{2,1,0:T(8,128)(2,1)S(1)} async-done(((bf16[8,8,1536]{2,1,0:T(8,128)(2,1)}), bf16[8,8,1536]{2,1,0:T(8,128)(2,1)S(1)}, u32[]{:S(2)}, u32[]{:S(2)}) %all-to-all-start.1) | async-done | bytes 196640 | tf_op jit(solution)/shard_map/all_to_all | solution.py:265
  44.6 5.0 %all-to-all-start.2 = ((bf16[4,10,1536]{2,1,0:T(8,128)(2,1)}), bf16[4,10,1536]{2,1,0:T(8,128)(2,1)S(1)}, u32[]{:S(2)}, u32[]{:S(2)}) async-start(bf16[4,10,1536]{2,1,0:T(8,128)(2,1)} %broadcast_in_dim.29), calls=%async_computation.2 | async-start | bytes 393216 | tf_op jit(solution)/shard_map/all_to_all | solution.py:279
  50.3 4.1 all-to-all-done.2
  62.1 8.3 %all-to-all-done.3 = bf16[8,10,1536]{2,1,0:T(8,128)(2,1)S(1)} async-done(((bf16[8,10,1536]{2,1,0:T(8,128)(2,1)}), bf16[8,10,1536]{2,1,0:T(8,128)(2,1)S(1)}, u32[]{:S(2)}, u32[]{:S(2)}) %all-to-all-start.3) | async-done | bytes 245792 | tf_op jit(solution)/shard_map/all_to_all | solution.py:283
  74.5 8.0 %collective-permute-done.2 = bf16[80,1536]{1,0:T(8,128)(2,1)S(1)} collective-permute-done((bf16[80,1536]{1,0:T(8,128)(2,1)S(1)}, bf16[80,1536]{1,0:T(8,128)(2,1)S(1)}, u32[]{:S(2)}, u32[]{:S(2)}) %collective-permute-start.2) | collective-permute-done | bytes 245792 | tf_op jit(solution)/shard_map/ppermute | solution.py:48
  87.2 4.7 %copy-done.6 = bf16[1,768,4608]{2,1,0:T(8,128)(2,1)S(1)} copy-done((bf16[1,768,4608]{2,1,0:T(8,128)(2,1)S(1)}, bf16[1,768,4608]{2,1,0:T(8,128)(2,1)}, u32[]{:S(2)}) %copy-start.6) | copy-done | bytes 7077912
  91.9 3.6 joined.2.weight_ref
  107.4 7.6 %attention.16 = (bf16[128,1536]{1,0:T(8,128)(2,1)S(1)}, bf16[128,1536]{1,0:T(8,128)(2,1)S(1)}) custom-call(bf16[128,4608]{1,0:T(8,128)(2,1)S(1)} %product.33.refs_0_, bf16[128,4608]{1,0:T(8,128)(2,1)S(1)} %product.34.refs_1_, bf16[128,4608]{1,0:T(8,128)(2,1)S(1)} %product.35.refs_2_, bf16[128,4608]{1,0:T(8,128)(2,1)S(1)} %product.36.refs_3_, ...), custom_call_target="tpu_custom_call" | custom-call | tf_op jit(solution)/shard_map/attention/pallas_call | solution.py:208
  115.0 7.8 %attention.17 = (bf16[128,1536]{1,0:T(8,128)(2,1)S(1)}, bf16[128,1536]{1,0:T(8,128)(2,1)S(1)}) custom-call(bf16[128,4608]{1,0:T(8,128)(2,1)S(1)} %product.33.refs_0_, bf16[128,4608]{1,0:T(8,128)(2,1)S(1)} %product.34.refs_1_, bf16[128,4608]{1,0:T(8,128)(2,1)S(1)} %product.35.refs_2_, bf16[128,4608]{1,0:T(8,128)(2,1)S(1)} %product.36.refs_3_, ...), custom_call_target="tpu_custom_call" | custom-call | tf_op jit(solution)/shard_map/attention/pallas_call | solution.py:208
  128.0 4.5 %collective-permute-done.9.rows_ref.refs_9_ = bf16[128,1536]{1,0:T(8,128)(2,1)S(1)} collective-permute-done((bf16[128,1536]{1,0:T(8,128)(2,1)S(1)}, bf16[128,1536]{1,0:T(8,128)(2,1)S(1)}, u32[]{:S(2)}, u32[]{:S(2)}) %collective-permute-start.9) | collective-permute-done | bytes 393248 | tf_op jit(solution)/shard_map/ppermute | solution.py:48
  147.4 8.0 %attention.18 = (bf16[128,1536]{1,0:T(8,128)(2,1)S(1)}, bf16[128,1536]{1,0:T(8,128)(2,1)S(1)}) custom-call(bf16[128,4608]{1,0:T(8,128)(2,1)S(1)} %product.38.refs_0_, bf16[128,4608]{1,0:T(8,128)(2,1)S(1)} %product.39.refs_1_, bf16[128,4608]{1,0:T(8,128)(2,1)S(1)} %product.40.refs_2_, bf16[128,4608]{1,0:T(8,128)(2,1)S(1)} %product.41.refs_3_, ...), custom_call_target="tpu_custom_call" | custom-call | tf_op jit(solution)/shard_map/attention/pallas_call | solution.py:208
  155.5 7.6 %attention.19 = (bf16[128,1536]{1,0:T(8,128)(2,1)S(1)}, bf16[128,1536]{1,0:T(8,128)(2,1)S(1)}) custom-call(bf16[128,4608]{1,0:T(8,128)(2,1)S(1)} %product.38.refs_0_, bf16[128,4608]{1,0:T(8,128)(2,1)S(1)} %product.39.refs_1_, bf16[128,4608]{1,0:T(8,128)(2,1)S(1)} %product.40.refs_2_, bf16[128,4608]{1,0:T(8,128)(2,1)S(1)} %product.41.refs_3_, ...), custom_call_target="tpu_custom_call" | custom-call | tf_op jit(solution)/shard_map/attention/pallas_call | solution.py:208
  184.6 8.5 %attention.20 = (bf16[128,1536]{1,0:T(8,128)(2,1)}, bf16[128,1536]{1,0:T(8,128)(2,1)S(1)}) custom-call(bf16[128,4608]{1,0:T(8,128)(2,1)S(1)} %product.42.refs_0_, bf16[128,4608]{1,0:T(8,128)(2,1)S(1)} %product.43.refs_1_, bf16[128,4608]{1,0:T(8,128)(2,1)S(1)} %product.44.refs_2_, bf16[128,4608]{1,0:T(8,128)(2,1)S(1)} %product.45.refs_3_, ...), custom_call_target="tpu_custom_call" | custom-call | tf_op jit(solution)/shard_map/attention/pallas_call | solution.py:208
  193.1 8.5 %attention.21 = (bf16[128,1536]{1,0:T(8,128)(2,1)}, bf16[128,1536]{1,0:T(8,128)(2,1)}) custom-call(bf16[128,4608]{1,0:T(8,128)(2,1)S(1)} %product.42.refs_0_, bf16[128,4608]{1,0:T(8,128)(2,1)S(1)} %product.43.refs_1_, bf16[128,4608]{1,0:T(8,128)(2,1)S(1)} %product.44.refs_2_, bf16[128,4608]{1,0:T(8,128)(2,1)S(1)} %product.45.refs_3_, ...), custom_call_target="tpu_custom_call" | custom-call | tf_op jit(solution)/shard_map/attention/pallas_call | solution.py:208
  209.4 5.0 %copy-done.3 = bf16[1536,4608]{1,0:T(8,128)(2,1)S(1)} copy-done((bf16[1536,4608]{1,0:T(8,128)(2,1)S(1)}, bf16[1536,4608]{1,0:T(8,128)(2,1)}, u32[]{:S(2)}) %copy-start.3) | copy-done | bytes 14155800
  226.5 9.0 %attention.22 = (bf16[128,1536]{1,0:T(8,128)(2,1)S(1)}, bf16[128,1536]{1,0:T(8,128)(2,1)S(1)}) custom-call(bf16[128,4608]{1,0:T(8,128)(2,1)S(1)} %product.46.refs_0_, bf16[128,4608]{1,0:T(8,128)(2,1)S(1)} %product.47.refs_1_, bf16[128,4608]{1,0:T(8,128)(2,1)S(1)} %product.48.refs_2_, bf16[128,4608]{1,0:T(8,128)(2,1)S(1)} %product.49.refs_3_, ...), custom_call_target="tpu_custom_call" | custom-call | tf_op jit(solution)/shard_map/attention/pallas_call | solution.py:208
  235.6 7.6 %attention.23 = (bf16[128,1536]{1,0:T(8,128)(2,1)S(1)}, bf16[128,1536]{1,0:T(8,128)(2,1)S(1)}) custom-call(bf16[128,4608]{1,0:T(8,128)(2,1)S(1)} %product.46.refs_0_, bf16[128,4608]{1,0:T(8,128)(2,1)S(1)} %product.47.refs_1_, bf16[128,4608]{1,0:T(8,128)(2,1)S(1)} %product.48.refs_2_, bf16[128,4608]{1,0:T(8,128)(2,1)S(1)} %product.49.refs_3_, ...), custom_call_target="tpu_custom_call" | custom-call | tf_op jit(solution)/shard_map/attention/pallas_call | solution.py:208
  256.9 8.1 %attention.24 = (bf16[128,1536]{1,0:T(8,128)(2,1)S(1)}, bf16[128,1536]{1,0:T(8,128)(2,1)S(1)}) custom-call(bf16[128,4608]{1,0:T(8,128)(2,1)S(1)} %product.50.refs_0_, bf16[128,4608]{1,0:T(8,128)(2,1)S(1)} %product.51.refs_1_, bf16[128,4608]{1,0:T(8,128)(2,1)S(1)} %product.52.refs_2_, bf16[128,4608]{1,0:T(8,128)(2,1)S(1)} %product.53.refs_3_, ...), custom_call_target="tpu_custom_call" | custom-call | tf_op jit(solution)/shard_map/attention/pallas_call | solution.py:208
  265.0 7.6 %attention.25 = (bf16[128,1536]{1,0:T(8,128)(2,1)S(1)}, bf16[128,1536]{1,0:T(8,128)(2,1)S(1)}) custom-call(bf16[128,4608]{1,0:T(8,128)(2,1)S(1)} %product.50.refs_0_, bf16[128,4608]{1,0:T(8,128)(2,1)S(1)} %product.51.refs_1_, bf16[128,4608]{1,0:T(8,128)(2,1)S(1)} %product.52.refs_2_, bf16[128,4608]{1,0:T(8,128)(2,1)S(1)} %product.53.refs_3_, ...), custom_call_target="tpu_custom_call" | custom-call | tf_op jit(solution)/shard_map/attention/pallas_call | solution.py:208
  278.0 8.8 %collective-permute-done.22.rows_ref.refs_9_ = bf16[128,1536]{1,0:T(8,128)(2,1)S(1)} collective-permute-done((bf16[128,1536]{1,0:T(8,128)(2,1)S(1)}, bf16[128,1536]{1,0:T(8,128)(2,1)S(1)}, u32[]{:S(2)}, u32[]{:S(2)}) %collective-permute-start.22) | collective-permute-done | bytes 393248 | tf_op jit(solution)/shard_map/ppermute | solution.py:48
  301.7 7.8 %attention.26 = (bf16[128,1536]{1,0:T(8,128)(2,1)S(1)}, bf16[128,1536]{1,0:T(8,128)(2,1)S(1)}) custom-call(bf16[128,4608]{1,0:T(8,128)(2,1)S(1)} %product.54.refs_0_, bf16[128,4608]{1,0:T(8,128)(2,1)S(1)} %product.55.refs_1_, bf16[128,4608]{1,0:T(8,128)(2,1)S(1)} %product.56.refs_2_, bf16[128,4608]{1,0:T(8,128)(2,1)S(1)} %product.57.refs_3_, ...), custom_call_target="tpu_custom_call" | custom-call | tf_op jit(solution)/shard_map/attention/pallas_call | solution.py:208
  309.6 7.6 %attention.27 = (bf16[128,1536]{1,0:T(8,128)(2,1)S(1)}, bf16[128,1536]{1,0:T(8,128)(2,1)S(1)}) custom-call(bf16[128,4608]{1,0:T(8,128)(2,1)S(1)} %product.54.refs_0_, bf16[128,4608]{1,0:T(8,128)(2,1)S(1)} %product.55.refs_1_, bf16[128,4608]{1,0:T(8,128)(2,1)S(1)} %product.56.refs_2_, bf16[128,4608]{1,0:T(8,128)(2,1)S(1)} %product.57.refs_3_, ...), custom_call_target="tpu_custom_call" | custom-call | tf_op jit(solution)/shard_map/attention/pallas_call | solution.py:208
  338.7 8.8 %attention.28 = (bf16[128,1536]{1,0:T(8,128)(2,1)}, bf16[128,1536]{1,0:T(8,128)(2,1)}) custom-call(bf16[128,4608]{1,0:T(8,128)(2,1)S(1)} %product.58.refs_0_, bf16[128,4608]{1,0:T(8,128)(2,1)S(1)} %product.59.refs_1_, bf16[128,4608]{1,0:T(8,128)(2,1)S(1)} %product.60.refs_2_, bf16[128,4608]{1,0:T(8,128)(2,1)S(1)} %product.61.refs_3_, ...), custom_call_target="tpu_custom_call" | custom-call | tf_op jit(solution)/shard_map/attention/pallas_call | solution.py:208
  347.5 8.5 %attention.29 = (bf16[128,1536]{1,0:T(8,128)(2,1)}, bf16[128,1536]{1,0:T(8,128)(2,1)}) custom-call(bf16[128,4608]{1,0:T(8,128)(2,1)S(1)} %product.58.refs_0_, bf16[128,4608]{1,0:T(8,128)(2,1)S(1)} %product.59.refs_1_, bf16[128,4608]{1,0:T(8,128)(2,1)S(1)} %product.60.refs_2_, bf16[128,4608]{1,0:T(8,128)(2,1)S(1)} %product.61.refs_3_, ...), custom_call_target="tpu_custom_call" | custom-call | tf_op jit(solution)/shard_map/attention/pallas_call | solution.py:208
  360.5 5.0 %copy-done.4 = bf16[1536,4608]{1,0:T(8,128)(2,1)S(1)} copy-done((bf16[1536,4608]{1,0:T(8,128)(2,1)S(1)}, bf16[1536,4608]{1,0:T(8,128)(2,1)}, u32[]{:S(2)}) %copy-start.4) | copy-done | bytes 14155800
  374.8 7.8 %attention.30 = (bf16[128,1536]{1,0:T(8,128)(2,1)S(1)}, bf16[128,1536]{1,0:T(8,128)(2,1)S(1)}) custom-call(bf16[128,4608]{1,0:T(8,128)(2,1)S(1)} %product.62.refs_0_, bf16[128,4608]{1,0:T(8,128)(2,1)S(1)} %product.63.refs_1_, bf16[128,4608]{1,0:T(8,128)(2,1)S(1)} %product.64.refs_2_, bf16[128,4608]{1,0:T(8,128)(2,1)S(1)} %product.65.refs_3_, ...), custom_call_target="tpu_custom_call" | custom-call | tf_op jit(solution)/shard_map/attention/pallas_call | solution.py:208
  382.5 7.6 %attention.31 = (bf16[128,1536]{1,0:T(8,128)(2,1)S(1)}, bf16[128,1536]{1,0:T(8,128)(2,1)S(1)}) custom-call(bf16[128,4608]{1,0:T(8,128)(2,1)S(1)} %product.62.refs_0_, bf16[128,4608]{1,0:T(8,128)(2,1)S(1)} %product.63.refs_1_, bf16[128,4608]{1,0:T(8,128)(2,1)S(1)} %product.64.refs_2_, bf16[128,4608]{1,0:T(8,128)(2,1)S(1)} %product.65.refs_3_, ...), custom_call_target="tpu_custom_call" | custom-call | tf_op jit(solution)/shard_map/attention/pallas_call | solution.py:208
  393.6 13.0 %all-to-all-start.4 = ((f32[32,8,128]{2,1,0:T(8,128)}), f32[32,8,128]{2,1,0:T(8,128)S(1)}, u32[]{:S(2)}, u32[]{:S(2)}) async-start(f32[32,8,128]{2,1,0:T(8,128)} %select_bitcast_fusion), calls=%async_computation.4 | async-start | bytes 262144 | tf_op jit(solution)/shard_map/all_to_all | solution.py:347
  406.6 10.5 %all-to-all-done.4 = f32[32,8,128]{2,1,0:T(8,128)S(1)} async-done(((f32[32,8,128]{2,1,0:T(8,128)}), f32[32,8,128]{2,1,0:T(8,128)S(1)}, u32[]{:S(2)}, u32[]{:S(2)}) %all-to-all-start.4) | async-done | bytes 131104 | tf_op jit(solution)/shard_map/all_to_all | solution.py:347
  (212 shorter events, 168.3 us)
Async XLA Ops:
  0.0 87.2 %collective-permute-start.4 = (bf16[768,4608]{1,0:T(8,128)(2,1)}, bf16[768,4608]{1,0:T(8,128)(2,1)}, u32[]{:S(2)}, u32[]{:S(2)}) collective-permute-start(bf16[768,4608]{1,0:T(8,128)(2,1)} %bitcast.58), channel_id=1, source_target_pairs={{1,0},{8,9},{17,16},{24,25},{33,32},{40,41},{49,48},{56,57},{65,64... | collective-permute-start | bytes 21233672 | tf_op jit(solution)/shard_map/ppermute | solution.py:48
  3.7 20.3 %all-to-all-start = ((bf16[4,64,1536]{2,1,0:T(8,128)(2,1)}), bf16[4,64,1536]{2,1,0:T(8,128)(2,1)S(1)}, u32[]{:S(2)}, u32[]{:S(2)}) async-start(bf16[4,64,1536]{2,1,0:T(8,128)(2,1)} %bitcast.1), calls=%async_computation | async-start | bytes 1572864 | tf_op jit(solution)/shard_map/all_to_all | solution.py:261
  10.5 74.3 %collective-permute-start.5 = (bf16[768,1536]{1,0:T(8,128)(2,1)}, bf16[768,1536]{1,0:T(8,128)(2,1)}, u32[]{:S(2)}, u32[]{:S(2)}) collective-permute-start(bf16[768,1536]{1,0:T(8,128)(2,1)} %bitcast.22.own_ref), channel_id=1, source_target_pairs={{1,0},{8,9},{17,16},{24,25},{33,32},{40,41},{49,48},{56,57},{65,64... | collective-permute-start | bytes 7077896 | tf_op jit(solution)/shard_map/ppermute | solution.py:48
  24.8 19.0 %all-to-all-start.1 = ((bf16[8,8,1536]{2,1,0:T(8,128)(2,1)}), bf16[8,8,1536]{2,1,0:T(8,128)(2,1)S(1)}, u32[]{:S(2)}, u32[]{:S(2)}) async-start(bf16[8,8,1536]{2,1,0:T(8,128)(2,1)} %bitcast.2), calls=%async_computation.1 | async-start | bytes 393216 | tf_op jit(solution)/shard_map/all_to_all | solution.py:265
  44.6 9.8 %all-to-all-start.2 = ((bf16[4,10,1536]{2,1,0:T(8,128)(2,1)}), bf16[4,10,1536]{2,1,0:T(8,128)(2,1)S(1)}, u32[]{:S(2)}, u32[]{:S(2)}) async-start(bf16[4,10,1536]{2,1,0:T(8,128)(2,1)} %broadcast_in_dim.29), calls=%async_computation.2 | async-start | bytes 393216 | tf_op jit(solution)/shard_map/all_to_all | solution.py:279
  55.2 15.3 %all-to-all-start.3 = ((bf16[8,10,1536]{2,1,0:T(8,128)(2,1)}), bf16[8,10,1536]{2,1,0:T(8,128)(2,1)S(1)}, u32[]{:S(2)}, u32[]{:S(2)}) async-start(bf16[8,10,1536]{2,1,0:T(8,128)(2,1)} %bitcast.3), calls=%async_computation.3 | async-start | bytes 786432 | tf_op jit(solution)/shard_map/all_to_all | solution.py:283
  70.6 11.9 %collective-permute-start.2 = (bf16[80,1536]{1,0:T(8,128)(2,1)S(1)}, bf16[80,1536]{1,0:T(8,128)(2,1)S(1)}, u32[]{:S(2)}, u32[]{:S(2)}) collective-permute-start(bf16[80,1536]{1,0:T(8,128)(2,1)S(1)} %reshape.149), channel_id=1, source_target_pairs={{6,0},{15,9},{22,16},{31,25},{38,32},{47,41},{54,48},{63,57},{70,6... | collective-permute-start | bytes 737288 | tf_op jit(solution)/shard_map/ppermute | solution.py:48
  71.9 10.7 %collective-permute-start.1 = (bf16[80,1536]{1,0:T(8,128)(2,1)S(1)}, bf16[80,1536]{1,0:T(8,128)(2,1)S(1)}, u32[]{:S(2)}, u32[]{:S(2)}) collective-permute-start(bf16[80,1536]{1,0:T(8,128)(2,1)S(1)} %reshape.149), channel_id=1, source_target_pairs={{4,0},{13,9},{20,16},{29,25},{36,32},{45,41},{52,48},{61,57},{68,6... | collective-permute-start | bytes 737288 | tf_op jit(solution)/shard_map/ppermute | solution.py:48
  73.2 9.5 %collective-permute-start = (bf16[80,1536]{1,0:T(8,128)(2,1)S(1)}, bf16[80,1536]{1,0:T(8,128)(2,1)S(1)}, u32[]{:S(2)}, u32[]{:S(2)}) collective-permute-start(bf16[80,1536]{1,0:T(8,128)(2,1)S(1)} %reshape.149), channel_id=1, source_target_pairs={{2,0},{11,9},{18,16},{27,25},{34,32},{43,41},{50,48},{59,57},{66,6... | collective-permute-start | bytes 737288 | tf_op jit(solution)/shard_map/ppermute | solution.py:48
  122.8 9.7 %collective-permute-start.9 = (bf16[128,1536]{1,0:T(8,128)(2,1)S(1)}, bf16[128,1536]{1,0:T(8,128)(2,1)S(1)}, u32[]{:S(2)}, u32[]{:S(2)}) collective-permute-start(bf16[128,1536]{1,0:T(8,128)(2,1)S(1)} %get-tuple-element.67), channel_id=1, source_target_pairs={{0,64},{9,73},{16,80},{25,89},{32,96},{41,105},{48,112},{57,121}} | collective-permute-start | bytes 1179656 | tf_op jit(solution)/shard_map/ppermute | solution.py:48
  124.1 12.6 %collective-permute-start.8 = (bf16[128,1536]{1,0:T(8,128)(2,1)S(1)}, bf16[128,1536]{1,0:T(8,128)(2,1)S(1)}, u32[]{:S(2)}, u32[]{:S(2)}) collective-permute-start(bf16[128,1536]{1,0:T(8,128)(2,1)S(1)} %get-tuple-element.66), channel_id=1, source_target_pairs={{0,64},{9,73},{16,80},{25,89},{32,96},{41,105},{48,112},{57,121}} | collective-permute-start | bytes 1179656 | tf_op jit(solution)/shard_map/ppermute | solution.py:48
  125.4 15.5 %collective-permute-start.7 = (bf16[128,1536]{1,0:T(8,128)(2,1)S(1)}, bf16[128,1536]{1,0:T(8,128)(2,1)S(1)}, u32[]{:S(2)}, u32[]{:S(2)}) collective-permute-start(bf16[128,1536]{1,0:T(8,128)(2,1)S(1)} %get-tuple-element.64), channel_id=1, source_target_pairs={{0,64},{9,73},{16,80},{25,89},{32,96},{41,105},{48,112},{57,121}} | collective-permute-start | bytes 1179656 | tf_op jit(solution)/shard_map/ppermute | solution.py:48
  126.7 18.4 %collective-permute-start.6 = (bf16[128,1536]{1,0:T(8,128)(2,1)S(1)}, bf16[128,1536]{1,0:T(8,128)(2,1)S(1)}, u32[]{:S(2)}, u32[]{:S(2)}) collective-permute-start(bf16[128,1536]{1,0:T(8,128)(2,1)S(1)} %get-tuple-element.63), channel_id=1, source_target_pairs={{0,64},{9,73},{16,80},{25,89},{32,96},{41,105},{48,112},{57,121}} | collective-permute-start | bytes 1179656 | tf_op jit(solution)/shard_map/ppermute | solution.py:48
  163.1 6.6 %collective-permute-start.13 = (bf16[128,1536]{1,0:T(8,128)(2,1)S(1)}, bf16[128,1536]{1,0:T(8,128)(2,1)S(1)}, u32[]{:S(2)}, u32[]{:S(2)}) collective-permute-start(bf16[128,1536]{1,0:T(8,128)(2,1)S(1)} %get-tuple-element.74), channel_id=1, source_target_pairs={{64,128},{73,137},{80,144},{89,153},{96,160},{105,169},{112,176},{... | collective-permute-start | bytes 1179656 | tf_op jit(solution)/shard_map/ppermute | solution.py:48
  164.4 9.5 %collective-permute-start.12 = (bf16[128,1536]{1,0:T(8,128)(2,1)S(1)}, bf16[128,1536]{1,0:T(8,128)(2,1)S(1)}, u32[]{:S(2)}, u32[]{:S(2)}) collective-permute-start(bf16[128,1536]{1,0:T(8,128)(2,1)S(1)} %get-tuple-element.73), channel_id=1, source_target_pairs={{64,128},{73,137},{80,144},{89,153},{96,160},{105,169},{112,176},{... | collective-permute-start | bytes 1179656 | tf_op jit(solution)/shard_map/ppermute | solution.py:48
  165.7 12.4 %collective-permute-start.11 = (bf16[128,1536]{1,0:T(8,128)(2,1)S(1)}, bf16[128,1536]{1,0:T(8,128)(2,1)S(1)}, u32[]{:S(2)}, u32[]{:S(2)}) collective-permute-start(bf16[128,1536]{1,0:T(8,128)(2,1)S(1)} %get-tuple-element.71), channel_id=1, source_target_pairs={{64,128},{73,137},{80,144},{89,153},{96,160},{105,169},{112,176},{... | collective-permute-start | bytes 1179656 | tf_op jit(solution)/shard_map/ppermute | solution.py:48
  167.1 15.2 %collective-permute-start.10 = (bf16[128,1536]{1,0:T(8,128)(2,1)S(1)}, bf16[128,1536]{1,0:T(8,128)(2,1)S(1)}, u32[]{:S(2)}, u32[]{:S(2)}) collective-permute-start(bf16[128,1536]{1,0:T(8,128)(2,1)S(1)} %get-tuple-element.70), channel_id=1, source_target_pairs={{64,128},{73,137},{80,144},{89,153},{96,160},{105,169},{112,176},{... | collective-permute-start | bytes 1179656 | tf_op jit(solution)/shard_map/ppermute | solution.py:48
  201.6 7.7 %collective-permute-start.17 = (bf16[128,1536]{1,0:T(8,128)(2,1)}, bf16[128,1536]{1,0:T(8,128)(2,1)S(1)}, u32[]{:S(2)}, u32[]{:S(2)}) collective-permute-start(bf16[128,1536]{1,0:T(8,128)(2,1)} %get-tuple-element.81), channel_id=1, source_target_pairs={{128,192},{137,201},{144,208},{153,217},{160,224},{169,233},{176,2... | collective-permute-start | bytes 1179656 | tf_op jit(solution)/shard_map/ppermute | solution.py:48
  202.3 14.4 %collective-permute-start.16 = (bf16[128,1536]{1,0:T(8,128)(2,1)}, bf16[128,1536]{1,0:T(8,128)(2,1)S(1)}, u32[]{:S(2)}, u32[]{:S(2)}) collective-permute-start(bf16[128,1536]{1,0:T(8,128)(2,1)} %get-tuple-element.80), channel_id=1, source_target_pairs={{128,192},{137,201},{144,208},{153,217},{160,224},{169,233},{176,2... | collective-permute-start | bytes 1179656 | tf_op jit(solution)/shard_map/ppermute | solution.py:48
  203.0 16.0 %collective-permute-start.15 = (bf16[128,1536]{1,0:T(8,128)(2,1)S(1)}, bf16[128,1536]{1,0:T(8,128)(2,1)S(1)}, u32[]{:S(2)}, u32[]{:S(2)}) collective-permute-start(bf16[128,1536]{1,0:T(8,128)(2,1)S(1)} %get-tuple-element.78), channel_id=1, source_target_pairs={{128,192},{137,201},{144,208},{153,217},{160,224},{169,233},{176,2... | collective-permute-start | bytes 1179656 | tf_op jit(solution)/shard_map/ppermute | solution.py:48
  203.7 19.4 %collective-permute-start.14 = (bf16[128,1536]{1,0:T(8,128)(2,1)}, bf16[128,1536]{1,0:T(8,128)(2,1)}, u32[]{:S(2)}, u32[]{:S(2)}) collective-permute-start(bf16[128,1536]{1,0:T(8,128)(2,1)} %get-tuple-element.77), channel_id=1, source_target_pairs={{128,192},{137,201},{144,208},{153,217},{160,224},{169,233},{176,2... | collective-permute-start | bytes 1179656 | tf_op jit(solution)/shard_map/ppermute | solution.py:48
  272.7 14.1 %collective-permute-start.22 = (bf16[128,1536]{1,0:T(8,128)(2,1)S(1)}, bf16[128,1536]{1,0:T(8,128)(2,1)S(1)}, u32[]{:S(2)}, u32[]{:S(2)}) collective-permute-start(bf16[128,1536]{1,0:T(8,128)(2,1)S(1)} %get-tuple-element.95), channel_id=1, source_target_pairs={{0,64},{9,73},{16,80},{25,89},{32,96},{41,105},{48,112},{57,121}} | collective-permute-start | bytes 1179656 | tf_op jit(solution)/shard_map/ppermute | solution.py:48
  274.0 17.1 %collective-permute-start.21 = (bf16[128,1536]{1,0:T(8,128)(2,1)S(1)}, bf16[128,1536]{1,0:T(8,128)(2,1)S(1)}, u32[]{:S(2)}, u32[]{:S(2)}) collective-permute-start(bf16[128,1536]{1,0:T(8,128)(2,1)S(1)} %get-tuple-element.94), channel_id=1, source_target_pairs={{0,64},{9,73},{16,80},{25,89},{32,96},{41,105},{48,112},{57,121}} | collective-permute-start | bytes 1179656 | tf_op jit(solution)/shard_map/ppermute | solution.py:48
  275.3 20.0 %collective-permute-start.20 = (bf16[128,1536]{1,0:T(8,128)(2,1)S(1)}, bf16[128,1536]{1,0:T(8,128)(2,1)S(1)}, u32[]{:S(2)}, u32[]{:S(2)}) collective-permute-start(bf16[128,1536]{1,0:T(8,128)(2,1)S(1)} %get-tuple-element.92), channel_id=1, source_target_pairs={{0,64},{9,73},{16,80},{25,89},{32,96},{41,105},{48,112},{57,121}} | collective-permute-start | bytes 1179656 | tf_op jit(solution)/shard_map/ppermute | solution.py:48
  276.6 22.9 %collective-permute-start.19 = (bf16[128,1536]{1,0:T(8,128)(2,1)S(1)}, bf16[128,1536]{1,0:T(8,128)(2,1)S(1)}, u32[]{:S(2)}, u32[]{:S(2)}) collective-permute-start(bf16[128,1536]{1,0:T(8,128)(2,1)S(1)} %get-tuple-element.91), channel_id=1, source_target_pairs={{0,64},{9,73},{16,80},{25,89},{32,96},{41,105},{48,112},{57,121}} | collective-permute-start | bytes 1179656 | tf_op jit(solution)/shard_map/ppermute | solution.py:48
  318.5 9.5 %collective-permute-start.25 = (bf16[128,1536]{1,0:T(8,128)(2,1)S(1)}, bf16[128,1536]{1,0:T(8,128)(2,1)S(1)}, u32[]{:S(2)}, u32[]{:S(2)}) collective-permute-start(bf16[128,1536]{1,0:T(8,128)(2,1)S(1)} %get-tuple-element.101), channel_id=1, source_target_pairs={{64,128},{73,137},{80,144},{89,153},{96,160},{105,169},{112,176},{... | collective-permute-start | bytes 1179656 | tf_op jit(solution)/shard_map/ppermute | solution.py:48
  319.8 12.4 %collective-permute-start.24 = (bf16[128,1536]{1,0:T(8,128)(2,1)S(1)}, bf16[128,1536]{1,0:T(8,128)(2,1)S(1)}, u32[]{:S(2)}, u32[]{:S(2)}) collective-permute-start(bf16[128,1536]{1,0:T(8,128)(2,1)S(1)} %get-tuple-element.99), channel_id=1, source_target_pairs={{64,128},{73,137},{80,144},{89,153},{96,160},{105,169},{112,176},{... | collective-permute-start | bytes 1179656 | tf_op jit(solution)/shard_map/ppermute | solution.py:48
  321.2 15.2 %collective-permute-start.23 = (bf16[128,1536]{1,0:T(8,128)(2,1)S(1)}, bf16[128,1536]{1,0:T(8,128)(2,1)S(1)}, u32[]{:S(2)}, u32[]{:S(2)}) collective-permute-start(bf16[128,1536]{1,0:T(8,128)(2,1)S(1)} %get-tuple-element.98), channel_id=1, source_target_pairs={{64,128},{73,137},{80,144},{89,153},{96,160},{105,169},{112,176},{... | collective-permute-start | bytes 1179656 | tf_op jit(solution)/shard_map/ppermute | solution.py:48
  356.6 11.1 %collective-permute-start.29 = (bf16[128,1536]{1,0:T(8,128)(2,1)}, bf16[128,1536]{1,0:T(8,128)(2,1)S(1)}, u32[]{:S(2)}, u32[]{:S(2)}) collective-permute-start(bf16[128,1536]{1,0:T(8,128)(2,1)} %get-tuple-element.108), channel_id=1, source_target_pairs={{128,192},{137,201},{144,208},{153,217},{160,224},{169,233},{176,2... | collective-permute-start | bytes 1179656 | tf_op jit(solution)/shard_map/ppermute | solution.py:48
  357.3 12.8 %collective-permute-start.28 = (bf16[128,1536]{1,0:T(8,128)(2,1)}, bf16[128,1536]{1,0:T(8,128)(2,1)S(1)}, u32[]{:S(2)}, u32[]{:S(2)}) collective-permute-start(bf16[128,1536]{1,0:T(8,128)(2,1)} %get-tuple-element.106), channel_id=1, source_target_pairs={{128,192},{137,201},{144,208},{153,217},{160,224},{169,233},{176,2... | collective-permute-start | bytes 1179656 | tf_op jit(solution)/shard_map/ppermute | solution.py:48
  358.0 14.4 %collective-permute-start.27 = (bf16[128,1536]{1,0:T(8,128)(2,1)}, bf16[128,1536]{1,0:T(8,128)(2,1)S(1)}, u32[]{:S(2)}, u32[]{:S(2)}) collective-permute-start(bf16[128,1536]{1,0:T(8,128)(2,1)} %get-tuple-element.105), channel_id=1, source_target_pairs={{128,192},{137,201},{144,208},{153,217},{160,224},{169,233},{176,2... | collective-permute-start | bytes 1179656 | tf_op jit(solution)/shard_map/ppermute | solution.py:48
  393.6 23.5 %all-to-all-start.4 = ((f32[32,8,128]{2,1,0:T(8,128)}), f32[32,8,128]{2,1,0:T(8,128)S(1)}, u32[]{:S(2)}, u32[]{:S(2)}) async-start(f32[32,8,128]{2,1,0:T(8,128)} %select_bitcast_fusion), calls=%async_computation.4 | async-start | bytes 262144 | tf_op jit(solution)/shard_map/all_to_all | solution.py:347
  (33 other events, 458.6 us)
where the time goes:
time: 424 us; the launch traced here: 418 us
  Pallas kernels  212 us (50%)
  waiting for transfers between devices  91.3 us (22%)
  starting transfers between devices  74.3 us (18%)
  local copies, waits for them, and re-layouts  22.7 us (5%)
  other arithmetic  7.2 us (2%)
  matrix products  6.86 us (2%)
    pallas_call x16, Pallas kernels, attention(): pl.pallas_call(functools.partial(attention_kernel, queries=queries, block...  128 us
    pallas_call x33, Pallas kernels, product(): pl.pallas_call(functools.partial(product_kernel, norm=norm, column=column...  77 us
    ppermute x32, waiting for transfers between devices, move(): return lax.ppermute(value, AXES, [(flat(*a), flat(*b)) for a, b in pairs])  47 us
    ppermute x32, starting transfers between devices, move(): return lax.ppermute(value, AXES, [(flat(*a), flat(*b)) for a, b in pairs])  37.7 us
    unnamed x56, local copies, waits for them, and re-layouts  17 us
    all_to_all x1, starting transfers between devices, on_device(): lax.all_to_all(latent.reshape(Z * Y, rows_here * latent_width // 128, 128...  13 us
    all_to_all x1, waiting for transfers between devices, on_device(): lax.all_to_all(partial.reshape(Y, quarter, width), 'y', split_axis=0, con...  12.1 us
    all_to_all x1, waiting for transfers between devices, on_device(): lax.all_to_all(latent.reshape(Z * Y, rows_here * latent_width // 128, 128...  10.5 us
  transfers between devices with their start and end apart: 37, of which 23 were waited for; matrix products, arithmetic and copies ran while one was open for 3% of the time, Pallas kernels for 10%

commit v1 on v0

--- a/solution.py
+++ b/solution.py
@@ -16,19 +16,12 @@
 AXES = ("x", "z", "y", "c")
 BF = jnp.bfloat16
 F32 = jnp.float32
-VMEM = 26 * 1024 * 1024
+VMEM = 20 * 1024 * 1024
 SPAN = 768
 CHUNKS = 4
 TOGETHER = 2
 
 epsilon = 1e-06
-
-
-def layer_norm(hidden):
-    values = hidden.astype(F32)
-    center = values - jnp.mean(values, axis=-1, keepdims=True)
-    spread = jnp.mean(center * center, axis=-1, keepdims=True)
-    return center * lax.rsqrt(spread + epsilon)
 
 
 def time_features(noise_level, feature_count):
@@ -64,7 +57,8 @@
     return pltpu.CompilerParams(vmem_limit_bytes=VMEM)
 
 
-def joined_kernel(core_ref, own_ref, other_ref, out_ref, sems):
+def joined_kernel(core_ref, own_ref, other_ref, *refs):
+    out_ref, sems = refs[-2:]
     half = own_ref.shape[0]
     core = core_ref[0]
     copies = (
@@ -81,37 +75,45 @@
         copy.wait()
 
 
-def joined(core, own, other):
+def joined(core, own, other, after):
     half, columns = own.shape
     return pl.pallas_call(
         joined_kernel,
-        in_specs=[scalar(), pl.BlockSpec(memory_space=pl.ANY), pl.BlockSpec(memory_space=pl.ANY)],
+        in_specs=[scalar()]
+        + [pl.BlockSpec(memory_space=pltpu.HBM)] * 2
+        + [pl.BlockSpec(memory_space=pl.ANY)] * len(after),
         out_specs=whole(),
         out_shape=jax.ShapeDtypeStruct((2 * half, columns), BF),
         scratch_shapes=[pltpu.SemaphoreType.DMA((2,))],
         compiler_params=params(),
+        cost_estimate=pl.CostEstimate(
+            flops=0, bytes_accessed=8 * half * columns, transcendentals=0
+        ),
         name="joined",
-    )(core, own, other)
-
-
-def product_kernel(rows_ref, shift_ref, scale_ref, weight_ref, out_ref, normed, *, norm, column):
-    count = rows_ref.shape[0]
-    step = min(count, 64)
-    if norm:
-
-        def body(i, carry):
-            there = pl.ds(pl.multiple_of(i * step, step), step)
-            values = rows_ref[there, :].astype(F32)
-            center = values - jnp.mean(values, axis=-1, keepdims=True)
-            spread = jnp.mean(center * center, axis=-1, keepdims=True)
-            values = center * lax.rsqrt(spread + epsilon)
-            normed[there, :] = (values * (1.0 + scale_ref[...]) + shift_ref[...]).astype(BF)
-            return carry
-
-        lax.fori_loop(0, count // step, body, 0, unroll=True)
-        source = normed
-    else:
-        source = rows_ref
+    )(core, own, other, *after)
+
+
+def normal(values):
+    center = values - jnp.mean(values, axis=-1, keepdims=True)
+    spread = jnp.mean(center * center, axis=-1, keepdims=True)
+    return center * lax.rsqrt(spread + epsilon)
+
+
+def product_kernel(*refs, pieces, column):
+    row_refs, refs = refs[:pieces], refs[pieces:]
+    weight_ref, refs = refs[0], refs[1:]
+    out_ref, source = refs[-2:]
+    done = 0
+    for ref in row_refs:
+        count = ref.shape[0]
+        for i in range(0, count, 64):
+            values = ref[i : i + 64, :]
+            if column == 0:
+                shift_ref, scale_ref = refs[:2]
+                values = normal(values.astype(F32))
+                values = (values * (1.0 + scale_ref[...]) + shift_ref[...]).astype(BF)
+            source[done + i : done + i + 64, :] = values
+        done += count
     for i in range(out_ref.shape[1] // SPAN):
         there = slice(i * SPAN, (i + 1) * SPAN)
         here = slice(column + i * SPAN, column + (i + 1) * SPAN)
@@ -120,24 +122,122 @@
         ).astype(BF)
 
 
-def product(rows, shift, scale, weight, column, norm):
-    count, width = rows.shape
+def product(rows, weight, column, modulate=(), after=()):
+    count = sum(part.shape[0] for part in rows)
+    width = weight.shape[0]
     columns = weight.shape[1] - column
     return pl.pallas_call(
-        functools.partial(product_kernel, norm=norm, column=column),
-        in_specs=[whole()] * 4,
+        functools.partial(product_kernel, pieces=len(rows), column=column),
+        in_specs=[whole()] * (len(rows) + 1 + len(modulate))
+        + [pl.BlockSpec(memory_space=pl.ANY)] * len(after),
         out_specs=whole(),
         out_shape=jax.ShapeDtypeStruct((count, columns), BF),
+        cost_estimate=pl.CostEstimate(
+            flops=2 * count * width * columns,
+            bytes_accessed=2 * 1024 * 1024,
+            transcendentals=0,
+        ),
         scratch_shapes=[pltpu.VMEM((count, width), BF)],
         compiler_params=params(),
         name="product",
-    )(rows, shift, scale, weight)
+    )(*rows, weight, *modulate, *after)
+
+
+def embed_kernel(latent_ref, weight_ref, *out_refs):
+    done = 0
+    for ref in out_refs:
+        count = ref.shape[0]
+        ref[...] = jnp.dot(
+            latent_ref[done : done + count, :], weight_ref[...], preferred_element_type=F32
+        ).astype(BF)
+        done += count
+
+
+def embedded(latent, weight):
+    rows = latent.shape[0] // CHUNKS
+    return pl.pallas_call(
+        embed_kernel,
+        in_specs=[whole()] * 2,
+        out_specs=[whole()] * CHUNKS,
+        out_shape=[jax.ShapeDtypeStruct((rows, weight.shape[1]), BF)] * CHUNKS,
+        compiler_params=params(),
+        name="embed",
+    )(latent, weight)
+
+
+def finish_kernel(pace_ref, *refs, step):
+    *row_refs, weight_ref, latent_ref, out_ref, rounded_ref = refs
+    pace = pace_ref[step]
+    done = 0
+    for ref in row_refs:
+        count = ref.shape[0]
+        there = slice(done, done + count)
+        velocity = jnp.dot(
+            normal(ref[...].astype(F32)).astype(BF),
+            weight_ref[...],
+            preferred_element_type=F32,
+        )
+        latent = latent_ref[there, :] + pace * velocity
+        out_ref[there, :] = latent
+        rounded_ref[there, :] = latent.astype(BF)
+        done += count
+
+
+def finished(pace, hidden, weight, latent, step):
+    return pl.pallas_call(
+        functools.partial(finish_kernel, step=step),
+        in_specs=[scalar()] + [whole()] * (len(hidden) + 2),
+        out_specs=[whole()] * 2,
+        out_shape=[
+            jax.ShapeDtypeStruct(latent.shape, F32),
+            jax.ShapeDtypeStruct(latent.shape, BF),
+        ],
+        compiler_params=params(),
+        name="finish",
+    )(pace, *hidden, weight, latent)
+
+
+def spread_kernel(parts_ref, out_ref):
+    count = out_ref.shape[1]
+    total = parts_ref[0, :count].astype(F32)
+    for k in range(1, parts_ref.shape[0]):
+        total = total + parts_ref[k, :count].astype(F32)
+    for k in range(out_ref.shape[0]):
+        out_ref[k] = total.astype(BF)
+
+
+def spread_over(parts, copies, count):
+    return pl.pallas_call(
+        spread_kernel,
+        in_specs=[whole()],
+        out_specs=whole(),
+        out_shape=jax.ShapeDtypeStruct((copies, count, parts.shape[2]), BF),
+        compiler_params=params(),
+        name="spread",
+    )(parts)
+
+
+def twice_kernel(rows_ref, out_ref):
+    for k in range(out_ref.shape[0]):
+        out_ref[k] = rows_ref[k * rows_ref.shape[0] // out_ref.shape[0]]
+
+
+def twice(rows, copies):
+    return pl.pallas_call(
+        twice_kernel,
+        in_specs=[whole()],
+        out_specs=whole(),
+        out_shape=jax.ShapeDtypeStruct((copies,) + rows.shape[1:], BF),
+        compiler_params=params(),
+        name="twice",
+    )(rows)
 
 
 def attention_kernel(*refs, queries, blocks):
     projected, refs = refs[:blocks], refs[blocks:]
     text_ref, bias_ref, gate_ref, weight_ref, *refs = refs
-    hidden_refs, out_refs, attended = refs[: len(queries)], refs[len(queries) : -1], refs[-1]
+    count = len(queries)
+    hidden_refs, out_refs, attended = refs[:count], refs[-count - 1 : -1], refs[-1]
     inner = weight_ref.shape[0]
     factor = math.log2(math.e) / math.sqrt(HEAD)
     lanes = lax.broadcasted_iota(jnp.int32, (1, 128), 1)
@@ -202,18 +302,24 @@
             done += count
 
 
-def attention(projected, text, bias, gate, weight, hidden, queries):
+def attention(projected, text, bias, gate, weight, hidden, queries, after=()):
     hidden = [hidden[i] for i in queries]
     rows = sum(part.shape[0] for part in hidden)
     return pl.pallas_call(
         functools.partial(attention_kernel, queries=queries, blocks=len(projected)),
-        in_specs=[whole()] * (len(projected) + 4 + len(hidden)),
+        in_specs=[whole()] * (len(projected) + 4 + len(hidden))
+        + [pl.BlockSpec(memory_space=pl.ANY)] * len(after),
+        cost_estimate=pl.CostEstimate(
+            flops=4 * rows * weight.shape[0] * weight.shape[1],
+            bytes_accessed=8 * 1024 * 1024,
+            transcendentals=0,
+        ),
         out_specs=[whole()] * len(hidden),
         out_shape=[jax.ShapeDtypeStruct(part.shape, BF) for part in hidden],
         scratch_shapes=[pltpu.VMEM((rows, weight.shape[0]), BF)],
         compiler_params=params(),
         name="attention",
-    )(*projected, text, bias, gate, weight, *hidden)
+    )(*projected, text, bias, gate, weight, *hidden, *after)
 
 
 def on_device(
@@ -245,8 +351,6 @@
     def hop(value, source, target):
         return move(value, [((source, b, 0, d), (target, b, 0, d)) for _, b, d in homes()])
 
-    attn_weight = joined(core, w_attention[0], across(w_attention[0]))
-    proj_weight = joined(core, w_project[0], across(w_project[0]))
     levels = plan.astype(F32)
     mod_rows = w_modulate.shape[1]
     features = jnp.stack([time_features(levels[k], C * mod_rows) for k in range(STEPS)])
@@ -256,32 +360,62 @@
 
     text = lax.dynamic_index_in_dim(text_rows[:, 0], x, 0, keepdims=False)
     partial = jnp.dot(text, context_weight, preferred_element_type=F32).astype(BF)
+    attn_mine, proj_mine, partial = lax.optimization_barrier(
+        (w_attention[0], w_project[0], partial)
+    )
     quarter = text_total // Y
     eighth = quarter // Z
-    parts = lax.all_to_all(
-        partial.reshape(Y, quarter, width), "y", split_axis=0, concat_axis=0, tiled=True
-    )
-    summed = jnp.sum(parts.astype(F32), axis=0).astype(BF)
-    parts = lax.all_to_all(
-        summed.reshape(Z, eighth, width), "z", split_axis=0, concat_axis=0, tiled=True
-    )
-    summed = jnp.sum(parts.astype(F32), axis=0).astype(BF)
-
-    latent = latent_noise[0, 0].reshape(-1)
+    latent = latent_noise[0, 0].reshape(1, rows_here * latent_width)
     high = latent.astype(BF)
     low = (latent - high.astype(F32)).astype(BF)
-    both = jnp.concatenate([high, low])
-    tail = -(-both.size // width)
-    piece = jnp.concatenate(
-        [summed, jnp.pad(both, (0, tail * width - both.size)).reshape(tail, width)], 0
-    )
-    held = eighth + tail
+    both = jnp.pad(jnp.concatenate([high, low], 0), ((0, 0), (0, width - latent.shape[1])))
+    parts = lax.all_to_all(
+        jnp.concatenate(
+            [partial.reshape(Y, quarter, width), jnp.broadcast_to(both[None], (Y, 2, width))], 1
+        ),
+        "y",
+        split_axis=0,
+        concat_axis=0,
+        tiled=True,
+    )
+    summed = jnp.sum(parts[:, :quarter].astype(F32), axis=0).astype(BF)
+    both = parts[:, quarter:].reshape(1, 2 * Y, width)
+    parts = lax.all_to_all(
+        jnp.concatenate(
+            [summed.reshape(Z, eighth, width), jnp.broadcast_to(both, (Z, 2 * Y, width))], 1
+        ),
+        "z",
+        split_axis=0,
+        concat_axis=0,
+        tiled=True,
+    )
+    both = parts[:, eighth:].reshape(patches // rows_here, 2, width)[:, :, : latent.shape[1]]
+    both = jnp.transpose(both, (1, 0, 2)).reshape(2, patches * latent_width // 128, 128)
+
+    def to_plane(value, plane):
+        sent = move(value, [((m, b, 0, d), (plane, b, 0, d)) for m, b, d in homes() if m != plane])
+        return jnp.where(image == plane, value, sent)
+
+    first = to_plane(both[0], 0).reshape(patches, latent_width)
+    latent = to_plane(both, BLOCKS - 1)
+    latent = (latent[0].astype(F32) + latent[1].astype(F32)).reshape(patches, latent_width)
+    length = jnp.sum(jnp.where(jnp.arange(X) == image, text_lengths[:, 0], 0))
+    bias = jnp.where(jnp.arange(text_total) < length, 0.0, -1e30).astype(F32)[None, :]
+    pace = (levels[1:] - levels[:-1]) / 1000.0
+    shifts, scales, gates = (
+        [modulation[k : k + 1, part * width : (part + 1) * width] for k in range(STEPS)]
+        for part in range(3)
+    )
+
+    ready = (first, latent, bias, *shifts, *scales, *gates)
+    attn_weight = joined(core, attn_mine, across(attn_mine), ready)
+    proj_weight = joined(core, proj_mine, across(proj_mine), (attn_weight,))
+
     shared = lax.all_to_all(
-        jnp.broadcast_to(piece[None], (X, held, width)), "x", split_axis=0, concat_axis=0, tiled=True
-    )
-    shared = jnp.repeat(shared, Z // X, axis=0)
-    shared = lax.all_to_all(shared, "z", split_axis=0, concat_axis=0, tiled=True)
-    pieces = [shared.reshape(Z * held, width)]
+        spread_over(parts, X, eighth), "x", split_axis=0, concat_axis=0, tiled=True
+    )
+    shared = lax.all_to_all(twice(shared, Z), "z", split_axis=0, concat_axis=0, tiled=True)
+    pieces = [shared.reshape(quarter, width)]
     for k in range(1, Y):
         pieces.append(
             move(
@@ -289,56 +423,41 @@
                 [((a, b, k, b % C), (a, b, 0, b % C)) for a in range(X) for b in range(Z)],
             )
         )
-    pieces = jnp.stack(pieces).reshape(Y, Z, held, width)
-    context = pieces[:, :, :eighth].reshape(text_total, width)
-    latents = pieces[:, :, eighth:].reshape(Y, Z, tail * width)[:, :, : both.size]
-    latents = latents.reshape(Y, Z, 2, rows_here, latent_width)
-    latents = jnp.transpose(latents, (2, 1, 0, 3, 4)).reshape(2, patches, latent_width)
-    latent = latents[0].astype(F32) + latents[1].astype(F32)
-
-    length = jnp.sum(jnp.where(jnp.arange(X) == image, text_lengths[:, 0], 0))
-    bias = jnp.where(jnp.arange(text_total) < length, 0.0, -1e30).astype(F32)[None, :]
-    nothing = jnp.zeros((1, width), F32)
-    keys = product(context, nothing, nothing, attn_weight, width, False)
-
-    rows = patches // CHUNKS
-
-    def embedded(value):
-        return [
-            jnp.dot(
-                value[i * rows : (i + 1) * rows], w_embed, preferred_element_type=F32
-            ).astype(BF)
-            for i in range(CHUNKS)
-        ]
-
-    hidden = embedded(latents[0])
+    keys = product(pieces, attn_weight, width)
+
+    hidden = embedded(first, w_embed)
     for turn in range(STEPS * BLOCKS):
         step, block = divmod(turn, BLOCKS)
-        shift = modulation[step : step + 1, :width]
-        scale = modulation[step : step + 1, width : 2 * width]
-        gate = modulation[step : step + 1, 2 * width :]
-        projected = [product(part, shift, scale, attn_weight, 0, True) for part in hidden]
+        gate = gates[step]
+        projected = []
+        for part in hidden:
+            projected.append(
+                product(
+                    [part], attn_weight, 0, (shifts[step], scales[step]), tuple(projected[-1:])
+                )
+            )
         following = []
         for i in range(0, CHUNKS, TOGETHER):
             queries = tuple(range(i, i + TOGETHER))
-            if following:
-                bound, following = lax.optimization_barrier((gate, following))
-            else:
-                bound = gate
             following = following + list(
-                attention(projected, keys, bias, bound, proj_weight, hidden, queries)
+                attention(
+                    projected,
+                    keys,
+                    bias,
+                    gate,
+                    proj_weight,
+                    hidden,
+                    queries,
+                    tuple(following[-1:]),
+                )
             )
         hidden = following
         if block < BLOCKS - 1:
             hidden = [hop(part, block, block + 1) for part in hidden]
         else:
-            final = jnp.concatenate(hidden, 0)
-            velocity = jnp.dot(
-                layer_norm(final).astype(BF), w_final, preferred_element_type=F32
-            )
-            latent = latent + (levels[step + 1] - levels[step]) / 1000.0 * velocity
+            latent, rounded = finished(pace, hidden, w_final, latent, step)
             if step < STEPS - 1:
-                hidden = embedded(hop(latent.astype(BF), block, 0))
+                hidden = embedded(hop(rounded, block, 0), w_embed)
 
     last = BLOCKS - 1
     latent = latent.reshape(patches * latent_width // 128, 128)

time: 424 us -> 379 us (0.89)
  waiting for transfers between devices: 91.3 us -> 62.4 us
  local copies, waits for them, and re-layouts: 22.7 us -> 12.1 us
  matrix products: 6.86 us -> 1.81 us
  starting transfers between devices: 74.3 us -> 78.7 us
    ppermute x32 -> x34, waiting for transfers between devices: 47 us -> 16.3 us  [move(): return lax.ppermute(value, AXES, [(flat(*a), flat(*b)) for a, b in pairs])]
    unnamed x56 -> x42, local copies, waits for them, and re-layouts: 17 us -> 10.1 us
    pallas_call x16, Pallas kernels: 128 us -> 123 us  [attention(): pl.pallas_call(functools.partial(attention_kernel, queries=queries, block...]
    pallas_call x35 -> x41, Pallas kernels: 83.1 us -> 87.7 us  [the longest x33 75 us: product(): pl.pallas_call(functools.partial(product_kernel, pieces=len(rows), column...]
    dot_general x10 -> x0, matrix products: 4.26 us -> none  [the longest x2 2.2 us: on_device(): jnp.dot(layer_norm(final).astype(BF), w_final, preferred_element_type=F32)]
    ppermute x32 -> x34, starting transfers between devices: 37.7 us -> 38.6 us  [move(): return lax.ppermute(value, AXES, [(flat(*a), flat(*b)) for a, b in pairs])]
  transfers between devices with their start and end apart: 37 -> 39, of which waited for: 23 -> 14; matrix products, arithmetic and copies ran while one was open for 3% -> 2% of each run, Pallas kernels for 10% -> 28%
where the time goes in v1:
time: 379 us; the launch traced here: 373 us
  Pallas kernels  211 us (56%)
  starting transfers between devices  78.7 us (21%)
  waiting for transfers between devices  62.4 us (16%)
  local copies, waits for them, and re-layouts  12.1 us (3%)
  other arithmetic  5.44 us (1%)
    pallas_call x16, Pallas kernels, attention(): pl.pallas_call(functools.partial(attention_kernel, queries=queries, block...  123 us
    pallas_call x33, Pallas kernels, product(): pl.pallas_call(functools.partial(product_kernel, pieces=len(rows), column...  75 us
    ppermute x34, starting transfers between devices, move(): return lax.ppermute(value, AXES, [(flat(*a), flat(*b)) for a, b in pairs])  38.6 us
    ppermute x34, waiting for transfers between devices, move(): return lax.ppermute(value, AXES, [(flat(*a), flat(*b)) for a, b in pairs])  16.3 us
    all_to_all x1, starting transfers between devices, on_device(): lax.all_to_all(latent.reshape(Z * Y, rows_here * latent_width // 128, 128...  13.5 us
    all_to_all x1, waiting for transfers between devices, on_device(): lax.all_to_all(jnp.concatenate([partial.reshape(Y, quarter, width), jnp.b...  12.6 us
    all_to_all x1, waiting for transfers between devices, on_device(): lax.all_to_all(latent.reshape(Z * Y, rows_here * latent_width // 128, 128...  10.5 us
    unnamed x42, local copies, waits for them, and re-layouts  10.1 us
  transfers between devices with their start and end apart: 39, of which 14 were waited for; matrix products, arithmetic and copies ran while one was open for 2% of the time, Pallas kernels for 28%

profile of v1, /device:TPU:2, one launch (start us, length us, event | category | flops | bytes accessed | tf_op | source)
XLA Modules:
  0.0 372.7 jit_solution(5962933671015376860)
XLA Ops:
  4.0 6.8 %all-to-all-start = ((bf16[4,66,1536]{2,1,0:T(8,128)(2,1)}), bf16[4,66,1536]{2,1,0:T(8,128)(2,1)S(1)}, u32[]{:S(2)}, u32[]{:S(2)}) async-start(bf16[4,66,1536]{2,1,0:T(8,128)(2,1)} %pad_maximum_fusion), calls=%async_computation | async-start | bytes 1769472 | tf_op jit(solution)/shard_map/all_to_all | solution.py:372
  12.8 12.6 %all-to-all-done = bf16[4,66,1536]{2,1,0:T(8,128)(2,1)S(1)} async-done(((bf16[4,66,1536]{2,1,0:T(8,128)(2,1)}), bf16[4,66,1536]{2,1,0:T(8,128)(2,1)S(1)}, u32[]{:S(2)}, u32[]{:S(2)}) %all-to-all-start) | async-done | bytes 811040 | tf_op jit(solution)/shard_map/all_to_all | solution.py:372
  26.4 8.6 %all-to-all-start.1 = ((bf16[8,16,1536]{2,1,0:T(8,128)(2,1)}), bf16[8,16,1536]{2,1,0:T(8,128)(2,1)S(1)}, u32[]{:S(2)}, u32[]{:S(2)}) async-start(bf16[8,16,1536]{2,1,0:T(8,128)(2,1)} %pad_maximum_fusion.1), calls=%async_computation.1 | async-start | bytes 786432 | tf_op jit(solution)/shard_map/all_to_all | solution.py:383
  39.8 9.9 %all-to-all-done.1.parts_ref = bf16[8,16,1536]{2,1,0:T(8,128)(2,1)S(1)} async-done(((bf16[8,16,1536]{2,1,0:T(8,128)(2,1)}), bf16[8,16,1536]{2,1,0:T(8,128)(2,1)S(1)}, u32[]{:S(2)}, u32[]{:S(2)}) %all-to-all-start.1) | async-done | bytes 393248 | tf_op jit(solution)/shard_map/all_to_all | solution.py:383
  52.1 7.8 %all-to-all-start.2 = ((bf16[4,8,1536]{2,1,0:T(8,128)(2,1)}), bf16[4,8,1536]{2,1,0:T(8,128)(2,1)S(1)}, u32[]{:S(2)}, u32[]{:S(2)}) async-start(bf16[4,8,1536]{2,1,0:T(8,128)(2,1)} %spread.1), calls=%async_computation.2 | async-start | bytes 196608 | tf_op jit(solution)/shard_map/all_to_all | solution.py:414
  60.6 3.7 all-to-all-done.2.rows_ref
  65.0 3.4 all-to-all-start.3
  68.6 9.5 %all-to-all-done.3 = bf16[8,8,1536]{2,1,0:T(8,128)(2,1)S(1)} async-done(((bf16[8,8,1536]{2,1,0:T(8,128)(2,1)}), bf16[8,8,1536]{2,1,0:T(8,128)(2,1)S(1)}, u32[]{:S(2)}, u32[]{:S(2)}) %all-to-all-start.3) | async-done | bytes 196640 | tf_op jit(solution)/shard_map/all_to_all | solution.py:417
  82.2 3.0 copy-done.5
  85.2 3.5 joined.2.refs_1_.refs_4_.refs_0_
  100.3 2.6 product.37.refs_4_
  102.9 7.5 %attention.16 = (bf16[128,1536]{1,0:T(8,128)(2,1)S(1)}, bf16[128,1536]{1,0:T(8,128)(2,1)S(1)}) custom-call(bf16[128,4608]{1,0:T(8,128)(2,1)S(1)} %product.33.refs_4_.refs_0_, bf16[128,4608]{1,0:T(8,128)(2,1)S(1)} %product.34.refs_4_.refs_1_, bf16[128,4608]{1,0:T(8,128)(2,1)S(1)} %product.35.refs_4_.refs_2_, bf16[128,4608]{1,0:T(8,128)(2,1)S(1)} %product.36.refs_3_, ...), custom_call_target="tpu_custom_call" | custom-call | flops 2415919104 | bytes 8388608 | tf_op jit(solution)/shard_map/attention/pallas_call | solution.py:308
  113.4 7.6 %attention.17 = (bf16[128,1536]{1,0:T(8,128)(2,1)S(1)}, bf16[128,1536]{1,0:T(8,128)(2,1)S(1)}) custom-call(bf16[128,4608]{1,0:T(8,128)(2,1)S(1)} %product.33.refs_4_.refs_0_, bf16[128,4608]{1,0:T(8,128)(2,1)S(1)} %product.34.refs_4_.refs_1_, bf16[128,4608]{1,0:T(8,128)(2,1)S(1)} %product.35.refs_4_.refs_2_, bf16[128,4608]{1,0:T(8,128)(2,1)S(1)} %product.36.refs_3_, ...), custom_call_target="tpu_custom_call" | custom-call | flops 2415919104 | bytes 8388608 | tf_op jit(solution)/shard_map/attention/pallas_call | solution.py:308
  128.2 2.6 collective-permute-done.10.refs_0_.refs_8_
  137.2 7.5 %attention.18 = (bf16[128,1536]{1,0:T(8,128)(2,1)S(1)}, bf16[128,1536]{1,0:T(8,128)(2,1)S(1)}) custom-call(bf16[128,4608]{1,0:T(8,128)(2,1)S(1)} %product.38.refs_4_.refs_0_, bf16[128,4608]{1,0:T(8,128)(2,1)S(1)} %product.39.refs_4_.refs_1_, bf16[128,4608]{1,0:T(8,128)(2,1)S(1)} %product.40.refs_4_.refs_2_, bf16[128,4608]{1,0:T(8,128)(2,1)S(1)} %product.41.refs_3_, ...), custom_call_target="tpu_custom_call" | custom-call | flops 2415919104 | bytes 8388608 | tf_op jit(solution)/shard_map/attention/pallas_call | solution.py:308
  147.6 7.6 %attention.19 = (bf16[128,1536]{1,0:T(8,128)(2,1)S(1)}, bf16[128,1536]{1,0:T(8,128)(2,1)S(1)}) custom-call(bf16[128,4608]{1,0:T(8,128)(2,1)S(1)} %product.38.refs_4_.refs_0_, bf16[128,4608]{1,0:T(8,128)(2,1)S(1)} %product.39.refs_4_.refs_1_, bf16[128,4608]{1,0:T(8,128)(2,1)S(1)} %product.40.refs_4_.refs_2_, bf16[128,4608]{1,0:T(8,128)(2,1)S(1)} %product.41.refs_3_, ...), custom_call_target="tpu_custom_call" | custom-call | flops 2415919104 | bytes 8388608 | tf_op jit(solution)/shard_map/attention/pallas_call | solution.py:308
  168.2 8.4 %attention.20 = (bf16[128,1536]{1,0:T(8,128)(2,1)}, bf16[128,1536]{1,0:T(8,128)(2,1)}) custom-call(bf16[128,4608]{1,0:T(8,128)(2,1)S(1)} %product.42.refs_4_.refs_0_, bf16[128,4608]{1,0:T(8,128)(2,1)S(1)} %product.43.refs_4_.refs_1_, bf16[128,4608]{1,0:T(8,128)(2,1)S(1)} %product.44.refs_4_.refs_2_, bf16[128,4608]{1,0:T(8,128)(2,1)S(1)} %product.45.refs_3_, ...), custom_call_target="tpu_custom_call" | custom-call | flops 2415919104 | bytes 8388608 | tf_op jit(solution)/shard_map/attention/pallas_call | solution.py:308
  178.2 8.2 %attention.21 = (bf16[128,1536]{1,0:T(8,128)(2,1)}, bf16[128,1536]{1,0:T(8,128)(2,1)S(1)}) custom-call(bf16[128,4608]{1,0:T(8,128)(2,1)S(1)} %product.42.refs_4_.refs_0_, bf16[128,4608]{1,0:T(8,128)(2,1)S(1)} %product.43.refs_4_.refs_1_, bf16[128,4608]{1,0:T(8,128)(2,1)S(1)} %product.44.refs_4_.refs_2_, bf16[128,4608]{1,0:T(8,128)(2,1)S(1)} %product.45.refs_3_, ...), custom_call_target="tpu_custom_call" | custom-call | flops 2415919104 | bytes 8388608 | tf_op jit(solution)/shard_map/attention/pallas_call | solution.py:308
  189.8 5.0 %copy-done.3 = bf16[1536,4608]{1,0:T(8,128)(2,1)S(1)} copy-done((bf16[1536,4608]{1,0:T(8,128)(2,1)S(1)}, bf16[1536,4608]{1,0:T(8,128)(2,1)}, u32[]{:S(2)}) %copy-start.3) | copy-done | bytes 14155800
  204.0 8.0 %attention.22 = (bf16[128,1536]{1,0:T(8,128)(2,1)S(1)}, bf16[128,1536]{1,0:T(8,128)(2,1)S(1)}) custom-call(bf16[128,4608]{1,0:T(8,128)(2,1)S(1)} %product.46.refs_4_.refs_0_, bf16[128,4608]{1,0:T(8,128)(2,1)S(1)} %product.47.refs_4_.refs_1_, bf16[128,4608]{1,0:T(8,128)(2,1)S(1)} %product.48.refs_4_.refs_2_, bf16[128,4608]{1,0:T(8,128)(2,1)S(1)} %product.49.refs_3_, ...), custom_call_target="tpu_custom_call" | custom-call | flops 2415919104 | bytes 8388608 | tf_op jit(solution)/shard_map/attention/pallas_call | solution.py:308
  212.0 7.5 %attention.23 = (bf16[128,1536]{1,0:T(8,128)(2,1)S(1)}, bf16[128,1536]{1,0:T(8,128)(2,1)S(1)}) custom-call(bf16[128,4608]{1,0:T(8,128)(2,1)S(1)} %product.46.refs_4_.refs_0_, bf16[128,4608]{1,0:T(8,128)(2,1)S(1)} %product.47.refs_4_.refs_1_, bf16[128,4608]{1,0:T(8,128)(2,1)S(1)} %product.48.refs_4_.refs_2_, bf16[128,4608]{1,0:T(8,128)(2,1)S(1)} %product.49.refs_3_, ...), custom_call_target="tpu_custom_call" | custom-call | flops 2415919104 | bytes 8388608 | tf_op jit(solution)/shard_map/attention/pallas_call | solution.py:308
  232.0 7.5 %attention.24 = (bf16[128,1536]{1,0:T(8,128)(2,1)S(1)}, bf16[128,1536]{1,0:T(8,128)(2,1)S(1)}) custom-call(bf16[128,4608]{1,0:T(8,128)(2,1)S(1)} %product.50.refs_4_.refs_0_, bf16[128,4608]{1,0:T(8,128)(2,1)S(1)} %product.51.refs_4_.refs_1_, bf16[128,4608]{1,0:T(8,128)(2,1)S(1)} %product.52.refs_4_.refs_2_, bf16[128,4608]{1,0:T(8,128)(2,1)S(1)} %product.53.refs_3_, ...), custom_call_target="tpu_custom_call" | custom-call | flops 2415919104 | bytes 8388608 | tf_op jit(solution)/shard_map/attention/pallas_call | solution.py:308
  242.4 7.5 %attention.25 = (bf16[128,1536]{1,0:T(8,128)(2,1)S(1)}, bf16[128,1536]{1,0:T(8,128)(2,1)S(1)}) custom-call(bf16[128,4608]{1,0:T(8,128)(2,1)S(1)} %product.50.refs_4_.refs_0_, bf16[128,4608]{1,0:T(8,128)(2,1)S(1)} %product.51.refs_4_.refs_1_, bf16[128,4608]{1,0:T(8,128)(2,1)S(1)} %product.52.refs_4_.refs_2_, bf16[128,4608]{1,0:T(8,128)(2,1)S(1)} %product.53.refs_3_, ...), custom_call_target="tpu_custom_call" | custom-call | flops 2415919104 | bytes 8388608 | tf_op jit(solution)/shard_map/attention/pallas_call | solution.py:308
  259.7 3.9 %collective-permute-done.23.refs_0_.refs_8_ = bf16[128,1536]{1,0:T(8,128)(2,1)S(1)} collective-permute-done((bf16[128,1536]{1,0:T(8,128)(2,1)S(1)}, bf16[128,1536]{1,0:T(8,128)(2,1)S(1)}, u32[]{:S(2)}, u32[]{:S(2)}) %collective-permute-start.23) | collective-permute-done | bytes 393248 | tf_op jit(solution)/shard_map/ppermute | solution.py:41
  270.1 7.6 %attention.26 = (bf16[128,1536]{1,0:T(8,128)(2,1)S(1)}, bf16[128,1536]{1,0:T(8,128)(2,1)S(1)}) custom-call(bf16[128,4608]{1,0:T(8,128)(2,1)S(1)} %product.54.refs_4_.refs_0_, bf16[128,4608]{1,0:T(8,128)(2,1)S(1)} %product.55.refs_4_.refs_1_, bf16[128,4608]{1,0:T(8,128)(2,1)S(1)} %product.56.refs_4_.refs_2_, bf16[128,4608]{1,0:T(8,128)(2,1)S(1)} %product.57.refs_3_, ...), custom_call_target="tpu_custom_call" | custom-call | flops 2415919104 | bytes 8388608 | tf_op jit(solution)/shard_map/attention/pallas_call | solution.py:308
  280.7 7.5 %attention.27 = (bf16[128,1536]{1,0:T(8,128)(2,1)S(1)}, bf16[128,1536]{1,0:T(8,128)(2,1)S(1)}) custom-call(bf16[128,4608]{1,0:T(8,128)(2,1)S(1)} %product.54.refs_4_.refs_0_, bf16[128,4608]{1,0:T(8,128)(2,1)S(1)} %product.55.refs_4_.refs_1_, bf16[128,4608]{1,0:T(8,128)(2,1)S(1)} %product.56.refs_4_.refs_2_, bf16[128,4608]{1,0:T(8,128)(2,1)S(1)} %product.57.refs_3_, ...), custom_call_target="tpu_custom_call" | custom-call | flops 2415919104 | bytes 8388608 | tf_op jit(solution)/shard_map/attention/pallas_call | solution.py:308
  301.3 7.5 %attention.28 = (bf16[128,1536]{1,0:T(8,128)(2,1)S(1)}, bf16[128,1536]{1,0:T(8,128)(2,1)S(1)}) custom-call(bf16[128,4608]{1,0:T(8,128)(2,1)S(1)} %product.58.refs_4_.refs_0_, bf16[128,4608]{1,0:T(8,128)(2,1)S(1)} %product.59.refs_4_.refs_1_, bf16[128,4608]{1,0:T(8,128)(2,1)S(1)} %product.60.refs_4_.refs_2_, bf16[128,4608]{1,0:T(8,128)(2,1)S(1)} %product.61.refs_3_, ...), custom_call_target="tpu_custom_call" | custom-call | flops 2415919104 | bytes 8388608 | tf_op jit(solution)/shard_map/attention/pallas_call | solution.py:308
  310.5 7.5 %attention.29 = (bf16[128,1536]{1,0:T(8,128)(2,1)S(1)}, bf16[128,1536]{1,0:T(8,128)(2,1)S(1)}) custom-call(bf16[128,4608]{1,0:T(8,128)(2,1)S(1)} %product.58.refs_4_.refs_0_, bf16[128,4608]{1,0:T(8,128)(2,1)S(1)} %product.59.refs_4_.refs_1_, bf16[128,4608]{1,0:T(8,128)(2,1)S(1)} %product.60.refs_4_.refs_2_, bf16[128,4608]{1,0:T(8,128)(2,1)S(1)} %product.61.refs_3_, ...), custom_call_target="tpu_custom_call" | custom-call | flops 2415919104 | bytes 8388608 | tf_op jit(solution)/shard_map/attention/pallas_call | solution.py:308
  328.5 7.8 %attention.30 = (bf16[128,1536]{1,0:T(8,128)(2,1)S(1)}, bf16[128,1536]{1,0:T(8,128)(2,1)S(1)}) custom-call(bf16[128,4608]{1,0:T(8,128)(2,1)S(1)} %product.62.refs_4_.refs_0_, bf16[128,4608]{1,0:T(8,128)(2,1)S(1)} %product.63.refs_4_.refs_1_, bf16[128,4608]{1,0:T(8,128)(2,1)S(1)} %product.64.refs_4_.refs_2_, bf16[128,4608]{1,0:T(8,128)(2,1)S(1)} %product.65.refs_3_, ...), custom_call_target="tpu_custom_call" | custom-call | flops 2415919104 | bytes 8388608 | tf_op jit(solution)/shard_map/attention/pallas_call | solution.py:308
  336.3 7.5 %attention.31 = (bf16[128,1536]{1,0:T(8,128)(2,1)S(1)}, bf16[128,1536]{1,0:T(8,128)(2,1)S(1)}) custom-call(bf16[128,4608]{1,0:T(8,128)(2,1)S(1)} %product.62.refs_4_.refs_0_, bf16[128,4608]{1,0:T(8,128)(2,1)S(1)} %product.63.refs_4_.refs_1_, bf16[128,4608]{1,0:T(8,128)(2,1)S(1)} %product.64.refs_4_.refs_2_, bf16[128,4608]{1,0:T(8,128)(2,1)S(1)} %product.65.refs_3_, ...), custom_call_target="tpu_custom_call" | custom-call | flops 2415919104 | bytes 8388608 | tf_op jit(solution)/shard_map/attention/pallas_call | solution.py:308
  347.8 13.5 %all-to-all-start.4 = ((f32[32,8,128]{2,1,0:T(8,128)}), f32[32,8,128]{2,1,0:T(8,128)S(1)}, u32[]{:S(2)}, u32[]{:S(2)}) async-start(f32[32,8,128]{2,1,0:T(8,128)} %select_bitcast_fusion), calls=%async_computation.4 | async-start | bytes 262144 | tf_op jit(solution)/shard_map/all_to_all | solution.py:466
  361.4 10.5 %all-to-all-done.4 = f32[32,8,128]{2,1,0:T(8,128)S(1)} async-done(((f32[32,8,128]{2,1,0:T(8,128)}), f32[32,8,128]{2,1,0:T(8,128)S(1)}, u32[]{:S(2)}, u32[]{:S(2)}) %all-to-all-start.4) | async-done | bytes 131104 | tf_op jit(solution)/shard_map/all_to_all | solution.py:466
  (183 shorter events, 141.4 us)
Async XLA Ops:
  1.5 80.7 %collective-permute-start.1 = (bf16[768,4608]{1,0:T(8,128)(2,1)}, bf16[768,4608]{1,0:T(8,128)(2,1)}, u32[]{:S(2)}, u32[]{:S(2)}) collective-permute-start(bf16[768,4608]{1,0:T(8,128)(2,1)} %bitcast.36), channel_id=1, source_target_pairs={{1,0},{8,9},{17,16},{24,25},{33,32},{40,41},{49,48},{56,57},{65,64... | collective-permute-start | bytes 21233672 | tf_op jit(solution)/shard_map/ppermute | solution.py:41
  4.0 21.3 %all-to-all-start = ((bf16[4,66,1536]{2,1,0:T(8,128)(2,1)}), bf16[4,66,1536]{2,1,0:T(8,128)(2,1)S(1)}, u32[]{:S(2)}, u32[]{:S(2)}) async-start(bf16[4,66,1536]{2,1,0:T(8,128)(2,1)} %pad_maximum_fusion), calls=%async_computation | async-start | bytes 1769472 | tf_op jit(solution)/shard_map/all_to_all | solution.py:372
  10.8 84.7 %collective-permute-start.7 = (bf16[768,1536]{1,0:T(8,128)(2,1)}, bf16[768,1536]{1,0:T(8,128)(2,1)}, u32[]{:S(2)}, u32[]{:S(2)}) collective-permute-start(bf16[768,1536]{1,0:T(8,128)(2,1)} %bitcast.1.own_ref), channel_id=1, source_target_pairs={{1,0},{8,9},{17,16},{24,25},{33,32},{40,41},{49,48},{56,57},{65,64... | collective-permute-start | bytes 7077896 | tf_op jit(solution)/shard_map/ppermute | solution.py:41
  26.4 23.4 %all-to-all-start.1 = ((bf16[8,16,1536]{2,1,0:T(8,128)(2,1)}), bf16[8,16,1536]{2,1,0:T(8,128)(2,1)S(1)}, u32[]{:S(2)}, u32[]{:S(2)}) async-start(bf16[8,16,1536]{2,1,0:T(8,128)(2,1)} %pad_maximum_fusion.1), calls=%async_computation.1 | async-start | bytes 786432 | tf_op jit(solution)/shard_map/all_to_all | solution.py:383
  50.0 9.9 %collective-permute-start = (bf16[256,128]{1,0:T(8,128)(2,1)S(1)}, bf16[256,128]{1,0:T(8,128)(2,1)S(1)}, u32[]{:S(2)}, u32[]{:S(2)}) collective-permute-start(bf16[256,128]{1,0:T(8,128)(2,1)S(1)} %squeeze.33), channel_id=1, source_target_pairs={{80,16},{89,25},{160,32},{169,41},{240,48},{249,57}} | collective-permute-start | bytes 196616 | tf_op jit(solution)/shard_map/ppermute | solution.py:41
  50.8 17.6 %collective-permute-start.2 = (bf16[2,256,128]{2,1,0:T(8,128)(2,1)S(1)}, bf16[2,256,128]{2,1,0:T(8,128)(2,1)S(1)}, u32[]{:S(2)}, u32[]{:S(2)}) collective-permute-start(bf16[2,256,128]{2,1,0:T(8,128)(2,1)S(1)} %reshape.145), channel_id=1, source_target_pairs={{0,192},{9,201},{80,208},{89,217},{160,224},{169,233}} | collective-permute-start | bytes 393224 | tf_op jit(solution)/shard_map/ppermute | solution.py:41
  52.1 12.1 %all-to-all-start.2 = ((bf16[4,8,1536]{2,1,0:T(8,128)(2,1)}), bf16[4,8,1536]{2,1,0:T(8,128)(2,1)S(1)}, u32[]{:S(2)}, u32[]{:S(2)}) async-start(bf16[4,8,1536]{2,1,0:T(8,128)(2,1)} %spread.1), calls=%async_computation.2 | async-start | bytes 196608 | tf_op jit(solution)/shard_map/all_to_all | solution.py:414
  65.0 13.1 %all-to-all-start.3 = ((bf16[8,8,1536]{2,1,0:T(8,128)(2,1)}), bf16[8,8,1536]{2,1,0:T(8,128)(2,1)S(1)}, u32[]{:S(2)}, u32[]{:S(2)}) async-start(bf16[8,8,1536]{2,1,0:T(8,128)(2,1)} %twice.1), calls=%async_computation.3 | async-start | bytes 393216 | tf_op jit(solution)/shard_map/all_to_all | solution.py:417
  78.1 22.1 %collective-permute-start.4 = (bf16[64,1536]{1,0:T(8,128)(2,1)S(1)}, bf16[64,1536]{1,0:T(8,128)(2,1)S(1)}, u32[]{:S(2)}, u32[]{:S(2)}) collective-permute-start(bf16[64,1536]{1,0:T(8,128)(2,1)S(1)} %bitcast.38), channel_id=1, source_target_pairs={{2,0},{11,9},{18,16},{27,25},{34,32},{43,41},{50,48},{59,57},{66,6... | collective-permute-start | bytes 589832 | tf_op jit(solution)/shard_map/ppermute | solution.py:41
  79.4 20.9 %collective-permute-start.5 = (bf16[64,1536]{1,0:T(8,128)(2,1)S(1)}, bf16[64,1536]{1,0:T(8,128)(2,1)S(1)}, u32[]{:S(2)}, u32[]{:S(2)}) collective-permute-start(bf16[64,1536]{1,0:T(8,128)(2,1)S(1)} %bitcast.39), channel_id=1, source_target_pairs={{4,0},{13,9},{20,16},{29,25},{36,32},{45,41},{52,48},{61,57},{68,6... | collective-permute-start | bytes 589832 | tf_op jit(solution)/shard_map/ppermute | solution.py:41
  80.7 19.6 %collective-permute-start.6 = (bf16[64,1536]{1,0:T(8,128)(2,1)S(1)}, bf16[64,1536]{1,0:T(8,128)(2,1)S(1)}, u32[]{:S(2)}, u32[]{:S(2)}) collective-permute-start(bf16[64,1536]{1,0:T(8,128)(2,1)S(1)} %bitcast.40), channel_id=1, source_target_pairs={{6,0},{15,9},{22,16},{31,25},{38,32},{47,41},{54,48},{63,57},{70,6... | collective-permute-start | bytes 589832 | tf_op jit(solution)/shard_map/ppermute | solution.py:41
  110.4 13.2 %collective-permute-start.8 = (bf16[128,1536]{1,0:T(8,128)(2,1)S(1)}, bf16[128,1536]{1,0:T(8,128)(2,1)S(1)}, u32[]{:S(2)}, u32[]{:S(2)}) collective-permute-start(bf16[128,1536]{1,0:T(8,128)(2,1)S(1)} %get-tuple-element.58), channel_id=1, source_target_pairs={{0,64},{9,73},{16,80},{25,89},{32,96},{41,105},{48,112},{57,121}} | collective-permute-start | bytes 1179656 | tf_op jit(solution)/shard_map/ppermute | solution.py:41
  111.7 14.2 %collective-permute-start.9 = (bf16[128,1536]{1,0:T(8,128)(2,1)S(1)}, bf16[128,1536]{1,0:T(8,128)(2,1)S(1)}, u32[]{:S(2)}, u32[]{:S(2)}) collective-permute-start(bf16[128,1536]{1,0:T(8,128)(2,1)S(1)} %get-tuple-element.59.refs_10_), channel_id=1, source_target_pairs={{0,64},{9,73},{16,80},{25,89},{32,96},{41,105},{48,112},{57,121}} | collective-permute-start | bytes 1179656 | tf_op jit(solution)/shard_map/ppermute | solution.py:41
  121.0 9.7 %collective-permute-start.10 = (bf16[128,1536]{1,0:T(8,128)(2,1)S(1)}, bf16[128,1536]{1,0:T(8,128)(2,1)S(1)}, u32[]{:S(2)}, u32[]{:S(2)}) collective-permute-start(bf16[128,1536]{1,0:T(8,128)(2,1)S(1)} %get-tuple-element.60), channel_id=1, source_target_pairs={{0,64},{9,73},{16,80},{25,89},{32,96},{41,105},{48,112},{57,121}} | collective-permute-start | bytes 1179656 | tf_op jit(solution)/shard_map/ppermute | solution.py:41
  122.3 12.6 %collective-permute-start.11 = (bf16[128,1536]{1,0:T(8,128)(2,1)S(1)}, bf16[128,1536]{1,0:T(8,128)(2,1)S(1)}, u32[]{:S(2)}, u32[]{:S(2)}) collective-permute-start(bf16[128,1536]{1,0:T(8,128)(2,1)S(1)} %get-tuple-element.61), channel_id=1, source_target_pairs={{0,64},{9,73},{16,80},{25,89},{32,96},{41,105},{48,112},{57,121}} | collective-permute-start | bytes 1179656 | tf_op jit(solution)/shard_map/ppermute | solution.py:41
  144.7 13.0 %collective-permute-start.12 = (bf16[128,1536]{1,0:T(8,128)(2,1)S(1)}, bf16[128,1536]{1,0:T(8,128)(2,1)S(1)}, u32[]{:S(2)}, u32[]{:S(2)}) collective-permute-start(bf16[128,1536]{1,0:T(8,128)(2,1)S(1)} %get-tuple-element.62), channel_id=1, source_target_pairs={{64,128},{73,137},{80,144},{89,153},{96,160},{105,169},{112,176},{... | collective-permute-start | bytes 1179656 | tf_op jit(solution)/shard_map/ppermute | solution.py:41
  146.1 14.0 %collective-permute-start.13 = (bf16[128,1536]{1,0:T(8,128)(2,1)S(1)}, bf16[128,1536]{1,0:T(8,128)(2,1)S(1)}, u32[]{:S(2)}, u32[]{:S(2)}) collective-permute-start(bf16[128,1536]{1,0:T(8,128)(2,1)S(1)} %get-tuple-element.63.refs_10_), channel_id=1, source_target_pairs={{64,128},{73,137},{80,144},{89,153},{96,160},{105,169},{112,176},{... | collective-permute-start | bytes 1179656 | tf_op jit(solution)/shard_map/ppermute | solution.py:41
  156.4 9.5 %collective-permute-start.15 = (bf16[128,1536]{1,0:T(8,128)(2,1)S(1)}, bf16[128,1536]{1,0:T(8,128)(2,1)S(1)}, u32[]{:S(2)}, u32[]{:S(2)}) collective-permute-start(bf16[128,1536]{1,0:T(8,128)(2,1)S(1)} %get-tuple-element.65), channel_id=1, source_target_pairs={{64,128},{73,137},{80,144},{89,153},{96,160},{105,169},{112,176},{... | collective-permute-start | bytes 1179656 | tf_op jit(solution)/shard_map/ppermute | solution.py:41
  176.6 13.2 %collective-permute-start.16 = (bf16[128,1536]{1,0:T(8,128)(2,1)}, bf16[128,1536]{1,0:T(8,128)(2,1)S(1)}, u32[]{:S(2)}, u32[]{:S(2)}) collective-permute-start(bf16[128,1536]{1,0:T(8,128)(2,1)} %get-tuple-element.66), channel_id=1, source_target_pairs={{128,192},{137,201},{144,208},{153,217},{160,224},{169,233},{176,2... | collective-permute-start | bytes 1179656 | tf_op jit(solution)/shard_map/ppermute | solution.py:41
  177.3 19.8 %collective-permute-start.17 = (bf16[128,1536]{1,0:T(8,128)(2,1)}, bf16[128,1536]{1,0:T(8,128)(2,1)S(1)}, u32[]{:S(2)}, u32[]{:S(2)}) collective-permute-start(bf16[128,1536]{1,0:T(8,128)(2,1)} %get-tuple-element.67.refs_10_), channel_id=1, source_target_pairs={{128,192},{137,201},{144,208},{153,217},{160,224},{169,233},{176,2... | collective-permute-start | bytes 1179656 | tf_op jit(solution)/shard_map/ppermute | solution.py:41
  187.2 12.2 %collective-permute-start.18 = (bf16[128,1536]{1,0:T(8,128)(2,1)}, bf16[128,1536]{1,0:T(8,128)(2,1)S(1)}, u32[]{:S(2)}, u32[]{:S(2)}) collective-permute-start(bf16[128,1536]{1,0:T(8,128)(2,1)} %get-tuple-element.68), channel_id=1, source_target_pairs={{128,192},{137,201},{144,208},{153,217},{160,224},{169,233},{176,2... | collective-permute-start | bytes 1179656 | tf_op jit(solution)/shard_map/ppermute | solution.py:41
  189.1 12.6 %collective-permute-start.19 = (bf16[128,1536]{1,0:T(8,128)(2,1)}, bf16[128,1536]{1,0:T(8,128)(2,1)S(1)}, u32[]{:S(2)}, u32[]{:S(2)}) collective-permute-start(bf16[128,1536]{1,0:T(8,128)(2,1)} %copy-done.10), channel_id=1, source_target_pairs={{128,192},{137,201},{144,208},{153,217},{160,224},{169,233},{176,2... | collective-permute-start | bytes 1179656 | tf_op jit(solution)/shard_map/ppermute | solution.py:41
  239.6 13.7 %collective-permute-start.21 = (bf16[128,1536]{1,0:T(8,128)(2,1)S(1)}, bf16[128,1536]{1,0:T(8,128)(2,1)S(1)}, u32[]{:S(2)}, u32[]{:S(2)}) collective-permute-start(bf16[128,1536]{1,0:T(8,128)(2,1)S(1)} %get-tuple-element.79), channel_id=1, source_target_pairs={{0,64},{9,73},{16,80},{25,89},{32,96},{41,105},{48,112},{57,121}} | collective-permute-start | bytes 1179656 | tf_op jit(solution)/shard_map/ppermute | solution.py:41
  240.9 16.6 %collective-permute-start.22 = (bf16[128,1536]{1,0:T(8,128)(2,1)S(1)}, bf16[128,1536]{1,0:T(8,128)(2,1)S(1)}, u32[]{:S(2)}, u32[]{:S(2)}) collective-permute-start(bf16[128,1536]{1,0:T(8,128)(2,1)S(1)} %get-tuple-element.80.refs_10_), channel_id=1, source_target_pairs={{0,64},{9,73},{16,80},{25,89},{32,96},{41,105},{48,112},{57,121}} | collective-permute-start | bytes 1179656 | tf_op jit(solution)/shard_map/ppermute | solution.py:41
  249.9 13.7 %collective-permute-start.23 = (bf16[128,1536]{1,0:T(8,128)(2,1)S(1)}, bf16[128,1536]{1,0:T(8,128)(2,1)S(1)}, u32[]{:S(2)}, u32[]{:S(2)}) collective-permute-start(bf16[128,1536]{1,0:T(8,128)(2,1)S(1)} %get-tuple-element.81), channel_id=1, source_target_pairs={{0,64},{9,73},{16,80},{25,89},{32,96},{41,105},{48,112},{57,121}} | collective-permute-start | bytes 1179656 | tf_op jit(solution)/shard_map/ppermute | solution.py:41
  251.2 16.6 %collective-permute-start.24 = (bf16[128,1536]{1,0:T(8,128)(2,1)S(1)}, bf16[128,1536]{1,0:T(8,128)(2,1)S(1)}, u32[]{:S(2)}, u32[]{:S(2)}) collective-permute-start(bf16[128,1536]{1,0:T(8,128)(2,1)S(1)} %get-tuple-element.82), channel_id=1, source_target_pairs={{0,64},{9,73},{16,80},{25,89},{32,96},{41,105},{48,112},{57,121}} | collective-permute-start | bytes 1179656 | tf_op jit(solution)/shard_map/ppermute | solution.py:41
  277.7 13.2 %collective-permute-start.25 = (bf16[128,1536]{1,0:T(8,128)(2,1)S(1)}, bf16[128,1536]{1,0:T(8,128)(2,1)S(1)}, u32[]{:S(2)}, u32[]{:S(2)}) collective-permute-start(bf16[128,1536]{1,0:T(8,128)(2,1)S(1)} %get-tuple-element.83), channel_id=1, source_target_pairs={{64,128},{73,137},{80,144},{89,153},{96,160},{105,169},{112,176},{... | collective-permute-start | bytes 1179656 | tf_op jit(solution)/shard_map/ppermute | solution.py:41
  279.0 14.2 %collective-permute-start.26 = (bf16[128,1536]{1,0:T(8,128)(2,1)S(1)}, bf16[128,1536]{1,0:T(8,128)(2,1)S(1)}, u32[]{:S(2)}, u32[]{:S(2)}) collective-permute-start(bf16[128,1536]{1,0:T(8,128)(2,1)S(1)} %get-tuple-element.84.refs_10_), channel_id=1, source_target_pairs={{64,128},{73,137},{80,144},{89,153},{96,160},{105,169},{112,176},{... | collective-permute-start | bytes 1179656 | tf_op jit(solution)/shard_map/ppermute | solution.py:41
  289.6 9.5 %collective-permute-start.28 = (bf16[128,1536]{1,0:T(8,128)(2,1)S(1)}, bf16[128,1536]{1,0:T(8,128)(2,1)S(1)}, u32[]{:S(2)}, u32[]{:S(2)}) collective-permute-start(bf16[128,1536]{1,0:T(8,128)(2,1)S(1)} %get-tuple-element.86), channel_id=1, source_target_pairs={{64,128},{73,137},{80,144},{89,153},{96,160},{105,169},{112,176},{... | collective-permute-start | bytes 1179656 | tf_op jit(solution)/shard_map/ppermute | solution.py:41
  308.9 10.5 %collective-permute-start.29 = (bf16[128,1536]{1,0:T(8,128)(2,1)S(1)}, bf16[128,1536]{1,0:T(8,128)(2,1)S(1)}, u32[]{:S(2)}, u32[]{:S(2)}) collective-permute-start(bf16[128,1536]{1,0:T(8,128)(2,1)S(1)} %get-tuple-element.87), channel_id=1, source_target_pairs={{128,192},{137,201},{144,208},{153,217},{160,224},{169,233},{176,2... | collective-permute-start | bytes 1179656 | tf_op jit(solution)/shard_map/ppermute | solution.py:41
  309.6 12.1 %collective-permute-start.30 = (bf16[128,1536]{1,0:T(8,128)(2,1)S(1)}, bf16[128,1536]{1,0:T(8,128)(2,1)S(1)}, u32[]{:S(2)}, u32[]{:S(2)}) collective-permute-start(bf16[128,1536]{1,0:T(8,128)(2,1)S(1)} %get-tuple-element.88.refs_10_), channel_id=1, source_target_pairs={{128,192},{137,201},{144,208},{153,217},{160,224},{169,233},{176,2... | collective-permute-start | bytes 1179656 | tf_op jit(solution)/shard_map/ppermute | solution.py:41
  347.8 24.0 %all-to-all-start.4 = ((f32[32,8,128]{2,1,0:T(8,128)}), f32[32,8,128]{2,1,0:T(8,128)S(1)}, u32[]{:S(2)}, u32[]{:S(2)}) async-start(f32[32,8,128]{2,1,0:T(8,128)} %select_bitcast_fusion), calls=%async_computation.4 | async-start | bytes 262144 | tf_op jit(solution)/shard_map/all_to_all | solution.py:466
  (27 other events, 391.4 us)

commit v2 on v1

--- a/solution.py
+++ b/solution.py
@@ -57,40 +57,42 @@
     return pltpu.CompilerParams(vmem_limit_bytes=VMEM)
 
 
-def joined_kernel(core_ref, own_ref, other_ref, *refs):
-    out_ref, sems = refs[-2:]
+def joined_kernel(core_ref, own_ref, *refs, pieces):
+    piece_refs, (out_ref, sems) = refs[:pieces], refs[-2:]
     half = own_ref.shape[0]
     core = core_ref[0]
-    copies = (
-        pltpu.make_async_copy(
-            own_ref, out_ref.at[pl.ds(pl.multiple_of(core * half, 16), half), :], sems.at[0]
-        ),
-        pltpu.make_async_copy(
-            other_ref, out_ref.at[pl.ds(pl.multiple_of((1 - core) * half, 16), half), :], sems.at[1]
-        ),
-    )
+
+    def target(start, count):
+        return out_ref.at[pl.ds(pl.multiple_of(start, 16), count), :]
+
+    copies = [pltpu.make_async_copy(own_ref, target(core * half, half), sems.at[0])]
+    done = 0
+    for k, ref in enumerate(piece_refs):
+        count = ref.shape[0]
+        copies.append(
+            pltpu.make_async_copy(ref, target((1 - core) * half + done, count), sems.at[k + 1])
+        )
+        done += count
     for copy in copies:
         copy.start()
     for copy in copies:
         copy.wait()
 
 
-def joined(core, own, other, after):
+def joined(core, own, pieces, after):
     half, columns = own.shape
     return pl.pallas_call(
-        joined_kernel,
+        functools.partial(joined_kernel, pieces=len(pieces)),
         in_specs=[scalar()]
-        + [pl.BlockSpec(memory_space=pltpu.HBM)] * 2
+        + [pl.BlockSpec(memory_space=pltpu.HBM)] * (1 + len(pieces))
         + [pl.BlockSpec(memory_space=pl.ANY)] * len(after),
         out_specs=whole(),
         out_shape=jax.ShapeDtypeStruct((2 * half, columns), BF),
-        scratch_shapes=[pltpu.SemaphoreType.DMA((2,))],
-        compiler_params=params(),
-        cost_estimate=pl.CostEstimate(
-            flops=0, bytes_accessed=8 * half * columns, transcendentals=0
-        ),
+        scratch_shapes=[pltpu.SemaphoreType.DMA((1 + len(pieces),))],
+        compiler_params=params(),
+        cost_estimate=pl.CostEstimate(flops=0, bytes_accessed=1024, transcendentals=0),
         name="joined",
-    )(core, own, other, *after)
+    )(core, own, *pieces, *after)
 
 
 def normal(values):
@@ -217,20 +219,21 @@
     )(parts)
 
 
-def twice_kernel(rows_ref, out_ref):
+def twice_kernel(rows_ref, *refs):
+    out_ref = refs[-1]
     for k in range(out_ref.shape[0]):
         out_ref[k] = rows_ref[k * rows_ref.shape[0] // out_ref.shape[0]]
 
 
-def twice(rows, copies):
+def twice(rows, copies, after):
     return pl.pallas_call(
         twice_kernel,
-        in_specs=[whole()],
+        in_specs=[whole()] + [pl.BlockSpec(memory_space=pl.ANY)] * len(after),
         out_specs=whole(),
         out_shape=jax.ShapeDtypeStruct((copies,) + rows.shape[1:], BF),
         compiler_params=params(),
         name="twice",
-    )(rows)
+    )(rows, *after)
 
 
 def attention_kernel(*refs, queries, blocks):
@@ -360,35 +363,33 @@
 
     text = lax.dynamic_index_in_dim(text_rows[:, 0], x, 0, keepdims=False)
     partial = jnp.dot(text, context_weight, preferred_element_type=F32).astype(BF)
-    attn_mine, proj_mine, partial = lax.optimization_barrier(
-        (w_attention[0], w_project[0], partial)
-    )
+    attn_mine, proj_mine = w_attention[0], w_project[0]
+    third = attn_mine.shape[0] // 3
+
+    def beside(operand, piece):
+        operand, piece = lax.optimization_barrier((operand, piece))
+        return operand, across(piece)
+
     quarter = text_total // Y
     eighth = quarter // Z
     latent = latent_noise[0, 0].reshape(1, rows_here * latent_width)
     high = latent.astype(BF)
     low = (latent - high.astype(F32)).astype(BF)
     both = jnp.pad(jnp.concatenate([high, low], 0), ((0, 0), (0, width - latent.shape[1])))
-    parts = lax.all_to_all(
-        jnp.concatenate(
-            [partial.reshape(Y, quarter, width), jnp.broadcast_to(both[None], (Y, 2, width))], 1
-        ),
-        "y",
-        split_axis=0,
-        concat_axis=0,
-        tiled=True,
-    )
+    message = jnp.concatenate(
+        [partial.reshape(Y, quarter, width), jnp.broadcast_to(both[None], (Y, 2, width))], 1
+    )
+    message, piece = beside(message, attn_mine[:third])
+    attn_pieces = [piece]
+    parts = lax.all_to_all(message, "y", split_axis=0, concat_axis=0, tiled=True)
     summed = jnp.sum(parts[:, :quarter].astype(F32), axis=0).astype(BF)
     both = parts[:, quarter:].reshape(1, 2 * Y, width)
-    parts = lax.all_to_all(
-        jnp.concatenate(
-            [summed.reshape(Z, eighth, width), jnp.broadcast_to(both, (Z, 2 * Y, width))], 1
-        ),
-        "z",
-        split_axis=0,
-        concat_axis=0,
-        tiled=True,
-    )
+    message = jnp.concatenate(
+        [summed.reshape(Z, eighth, width), jnp.broadcast_to(both, (Z, 2 * Y, width))], 1
+    )
+    message, piece = beside(message, attn_mine[third : 2 * third])
+    attn_pieces.append(piece)
+    parts = lax.all_to_all(message, "z", split_axis=0, concat_axis=0, tiled=True)
     both = parts[:, eighth:].reshape(patches // rows_here, 2, width)[:, :, : latent.shape[1]]
     both = jnp.transpose(both, (1, 0, 2)).reshape(2, patches * latent_width // 128, 128)
 
@@ -407,14 +408,25 @@
         for part in range(3)
     )
 
-    ready = (first, latent, bias, *shifts, *scales, *gates)
-    attn_weight = joined(core, attn_mine, across(attn_mine), ready)
-    proj_weight = joined(core, proj_mine, across(proj_mine), (attn_weight,))
-
-    shared = lax.all_to_all(
-        spread_over(parts, X, eighth), "x", split_axis=0, concat_axis=0, tiled=True
-    )
-    shared = lax.all_to_all(twice(shared, Z), "z", split_axis=0, concat_axis=0, tiled=True)
+    message, piece = beside(spread_over(parts, X, eighth), attn_mine[2 * third :])
+    attn_pieces.append(piece)
+    shared = lax.all_to_all(message, "x", split_axis=0, concat_axis=0, tiled=True)
+    early = (first, latent, bias, w_final, w_embed, *shifts, *scales, *gates)
+    message, piece = beside(twice(shared, Z, early), proj_mine)
+    shared = lax.all_to_all(message, "z", split_axis=0, concat_axis=0, tiled=True)
+    ready = (first, latent, bias, w_final, w_embed, *shifts, *scales, *gates)
+    attn_weight = joined(core, attn_mine, attn_pieces, ready)
+    hidden = embedded(first, w_embed)
+
+    def products(hidden, step):
+        done = []
+        for part in hidden:
+            done.append(
+                product([part], attn_weight, 0, (shifts[step], scales[step]), tuple(done[-1:]))
+            )
+        return done
+
+    projected = products(hidden, 0)
     pieces = [shared.reshape(quarter, width)]
     for k in range(1, Y):
         pieces.append(
@@ -423,19 +435,14 @@
                 [((a, b, k, b % C), (a, b, 0, b % C)) for a in range(X) for b in range(Z)],
             )
         )
+    proj_weight = joined(core, proj_mine, [piece], ready)
     keys = product(pieces, attn_weight, width)
 
-    hidden = embedded(first, w_embed)
     for turn in range(STEPS * BLOCKS):
         step, block = divmod(turn, BLOCKS)
         gate = gates[step]
-        projected = []
-        for part in hidden:
-            projected.append(
-                product(
-                    [part], attn_weight, 0, (shifts[step], scales[step]), tuple(projected[-1:])
-                )
-            )
+        if turn > 0:
+            projected = products(hidden, step)
         following = []
         for i in range(0, CHUNKS, TOGETHER):
             queries = tuple(range(i, i + TOGETHER))

time: 379 us -> 379 us (level)
    unnamed x42 -> x20, local copies, waits for them, and re-layouts: 10.1 us -> 3.32 us
    slice x0 -> x1, local copies, waits for them, and re-layouts: none -> 6.12 us  [on_device(): attn_mine[2 * third:]]
    ppermute x34 -> x36, waiting for transfers between devices: 16.3 us -> 21.8 us  [move(): return lax.ppermute(value, AXES, [(flat(*a), flat(*b)) for a, b in pairs])]
    ppermute x34 -> x36, starting transfers between devices: 38.6 us -> 41.4 us  [move(): return lax.ppermute(value, AXES, [(flat(*a), flat(*b)) for a, b in pairs])]
  transfers between devices with their start and end apart: 39 -> 41, of which waited for: 14 -> 13; matrix products, arithmetic and copies ran while one was open for 2% -> 1% of each run, Pallas kernels for 28% -> 28%
where the time goes in v2:
time: 379 us; the launch traced here: 373 us
  Pallas kernels  209 us (55%)
  starting transfers between devices  79.1 us (21%)
  waiting for transfers between devices  64.7 us (17%)
  local copies, waits for them, and re-layouts  12.3 us (3%)
  other arithmetic  5.29 us (1%)
    pallas_call x16, Pallas kernels, attention(): pl.pallas_call(functools.partial(attention_kernel, queries=queries, block...  121 us
    pallas_call x33, Pallas kernels, product(): pl.pallas_call(functools.partial(product_kernel, pieces=len(rows), column...  74.9 us
    ppermute x36, starting transfers between devices, move(): return lax.ppermute(value, AXES, [(flat(*a), flat(*b)) for a, b in pairs])  41.4 us
    ppermute x36, waiting for transfers between devices, move(): return lax.ppermute(value, AXES, [(flat(*a), flat(*b)) for a, b in pairs])  21.8 us
    all_to_all x2, waiting for transfers between devices, on_device(): lax.all_to_all(message, 'z', split_axis=0, concat_axis=0, tiled=True)  15.7 us
    all_to_all x1, starting transfers between devices, on_device(): lax.all_to_all(latent.reshape(Z * Y, rows_here * latent_width // 128, 128...  13.3 us
    all_to_all x1, waiting for transfers between devices, on_device(): lax.all_to_all(message, 'y', split_axis=0, concat_axis=0, tiled=True)  12.7 us
    all_to_all x2, starting transfers between devices, on_device(): lax.all_to_all(message, 'z', split_axis=0, concat_axis=0, tiled=True)  12 us
  transfers between devices with their start and end apart: 41, of which 13 were waited for; matrix products, arithmetic and copies ran while one was open for 1% of the time, Pallas kernels for 28%

profile of v2, /device:TPU:2, one launch (start us, length us, event | category | flops | bytes accessed | tf_op | source)
XLA Modules:
  0.0 372.9 jit_solution(4154934574348045349)
XLA Ops:
  0.9 6.1 %slice_bitcast_fusion = (bf16[256,4608]{1,0:T(8,128)(2,1)}, bf16[256,4608]{1,0:T(8,128)(2,1)}, bf16[256,4608]{1,0:T(8,128)(2,1)}) fusion(bf16[1,768,4608]{2,1,0:T(8,128)(2,1)} %param.16), kind=kLoop, calls=%fused_computation.1 | loop fusion | bytes 14155776 | tf_op jit(solution)/shard_map/slice | solution.py:411
  9.3 4.6 %all-to-all-start = ((bf16[4,66,1536]{2,1,0:T(8,128)(2,1)}), bf16[4,66,1536]{2,1,0:T(8,128)(2,1)S(1)}, u32[]{:S(2)}, u32[]{:S(2)}) async-start(bf16[4,66,1536]{2,1,0:T(8,128)(2,1)} %pad_maximum_fusion), calls=%async_computation | async-start | bytes 1769472 | tf_op jit(solution)/shard_map/all_to_all | solution.py:384
  14.6 12.7 %all-to-all-done = bf16[4,66,1536]{2,1,0:T(8,128)(2,1)S(1)} async-done(((bf16[4,66,1536]{2,1,0:T(8,128)(2,1)}), bf16[4,66,1536]{2,1,0:T(8,128)(2,1)S(1)}, u32[]{:S(2)}, u32[]{:S(2)}) %all-to-all-start) | async-done | bytes 811040 | tf_op jit(solution)/shard_map/all_to_all | solution.py:384
  28.2 8.6 %all-to-all-start.1 = ((bf16[8,16,1536]{2,1,0:T(8,128)(2,1)}), bf16[8,16,1536]{2,1,0:T(8,128)(2,1)S(1)}, u32[]{:S(2)}, u32[]{:S(2)}) async-start(bf16[8,16,1536]{2,1,0:T(8,128)(2,1)} %pad_maximum_fusion.1), calls=%async_computation.1 | async-start | bytes 786432 | tf_op jit(solution)/shard_map/all_to_all | solution.py:392
  43.9 6.4 %all-to-all-done.1.parts_ref = bf16[8,16,1536]{2,1,0:T(8,128)(2,1)S(1)} async-done(((bf16[8,16,1536]{2,1,0:T(8,128)(2,1)}), bf16[8,16,1536]{2,1,0:T(8,128)(2,1)S(1)}, u32[]{:S(2)}, u32[]{:S(2)}) %all-to-all-start.1) | async-done | bytes 393248 | tf_op jit(solution)/shard_map/all_to_all | solution.py:392
  54.2 7.8 %all-to-all-start.2 = ((bf16[4,8,1536]{2,1,0:T(8,128)(2,1)}), bf16[4,8,1536]{2,1,0:T(8,128)(2,1)S(1)}, u32[]{:S(2)}, u32[]{:S(2)}) async-start(bf16[4,8,1536]{2,1,0:T(8,128)(2,1)} %spread.1), calls=%async_computation.2 | async-start | bytes 196608 | tf_op jit(solution)/shard_map/all_to_all | solution.py:413
  62.3 4.1 %all-to-all-done.2.rows_ref = bf16[4,8,1536]{2,1,0:T(8,128)(2,1)S(1)} async-done(((bf16[4,8,1536]{2,1,0:T(8,128)(2,1)}), bf16[4,8,1536]{2,1,0:T(8,128)(2,1)S(1)}, u32[]{:S(2)}, u32[]{:S(2)}) %all-to-all-start.2) | async-done | bytes 98336 | tf_op jit(solution)/shard_map/all_to_all | solution.py:413
  68.3 3.4 all-to-all-start.3
  72.3 9.2 %all-to-all-done.3 = bf16[8,8,1536]{2,1,0:T(8,128)(2,1)S(1)} async-done(((bf16[8,8,1536]{2,1,0:T(8,128)(2,1)}), bf16[8,8,1536]{2,1,0:T(8,128)(2,1)S(1)}, u32[]{:S(2)}, u32[]{:S(2)}) %all-to-all-start.3) | async-done | bytes 196640 | tf_op jit(solution)/shard_map/all_to_all | solution.py:416
  85.6 3.0 copy-done.2
  88.7 3.6 joined.2.refs_1_.refs_4_
  101.4 2.6 product.37.refs_4_
  105.9 7.5 %attention.16 = (bf16[128,1536]{1,0:T(8,128)(2,1)S(1)}, bf16[128,1536]{1,0:T(8,128)(2,1)S(1)}) custom-call(bf16[128,4608]{1,0:T(8,128)(2,1)S(1)} %product.33.refs_4_.refs_0_, bf16[128,4608]{1,0:T(8,128)(2,1)S(1)} %product.34.refs_4_.refs_1_, bf16[128,4608]{1,0:T(8,128)(2,1)S(1)} %product.35.refs_4_.refs_2_, bf16[128,4608]{1,0:T(8,128)(2,1)S(1)} %product.36.refs_3_, ...), custom_call_target="tpu_custom_call" | custom-call | flops 2415919104 | bytes 8388608 | tf_op jit(solution)/shard_map/attention/pallas_call | solution.py:311
  116.4 7.5 %attention.17 = (bf16[128,1536]{1,0:T(8,128)(2,1)S(1)}, bf16[128,1536]{1,0:T(8,128)(2,1)S(1)}) custom-call(bf16[128,4608]{1,0:T(8,128)(2,1)S(1)} %product.33.refs_4_.refs_0_, bf16[128,4608]{1,0:T(8,128)(2,1)S(1)} %product.34.refs_4_.refs_1_, bf16[128,4608]{1,0:T(8,128)(2,1)S(1)} %product.35.refs_4_.refs_2_, bf16[128,4608]{1,0:T(8,128)(2,1)S(1)} %product.36.refs_3_, ...), custom_call_target="tpu_custom_call" | custom-call | flops 2415919104 | bytes 8388608 | tf_op jit(solution)/shard_map/attention/pallas_call | solution.py:311
  140.2 7.5 %attention.18 = (bf16[128,1536]{1,0:T(8,128)(2,1)S(1)}, bf16[128,1536]{1,0:T(8,128)(2,1)S(1)}) custom-call(bf16[128,4608]{1,0:T(8,128)(2,1)S(1)} %product.38.refs_4_.refs_0_, bf16[128,4608]{1,0:T(8,128)(2,1)S(1)} %product.39.refs_4_.refs_1_, bf16[128,4608]{1,0:T(8,128)(2,1)S(1)} %product.40.refs_4_.refs_2_, bf16[128,4608]{1,0:T(8,128)(2,1)S(1)} %product.41.refs_3_, ...), custom_call_target="tpu_custom_call" | custom-call | flops 2415919104 | bytes 8388608 | tf_op jit(solution)/shard_map/attention/pallas_call | solution.py:311
  150.5 7.5 %attention.19 = (bf16[128,1536]{1,0:T(8,128)(2,1)S(1)}, bf16[128,1536]{1,0:T(8,128)(2,1)S(1)}) custom-call(bf16[128,4608]{1,0:T(8,128)(2,1)S(1)} %product.38.refs_4_.refs_0_, bf16[128,4608]{1,0:T(8,128)(2,1)S(1)} %product.39.refs_4_.refs_1_, bf16[128,4608]{1,0:T(8,128)(2,1)S(1)} %product.40.refs_4_.refs_2_, bf16[128,4608]{1,0:T(8,128)(2,1)S(1)} %product.41.refs_3_, ...), custom_call_target="tpu_custom_call" | custom-call | flops 2415919104 | bytes 8388608 | tf_op jit(solution)/shard_map/attention/pallas_call | solution.py:311
  171.1 7.5 %attention.20 = (bf16[128,1536]{1,0:T(8,128)(2,1)S(1)}, bf16[128,1536]{1,0:T(8,128)(2,1)S(1)}) custom-call(bf16[128,4608]{1,0:T(8,128)(2,1)S(1)} %product.42.refs_4_.refs_0_, bf16[128,4608]{1,0:T(8,128)(2,1)S(1)} %product.43.refs_4_.refs_1_, bf16[128,4608]{1,0:T(8,128)(2,1)S(1)} %product.44.refs_4_.refs_2_, bf16[128,4608]{1,0:T(8,128)(2,1)S(1)} %product.45.refs_3_, ...), custom_call_target="tpu_custom_call" | custom-call | flops 2415919104 | bytes 8388608 | tf_op jit(solution)/shard_map/attention/pallas_call | solution.py:311
  180.3 7.5 %attention.21 = (bf16[128,1536]{1,0:T(8,128)(2,1)S(1)}, bf16[128,1536]{1,0:T(8,128)(2,1)S(1)}) custom-call(bf16[128,4608]{1,0:T(8,128)(2,1)S(1)} %product.42.refs_4_.refs_0_, bf16[128,4608]{1,0:T(8,128)(2,1)S(1)} %product.43.refs_4_.refs_1_, bf16[128,4608]{1,0:T(8,128)(2,1)S(1)} %product.44.refs_4_.refs_2_, bf16[128,4608]{1,0:T(8,128)(2,1)S(1)} %product.45.refs_3_, ...), custom_call_target="tpu_custom_call" | custom-call | flops 2415919104 | bytes 8388608 | tf_op jit(solution)/shard_map/attention/pallas_call | solution.py:311
  198.4 8.0 %attention.22 = (bf16[128,1536]{1,0:T(8,128)(2,1)S(1)}, bf16[128,1536]{1,0:T(8,128)(2,1)S(1)}) custom-call(bf16[128,4608]{1,0:T(8,128)(2,1)S(1)} %product.46.refs_4_.refs_0_, bf16[128,4608]{1,0:T(8,128)(2,1)S(1)} %product.47.refs_4_.refs_1_, bf16[128,4608]{1,0:T(8,128)(2,1)S(1)} %product.48.refs_4_.refs_2_, bf16[128,4608]{1,0:T(8,128)(2,1)S(1)} %product.49.refs_3_, ...), custom_call_target="tpu_custom_call" | custom-call | flops 2415919104 | bytes 8388608 | tf_op jit(solution)/shard_map/attention/pallas_call | solution.py:311
  206.3 7.5 %attention.23 = (bf16[128,1536]{1,0:T(8,128)(2,1)S(1)}, bf16[128,1536]{1,0:T(8,128)(2,1)S(1)}) custom-call(bf16[128,4608]{1,0:T(8,128)(2,1)S(1)} %product.46.refs_4_.refs_0_, bf16[128,4608]{1,0:T(8,128)(2,1)S(1)} %product.47.refs_4_.refs_1_, bf16[128,4608]{1,0:T(8,128)(2,1)S(1)} %product.48.refs_4_.refs_2_, bf16[128,4608]{1,0:T(8,128)(2,1)S(1)} %product.49.refs_3_, ...), custom_call_target="tpu_custom_call" | custom-call | flops 2415919104 | bytes 8388608 | tf_op jit(solution)/shard_map/attention/pallas_call | solution.py:311
  226.3 7.6 %attention.24 = (bf16[128,1536]{1,0:T(8,128)(2,1)S(1)}, bf16[128,1536]{1,0:T(8,128)(2,1)S(1)}) custom-call(bf16[128,4608]{1,0:T(8,128)(2,1)S(1)} %product.50.refs_4_.refs_0_, bf16[128,4608]{1,0:T(8,128)(2,1)S(1)} %product.51.refs_4_.refs_1_, bf16[128,4608]{1,0:T(8,128)(2,1)S(1)} %product.52.refs_4_.refs_2_, bf16[128,4608]{1,0:T(8,128)(2,1)S(1)} %product.53.refs_3_, ...), custom_call_target="tpu_custom_call" | custom-call | flops 2415919104 | bytes 8388608 | tf_op jit(solution)/shard_map/attention/pallas_call | solution.py:311
  236.6 7.6 %attention.25 = (bf16[128,1536]{1,0:T(8,128)(2,1)S(1)}, bf16[128,1536]{1,0:T(8,128)(2,1)S(1)}) custom-call(bf16[128,4608]{1,0:T(8,128)(2,1)S(1)} %product.50.refs_4_.refs_0_, bf16[128,4608]{1,0:T(8,128)(2,1)S(1)} %product.51.refs_4_.refs_1_, bf16[128,4608]{1,0:T(8,128)(2,1)S(1)} %product.52.refs_4_.refs_2_, bf16[128,4608]{1,0:T(8,128)(2,1)S(1)} %product.53.refs_3_, ...), custom_call_target="tpu_custom_call" | custom-call | flops 2415919104 | bytes 8388608 | tf_op jit(solution)/shard_map/attention/pallas_call | solution.py:311
  246.8 6.7 %collective-permute-done.23.refs_0_.refs_8_ = bf16[128,1536]{1,0:T(8,128)(2,1)S(1)} collective-permute-done((bf16[128,1536]{1,0:T(8,128)(2,1)S(1)}, bf16[128,1536]{1,0:T(8,128)(2,1)S(1)}, u32[]{:S(2)}, u32[]{:S(2)}) %collective-permute-start.23) | collective-permute-done | bytes 393248 | tf_op jit(solution)/shard_map/ppermute | solution.py:41
  260.0 3.9 %collective-permute-done.25.refs_0_.refs_8_ = bf16[128,1536]{1,0:T(8,128)(2,1)S(1)} collective-permute-done((bf16[128,1536]{1,0:T(8,128)(2,1)S(1)}, bf16[128,1536]{1,0:T(8,128)(2,1)S(1)}, u32[]{:S(2)}, u32[]{:S(2)}) %collective-permute-start.25) | collective-permute-done | bytes 393248 | tf_op jit(solution)/shard_map/ppermute | solution.py:41
  270.4 7.6 %attention.26 = (bf16[128,1536]{1,0:T(8,128)(2,1)S(1)}, bf16[128,1536]{1,0:T(8,128)(2,1)S(1)}) custom-call(bf16[128,4608]{1,0:T(8,128)(2,1)S(1)} %product.54.refs_4_.refs_0_, bf16[128,4608]{1,0:T(8,128)(2,1)S(1)} %product.55.refs_4_.refs_1_, bf16[128,4608]{1,0:T(8,128)(2,1)S(1)} %product.56.refs_4_.refs_2_, bf16[128,4608]{1,0:T(8,128)(2,1)S(1)} %product.57.refs_3_, ...), custom_call_target="tpu_custom_call" | custom-call | flops 2415919104 | bytes 8388608 | tf_op jit(solution)/shard_map/attention/pallas_call | solution.py:311
  281.1 7.6 %attention.27 = (bf16[128,1536]{1,0:T(8,128)(2,1)S(1)}, bf16[128,1536]{1,0:T(8,128)(2,1)S(1)}) custom-call(bf16[128,4608]{1,0:T(8,128)(2,1)S(1)} %product.54.refs_4_.refs_0_, bf16[128,4608]{1,0:T(8,128)(2,1)S(1)} %product.55.refs_4_.refs_1_, bf16[128,4608]{1,0:T(8,128)(2,1)S(1)} %product.56.refs_4_.refs_2_, bf16[128,4608]{1,0:T(8,128)(2,1)S(1)} %product.57.refs_3_, ...), custom_call_target="tpu_custom_call" | custom-call | flops 2415919104 | bytes 8388608 | tf_op jit(solution)/shard_map/attention/pallas_call | solution.py:311
  301.7 7.6 %attention.28 = (bf16[128,1536]{1,0:T(8,128)(2,1)S(1)}, bf16[128,1536]{1,0:T(8,128)(2,1)S(1)}) custom-call(bf16[128,4608]{1,0:T(8,128)(2,1)S(1)} %product.58.refs_4_.refs_0_, bf16[128,4608]{1,0:T(8,128)(2,1)S(1)} %product.59.refs_4_.refs_1_, bf16[128,4608]{1,0:T(8,128)(2,1)S(1)} %product.60.refs_4_.refs_2_, bf16[128,4608]{1,0:T(8,128)(2,1)S(1)} %product.61.refs_3_, ...), custom_call_target="tpu_custom_call" | custom-call | flops 2415919104 | bytes 8388608 | tf_op jit(solution)/shard_map/attention/pallas_call | solution.py:311
  310.8 7.6 %attention.29 = (bf16[128,1536]{1,0:T(8,128)(2,1)S(1)}, bf16[128,1536]{1,0:T(8,128)(2,1)S(1)}) custom-call(bf16[128,4608]{1,0:T(8,128)(2,1)S(1)} %product.58.refs_4_.refs_0_, bf16[128,4608]{1,0:T(8,128)(2,1)S(1)} %product.59.refs_4_.refs_1_, bf16[128,4608]{1,0:T(8,128)(2,1)S(1)} %product.60.refs_4_.refs_2_, bf16[128,4608]{1,0:T(8,128)(2,1)S(1)} %product.61.refs_3_, ...), custom_call_target="tpu_custom_call" | custom-call | flops 2415919104 | bytes 8388608 | tf_op jit(solution)/shard_map/attention/pallas_call | solution.py:311
  328.9 7.8 %attention.30 = (bf16[128,1536]{1,0:T(8,128)(2,1)S(1)}, bf16[128,1536]{1,0:T(8,128)(2,1)S(1)}) custom-call(bf16[128,4608]{1,0:T(8,128)(2,1)S(1)} %product.62.refs_4_.refs_0_, bf16[128,4608]{1,0:T(8,128)(2,1)S(1)} %product.63.refs_4_.refs_1_, bf16[128,4608]{1,0:T(8,128)(2,1)S(1)} %product.64.refs_4_.refs_2_, bf16[128,4608]{1,0:T(8,128)(2,1)S(1)} %product.65.refs_3_, ...), custom_call_target="tpu_custom_call" | custom-call | flops 2415919104 | bytes 8388608 | tf_op jit(solution)/shard_map/attention/pallas_call | solution.py:311
  336.7 7.6 %attention.31 = (bf16[128,1536]{1,0:T(8,128)(2,1)S(1)}, bf16[128,1536]{1,0:T(8,128)(2,1)S(1)}) custom-call(bf16[128,4608]{1,0:T(8,128)(2,1)S(1)} %product.62.refs_4_.refs_0_, bf16[128,4608]{1,0:T(8,128)(2,1)S(1)} %product.63.refs_4_.refs_1_, bf16[128,4608]{1,0:T(8,128)(2,1)S(1)} %product.64.refs_4_.refs_2_, bf16[128,4608]{1,0:T(8,128)(2,1)S(1)} %product.65.refs_3_, ...), custom_call_target="tpu_custom_call" | custom-call | flops 2415919104 | bytes 8388608 | tf_op jit(solution)/shard_map/attention/pallas_call | solution.py:311
  348.2 13.3 %all-to-all-start.4 = ((f32[32,8,128]{2,1,0:T(8,128)}), f32[32,8,128]{2,1,0:T(8,128)S(1)}, u32[]{:S(2)}, u32[]{:S(2)}) async-start(f32[32,8,128]{2,1,0:T(8,128)} %select_bitcast_fusion), calls=%async_computation.4 | async-start | bytes 262144 | tf_op jit(solution)/shard_map/all_to_all | solution.py:473
  361.6 10.5 %all-to-all-done.4 = f32[32,8,128]{2,1,0:T(8,128)S(1)} async-done(((f32[32,8,128]{2,1,0:T(8,128)}), f32[32,8,128]{2,1,0:T(8,128)S(1)}, u32[]{:S(2)}, u32[]{:S(2)}) %all-to-all-start.4) | async-done | bytes 131104 | tf_op jit(solution)/shard_map/all_to_all | solution.py:473
  (164 shorter events, 143.4 us)
Async XLA Ops:
  9.3 17.9 %all-to-all-start = ((bf16[4,66,1536]{2,1,0:T(8,128)(2,1)}), bf16[4,66,1536]{2,1,0:T(8,128)(2,1)S(1)}, u32[]{:S(2)}, u32[]{:S(2)}) async-start(bf16[4,66,1536]{2,1,0:T(8,128)(2,1)} %pad_maximum_fusion), calls=%async_computation | async-start | bytes 1769472 | tf_op jit(solution)/shard_map/all_to_all | solution.py:384
  28.2 22.1 %all-to-all-start.1 = ((bf16[8,16,1536]{2,1,0:T(8,128)(2,1)}), bf16[8,16,1536]{2,1,0:T(8,128)(2,1)S(1)}, u32[]{:S(2)}, u32[]{:S(2)}) async-start(bf16[8,16,1536]{2,1,0:T(8,128)(2,1)} %pad_maximum_fusion.1), calls=%async_computation.1 | async-start | bytes 786432 | tf_op jit(solution)/shard_map/all_to_all | solution.py:392
  39.9 43.0 %collective-permute-start.1 = (bf16[256,4608]{1,0:T(8,128)(2,1)}, bf16[256,4608]{1,0:T(8,128)(2,1)}, u32[]{:S(2)}, u32[]{:S(2)}) collective-permute-start(bf16[256,4608]{1,0:T(8,128)(2,1)} %get-tuple-element.59), channel_id=1, source_target_pairs={{1,0},{8,9},{17,16},{24,25},{33,32},{40,41},{49,48},{56,57},{65,64... | collective-permute-start | bytes 7077896 | tf_op jit(solution)/shard_map/ppermute | solution.py:41
  42.6 41.5 %collective-permute-start.2 = (bf16[256,4608]{1,0:T(8,128)(2,1)}, bf16[256,4608]{1,0:T(8,128)(2,1)}, u32[]{:S(2)}, u32[]{:S(2)}) collective-permute-start(bf16[256,4608]{1,0:T(8,128)(2,1)} %get-tuple-element.60), channel_id=1, source_target_pairs={{1,0},{8,9},{17,16},{24,25},{33,32},{40,41},{49,48},{56,57},{65,64... | collective-permute-start | bytes 7077896 | tf_op jit(solution)/shard_map/ppermute | solution.py:41
  50.6 11.4 %collective-permute-start = (bf16[256,128]{1,0:T(8,128)(2,1)S(1)}, bf16[256,128]{1,0:T(8,128)(2,1)S(1)}, u32[]{:S(2)}, u32[]{:S(2)}) collective-permute-start(bf16[256,128]{1,0:T(8,128)(2,1)S(1)} %squeeze.31), channel_id=1, source_target_pairs={{80,16},{89,25},{160,32},{169,41},{240,48},{249,57}} | collective-permute-start | bytes 196616 | tf_op jit(solution)/shard_map/ppermute | solution.py:41
  52.1 33.5 %collective-permute-start.3 = (bf16[256,4608]{1,0:T(8,128)(2,1)}, bf16[256,4608]{1,0:T(8,128)(2,1)}, u32[]{:S(2)}, u32[]{:S(2)}) collective-permute-start(bf16[256,4608]{1,0:T(8,128)(2,1)} %get-tuple-element.61), channel_id=1, source_target_pairs={{1,0},{8,9},{17,16},{24,25},{33,32},{40,41},{49,48},{56,57},{65,64... | collective-permute-start | bytes 7077896 | tf_op jit(solution)/shard_map/ppermute | solution.py:41
  53.5 8.6 %collective-permute-start.4 = (bf16[2,256,128]{2,1,0:T(8,128)(2,1)S(1)}, bf16[2,256,128]{2,1,0:T(8,128)(2,1)S(1)}, u32[]{:S(2)}, u32[]{:S(2)}) collective-permute-start(bf16[2,256,128]{2,1,0:T(8,128)(2,1)S(1)} %reshape.148), channel_id=1, source_target_pairs={{0,192},{9,201},{80,208},{89,217},{160,224},{169,233}} | collective-permute-start | bytes 393224 | tf_op jit(solution)/shard_map/ppermute | solution.py:41
  54.2 12.2 %all-to-all-start.2 = ((bf16[4,8,1536]{2,1,0:T(8,128)(2,1)}), bf16[4,8,1536]{2,1,0:T(8,128)(2,1)S(1)}, u32[]{:S(2)}, u32[]{:S(2)}) async-start(bf16[4,8,1536]{2,1,0:T(8,128)(2,1)} %spread.1), calls=%async_computation.2 | async-start | bytes 196608 | tf_op jit(solution)/shard_map/all_to_all | solution.py:413
  67.0 37.0 %collective-permute-start.9 = (bf16[768,1536]{1,0:T(8,128)(2,1)}, bf16[768,1536]{1,0:T(8,128)(2,1)}, u32[]{:S(2)}, u32[]{:S(2)}) collective-permute-start(bf16[768,1536]{1,0:T(8,128)(2,1)} %bitcast.39), channel_id=1, source_target_pairs={{1,0},{8,9},{17,16},{24,25},{33,32},{40,41},{49,48},{56,57},{65,64... | collective-permute-start | bytes 7077896 | tf_op jit(solution)/shard_map/ppermute | solution.py:41
  68.3 13.2 %all-to-all-start.3 = ((bf16[8,8,1536]{2,1,0:T(8,128)(2,1)}), bf16[8,8,1536]{2,1,0:T(8,128)(2,1)S(1)}, u32[]{:S(2)}, u32[]{:S(2)}) async-start(bf16[8,8,1536]{2,1,0:T(8,128)(2,1)} %twice.1), calls=%async_computation.3 | async-start | bytes 393216 | tf_op jit(solution)/shard_map/all_to_all | solution.py:416
  81.5 19.8 %collective-permute-start.6 = (bf16[64,1536]{1,0:T(8,128)(2,1)S(1)}, bf16[64,1536]{1,0:T(8,128)(2,1)S(1)}, u32[]{:S(2)}, u32[]{:S(2)}) collective-permute-start(bf16[64,1536]{1,0:T(8,128)(2,1)S(1)} %bitcast.41), channel_id=1, source_target_pairs={{2,0},{11,9},{18,16},{27,25},{34,32},{43,41},{50,48},{59,57},{66,6... | collective-permute-start | bytes 589832 | tf_op jit(solution)/shard_map/ppermute | solution.py:41
  82.8 18.5 %collective-permute-start.7 = (bf16[64,1536]{1,0:T(8,128)(2,1)S(1)}, bf16[64,1536]{1,0:T(8,128)(2,1)S(1)}, u32[]{:S(2)}, u32[]{:S(2)}) collective-permute-start(bf16[64,1536]{1,0:T(8,128)(2,1)S(1)} %bitcast.42), channel_id=1, source_target_pairs={{4,0},{13,9},{20,16},{29,25},{36,32},{45,41},{52,48},{61,57},{68,6... | collective-permute-start | bytes 589832 | tf_op jit(solution)/shard_map/ppermute | solution.py:41
  84.1 17.2 %collective-permute-start.8 = (bf16[64,1536]{1,0:T(8,128)(2,1)S(1)}, bf16[64,1536]{1,0:T(8,128)(2,1)S(1)}, u32[]{:S(2)}, u32[]{:S(2)}) collective-permute-start(bf16[64,1536]{1,0:T(8,128)(2,1)S(1)} %bitcast.43), channel_id=1, source_target_pairs={{6,0},{15,9},{22,16},{31,25},{38,32},{47,41},{54,48},{63,57},{70,6... | collective-permute-start | bytes 589832 | tf_op jit(solution)/shard_map/ppermute | solution.py:41
  113.4 13.2 %collective-permute-start.10 = (bf16[128,1536]{1,0:T(8,128)(2,1)S(1)}, bf16[128,1536]{1,0:T(8,128)(2,1)S(1)}, u32[]{:S(2)}, u32[]{:S(2)}) collective-permute-start(bf16[128,1536]{1,0:T(8,128)(2,1)S(1)} %get-tuple-element.68), channel_id=1, source_target_pairs={{0,64},{9,73},{16,80},{25,89},{32,96},{41,105},{48,112},{57,121}} | collective-permute-start | bytes 1179656 | tf_op jit(solution)/shard_map/ppermute | solution.py:41
  114.7 14.1 %collective-permute-start.11 = (bf16[128,1536]{1,0:T(8,128)(2,1)S(1)}, bf16[128,1536]{1,0:T(8,128)(2,1)S(1)}, u32[]{:S(2)}, u32[]{:S(2)}) collective-permute-start(bf16[128,1536]{1,0:T(8,128)(2,1)S(1)} %get-tuple-element.69.refs_10_), channel_id=1, source_target_pairs={{0,64},{9,73},{16,80},{25,89},{32,96},{41,105},{48,112},{57,121}} | collective-permute-start | bytes 1179656 | tf_op jit(solution)/shard_map/ppermute | solution.py:41
  124.0 9.7 %collective-permute-start.12 = (bf16[128,1536]{1,0:T(8,128)(2,1)S(1)}, bf16[128,1536]{1,0:T(8,128)(2,1)S(1)}, u32[]{:S(2)}, u32[]{:S(2)}) collective-permute-start(bf16[128,1536]{1,0:T(8,128)(2,1)S(1)} %get-tuple-element.70), channel_id=1, source_target_pairs={{0,64},{9,73},{16,80},{25,89},{32,96},{41,105},{48,112},{57,121}} | collective-permute-start | bytes 1179656 | tf_op jit(solution)/shard_map/ppermute | solution.py:41
  125.3 12.6 %collective-permute-start.13 = (bf16[128,1536]{1,0:T(8,128)(2,1)S(1)}, bf16[128,1536]{1,0:T(8,128)(2,1)S(1)}, u32[]{:S(2)}, u32[]{:S(2)}) collective-permute-start(bf16[128,1536]{1,0:T(8,128)(2,1)S(1)} %get-tuple-element.71), channel_id=1, source_target_pairs={{0,64},{9,73},{16,80},{25,89},{32,96},{41,105},{48,112},{57,121}} | collective-permute-start | bytes 1179656 | tf_op jit(solution)/shard_map/ppermute | solution.py:41
  147.7 13.0 %collective-permute-start.14 = (bf16[128,1536]{1,0:T(8,128)(2,1)S(1)}, bf16[128,1536]{1,0:T(8,128)(2,1)S(1)}, u32[]{:S(2)}, u32[]{:S(2)}) collective-permute-start(bf16[128,1536]{1,0:T(8,128)(2,1)S(1)} %get-tuple-element.72), channel_id=1, source_target_pairs={{64,128},{73,137},{80,144},{89,153},{96,160},{105,169},{112,176},{... | collective-permute-start | bytes 1179656 | tf_op jit(solution)/shard_map/ppermute | solution.py:41
  149.0 14.0 %collective-permute-start.15 = (bf16[128,1536]{1,0:T(8,128)(2,1)S(1)}, bf16[128,1536]{1,0:T(8,128)(2,1)S(1)}, u32[]{:S(2)}, u32[]{:S(2)}) collective-permute-start(bf16[128,1536]{1,0:T(8,128)(2,1)S(1)} %get-tuple-element.73.refs_10_), channel_id=1, source_target_pairs={{64,128},{73,137},{80,144},{89,153},{96,160},{105,169},{112,176},{... | collective-permute-start | bytes 1179656 | tf_op jit(solution)/shard_map/ppermute | solution.py:41
  159.4 9.5 %collective-permute-start.17 = (bf16[128,1536]{1,0:T(8,128)(2,1)S(1)}, bf16[128,1536]{1,0:T(8,128)(2,1)S(1)}, u32[]{:S(2)}, u32[]{:S(2)}) collective-permute-start(bf16[128,1536]{1,0:T(8,128)(2,1)S(1)} %get-tuple-element.75), channel_id=1, source_target_pairs={{64,128},{73,137},{80,144},{89,153},{96,160},{105,169},{112,176},{... | collective-permute-start | bytes 1179656 | tf_op jit(solution)/shard_map/ppermute | solution.py:41
  178.7 10.6 %collective-permute-start.18 = (bf16[128,1536]{1,0:T(8,128)(2,1)S(1)}, bf16[128,1536]{1,0:T(8,128)(2,1)S(1)}, u32[]{:S(2)}, u32[]{:S(2)}) collective-permute-start(bf16[128,1536]{1,0:T(8,128)(2,1)S(1)} %get-tuple-element.76), channel_id=1, source_target_pairs={{128,192},{137,201},{144,208},{153,217},{160,224},{169,233},{176,2... | collective-permute-start | bytes 1179656 | tf_op jit(solution)/shard_map/ppermute | solution.py:41
  179.4 12.2 %collective-permute-start.19 = (bf16[128,1536]{1,0:T(8,128)(2,1)S(1)}, bf16[128,1536]{1,0:T(8,128)(2,1)S(1)}, u32[]{:S(2)}, u32[]{:S(2)}) collective-permute-start(bf16[128,1536]{1,0:T(8,128)(2,1)S(1)} %get-tuple-element.77.refs_10_), channel_id=1, source_target_pairs={{128,192},{137,201},{144,208},{153,217},{160,224},{169,233},{176,2... | collective-permute-start | bytes 1179656 | tf_op jit(solution)/shard_map/ppermute | solution.py:41
  233.8 19.7 %collective-permute-start.23 = (bf16[128,1536]{1,0:T(8,128)(2,1)S(1)}, bf16[128,1536]{1,0:T(8,128)(2,1)S(1)}, u32[]{:S(2)}, u32[]{:S(2)}) collective-permute-start(bf16[128,1536]{1,0:T(8,128)(2,1)S(1)} %get-tuple-element.89), channel_id=1, source_target_pairs={{0,64},{9,73},{16,80},{25,89},{32,96},{41,105},{48,112},{57,121}} | collective-permute-start | bytes 1179656 | tf_op jit(solution)/shard_map/ppermute | solution.py:41
  235.1 22.6 %collective-permute-start.24 = (bf16[128,1536]{1,0:T(8,128)(2,1)S(1)}, bf16[128,1536]{1,0:T(8,128)(2,1)S(1)}, u32[]{:S(2)}, u32[]{:S(2)}) collective-permute-start(bf16[128,1536]{1,0:T(8,128)(2,1)S(1)} %get-tuple-element.90.refs_10_), channel_id=1, source_target_pairs={{0,64},{9,73},{16,80},{25,89},{32,96},{41,105},{48,112},{57,121}} | collective-permute-start | bytes 1179656 | tf_op jit(solution)/shard_map/ppermute | solution.py:41
  244.2 19.8 %collective-permute-start.25 = (bf16[128,1536]{1,0:T(8,128)(2,1)S(1)}, bf16[128,1536]{1,0:T(8,128)(2,1)S(1)}, u32[]{:S(2)}, u32[]{:S(2)}) collective-permute-start(bf16[128,1536]{1,0:T(8,128)(2,1)S(1)} %get-tuple-element.91), channel_id=1, source_target_pairs={{0,64},{9,73},{16,80},{25,89},{32,96},{41,105},{48,112},{57,121}} | collective-permute-start | bytes 1179656 | tf_op jit(solution)/shard_map/ppermute | solution.py:41
  245.5 22.7 %collective-permute-start.26 = (bf16[128,1536]{1,0:T(8,128)(2,1)S(1)}, bf16[128,1536]{1,0:T(8,128)(2,1)S(1)}, u32[]{:S(2)}, u32[]{:S(2)}) collective-permute-start(bf16[128,1536]{1,0:T(8,128)(2,1)S(1)} %get-tuple-element.92), channel_id=1, source_target_pairs={{0,64},{9,73},{16,80},{25,89},{32,96},{41,105},{48,112},{57,121}} | collective-permute-start | bytes 1179656 | tf_op jit(solution)/shard_map/ppermute | solution.py:41
  278.0 13.3 %collective-permute-start.27 = (bf16[128,1536]{1,0:T(8,128)(2,1)S(1)}, bf16[128,1536]{1,0:T(8,128)(2,1)S(1)}, u32[]{:S(2)}, u32[]{:S(2)}) collective-permute-start(bf16[128,1536]{1,0:T(8,128)(2,1)S(1)} %get-tuple-element.93), channel_id=1, source_target_pairs={{64,128},{73,137},{80,144},{89,153},{96,160},{105,169},{112,176},{... | collective-permute-start | bytes 1179656 | tf_op jit(solution)/shard_map/ppermute | solution.py:41
  279.3 14.2 %collective-permute-start.28 = (bf16[128,1536]{1,0:T(8,128)(2,1)S(1)}, bf16[128,1536]{1,0:T(8,128)(2,1)S(1)}, u32[]{:S(2)}, u32[]{:S(2)}) collective-permute-start(bf16[128,1536]{1,0:T(8,128)(2,1)S(1)} %get-tuple-element.94.refs_10_), channel_id=1, source_target_pairs={{64,128},{73,137},{80,144},{89,153},{96,160},{105,169},{112,176},{... | collective-permute-start | bytes 1179656 | tf_op jit(solution)/shard_map/ppermute | solution.py:41
  289.9 9.5 %collective-permute-start.30 = (bf16[128,1536]{1,0:T(8,128)(2,1)S(1)}, bf16[128,1536]{1,0:T(8,128)(2,1)S(1)}, u32[]{:S(2)}, u32[]{:S(2)}) collective-permute-start(bf16[128,1536]{1,0:T(8,128)(2,1)S(1)} %get-tuple-element.96), channel_id=1, source_target_pairs={{64,128},{73,137},{80,144},{89,153},{96,160},{105,169},{112,176},{... | collective-permute-start | bytes 1179656 | tf_op jit(solution)/shard_map/ppermute | solution.py:41
  309.3 10.5 %collective-permute-start.31 = (bf16[128,1536]{1,0:T(8,128)(2,1)S(1)}, bf16[128,1536]{1,0:T(8,128)(2,1)S(1)}, u32[]{:S(2)}, u32[]{:S(2)}) collective-permute-start(bf16[128,1536]{1,0:T(8,128)(2,1)S(1)} %get-tuple-element.97), channel_id=1, source_target_pairs={{128,192},{137,201},{144,208},{153,217},{160,224},{169,233},{176,2... | collective-permute-start | bytes 1179656 | tf_op jit(solution)/shard_map/ppermute | solution.py:41
  309.9 12.1 %collective-permute-start.32 = (bf16[128,1536]{1,0:T(8,128)(2,1)S(1)}, bf16[128,1536]{1,0:T(8,128)(2,1)S(1)}, u32[]{:S(2)}, u32[]{:S(2)}) collective-permute-start(bf16[128,1536]{1,0:T(8,128)(2,1)S(1)} %get-tuple-element.98.refs_10_), channel_id=1, source_target_pairs={{128,192},{137,201},{144,208},{153,217},{160,224},{169,233},{176,2... | collective-permute-start | bytes 1179656 | tf_op jit(solution)/shard_map/ppermute | solution.py:41
  348.2 23.8 %all-to-all-start.4 = ((f32[32,8,128]{2,1,0:T(8,128)}), f32[32,8,128]{2,1,0:T(8,128)S(1)}, u32[]{:S(2)}, u32[]{:S(2)}) async-start(f32[32,8,128]{2,1,0:T(8,128)} %select_bitcast_fusion), calls=%async_computation.4 | async-start | bytes 262144 | tf_op jit(solution)/shard_map/all_to_all | solution.py:473
  (18 other events, 172.8 us)

commit v3 on v2

--- a/solution.py
+++ b/solution.py
@@ -18,8 +18,8 @@
 F32 = jnp.float32
 VMEM = 20 * 1024 * 1024
 SPAN = 768
-CHUNKS = 4
-TOGETHER = 2
+CALLS = ((128, 128), (128, 128))
+CHUNKS = sum(CALLS, ())
 
 epsilon = 1e-06
 
@@ -156,12 +156,11 @@
 
 
 def embedded(latent, weight):
-    rows = latent.shape[0] // CHUNKS
     return pl.pallas_call(
         embed_kernel,
         in_specs=[whole()] * 2,
-        out_specs=[whole()] * CHUNKS,
-        out_shape=[jax.ShapeDtypeStruct((rows, weight.shape[1]), BF)] * CHUNKS,
+        out_specs=[whole()] * len(CHUNKS),
+        out_shape=[jax.ShapeDtypeStruct((rows, weight.shape[1]), BF) for rows in CHUNKS],
         compiler_params=params(),
         name="embed",
     )(latent, weight)
@@ -364,7 +363,6 @@
     text = lax.dynamic_index_in_dim(text_rows[:, 0], x, 0, keepdims=False)
     partial = jnp.dot(text, context_weight, preferred_element_type=F32).astype(BF)
     attn_mine, proj_mine = w_attention[0], w_project[0]
-    third = attn_mine.shape[0] // 3
 
     def beside(operand, piece):
         operand, piece = lax.optimization_barrier((operand, piece))
@@ -379,16 +377,13 @@
     message = jnp.concatenate(
         [partial.reshape(Y, quarter, width), jnp.broadcast_to(both[None], (Y, 2, width))], 1
     )
-    message, piece = beside(message, attn_mine[:third])
-    attn_pieces = [piece]
+    message, attn_piece = beside(message, attn_mine)
     parts = lax.all_to_all(message, "y", split_axis=0, concat_axis=0, tiled=True)
     summed = jnp.sum(parts[:, :quarter].astype(F32), axis=0).astype(BF)
     both = parts[:, quarter:].reshape(1, 2 * Y, width)
     message = jnp.concatenate(
         [summed.reshape(Z, eighth, width), jnp.broadcast_to(both, (Z, 2 * Y, width))], 1
     )
-    message, piece = beside(message, attn_mine[third : 2 * third])
-    attn_pieces.append(piece)
     parts = lax.all_to_all(message, "z", split_axis=0, concat_axis=0, tiled=True)
     both = parts[:, eighth:].reshape(patches // rows_here, 2, width)[:, :, : latent.shape[1]]
     both = jnp.transpose(both, (1, 0, 2)).reshape(2, patches * latent_width // 128, 128)
@@ -408,14 +403,13 @@
         for part in range(3)
     )
 
-    message, piece = beside(spread_over(parts, X, eighth), attn_mine[2 * third :])
-    attn_pieces.append(piece)
+    message = spread_over(parts, X, eighth)
     shared = lax.all_to_all(message, "x", split_axis=0, concat_axis=0, tiled=True)
     early = (first, latent, bias, w_final, w_embed, *shifts, *scales, *gates)
     message, piece = beside(twice(shared, Z, early), proj_mine)
     shared = lax.all_to_all(message, "z", split_axis=0, concat_axis=0, tiled=True)
     ready = (first, latent, bias, w_final, w_embed, *shifts, *scales, *gates)
-    attn_weight = joined(core, attn_mine, attn_pieces, ready)
+    attn_weight = joined(core, attn_mine, [attn_piece], ready)
     hidden = embedded(first, w_embed)
 
     def products(hidden, step):
@@ -444,8 +438,8 @@
         if turn > 0:
             projected = products(hidden, step)
         following = []
-        for i in range(0, CHUNKS, TOGETHER):
-            queries = tuple(range(i, i + TOGETHER))
+        for call in CALLS:
+            queries = tuple(range(len(following), len(following) + len(call)))
             following = following + list(
                 attention(
                     projected,

time: 379 us -> 379 us (level)
  waiting for transfers between devices: 64.7 us -> 69.8 us
  local copies, waits for them, and re-layouts: 12.3 us -> 7.7 us
    slice x1 -> x0, local copies, waits for them, and re-layouts: 6.12 us -> none  [on_device(): attn_mine[2 * third:]]
    ppermute x36 -> x34, starting transfers between devices: 41.4 us -> 38.9 us  [move(): return lax.ppermute(value, AXES, [(flat(*a), flat(*b)) for a, b in pairs])]
    ppermute x36 -> x34, waiting for transfers between devices: 21.8 us -> 22.1 us  [move(): return lax.ppermute(value, AXES, [(flat(*a), flat(*b)) for a, b in pairs])]
  transfers between devices with their start and end apart: 41 -> 39, of which waited for: 13 -> 14; matrix products, arithmetic and copies ran while one was open for 1% -> 1% of each run, Pallas kernels for 28% -> 27%
where the time goes in v3:
time: 379 us; the launch traced here: 373 us
  Pallas kernels  208 us (55%)
  starting transfers between devices  78.7 us (21%)
  waiting for transfers between devices  69.8 us (18%)
  local copies, waits for them, and re-layouts  7.7 us (2%)
  other arithmetic  5.35 us (1%)
    pallas_call x16, Pallas kernels, attention(): pl.pallas_call(functools.partial(attention_kernel, queries=queries, block...  121 us
    pallas_call x33, Pallas kernels, product(): pl.pallas_call(functools.partial(product_kernel, pieces=len(rows), column...  74.8 us
    ppermute x34, starting transfers between devices, move(): return lax.ppermute(value, AXES, [(flat(*a), flat(*b)) for a, b in pairs])  38.9 us
    ppermute x34, waiting for transfers between devices, move(): return lax.ppermute(value, AXES, [(flat(*a), flat(*b)) for a, b in pairs])  22.1 us
    all_to_all x2, waiting for transfers between devices, on_device(): lax.all_to_all(message, 'z', split_axis=0, concat_axis=0, tiled=True)  19.2 us
    all_to_all x1, waiting for transfers between devices, on_device(): lax.all_to_all(message, 'y', split_axis=0, concat_axis=0, tiled=True)  14 us
    all_to_all x1, starting transfers between devices, on_device(): lax.all_to_all(latent.reshape(Z * Y, rows_here * latent_width // 128, 128...  13.4 us
    all_to_all x2, starting transfers between devices, on_device(): lax.all_to_all(message, 'z', split_axis=0, concat_axis=0, tiled=True)  12 us
  transfers between devices with their start and end apart: 39, of which 14 were waited for; matrix products, arithmetic and copies ran while one was open for 1% of the time, Pallas kernels for 27%

profile of v3, /device:TPU:2, one launch (start us, length us, event | category | flops | bytes accessed | tf_op | source)
XLA Modules:
  0.0 372.9 jit_solution(3505766197781807922)
XLA Ops:
  4.8 6.7 %all-to-all-start = ((bf16[4,66,1536]{2,1,0:T(8,128)(2,1)}), bf16[4,66,1536]{2,1,0:T(8,128)(2,1)S(1)}, u32[]{:S(2)}, u32[]{:S(2)}) async-start(bf16[4,66,1536]{2,1,0:T(8,128)(2,1)} %pad_maximum_fusion), calls=%async_computation | async-start | bytes 1769472 | tf_op jit(solution)/shard_map/all_to_all | solution.py:381
  12.0 14.0 %all-to-all-done = bf16[4,66,1536]{2,1,0:T(8,128)(2,1)S(1)} async-done(((bf16[4,66,1536]{2,1,0:T(8,128)(2,1)}), bf16[4,66,1536]{2,1,0:T(8,128)(2,1)S(1)}, u32[]{:S(2)}, u32[]{:S(2)}) %all-to-all-start) | async-done | bytes 811040 | tf_op jit(solution)/shard_map/all_to_all | solution.py:381
  27.0 8.6 %all-to-all-start.1 = ((bf16[8,16,1536]{2,1,0:T(8,128)(2,1)}), bf16[8,16,1536]{2,1,0:T(8,128)(2,1)S(1)}, u32[]{:S(2)}, u32[]{:S(2)}) async-start(bf16[8,16,1536]{2,1,0:T(8,128)(2,1)} %pad_maximum_fusion.1), calls=%async_computation.1 | async-start | bytes 786432 | tf_op jit(solution)/shard_map/all_to_all | solution.py:387
  40.3 10.0 %all-to-all-done.1.parts_ref = bf16[8,16,1536]{2,1,0:T(8,128)(2,1)S(1)} async-done(((bf16[8,16,1536]{2,1,0:T(8,128)(2,1)}), bf16[8,16,1536]{2,1,0:T(8,128)(2,1)S(1)}, u32[]{:S(2)}, u32[]{:S(2)}) %all-to-all-start.1) | async-done | bytes 393248 | tf_op jit(solution)/shard_map/all_to_all | solution.py:387
  52.9 7.8 %all-to-all-start.2 = ((bf16[4,8,1536]{2,1,0:T(8,128)(2,1)}), bf16[4,8,1536]{2,1,0:T(8,128)(2,1)S(1)}, u32[]{:S(2)}, u32[]{:S(2)}) async-start(bf16[4,8,1536]{2,1,0:T(8,128)(2,1)} %spread.1), calls=%async_computation.2 | async-start | bytes 196608 | tf_op jit(solution)/shard_map/all_to_all | solution.py:407
  61.0 4.1 %all-to-all-done.2.rows_ref = bf16[4,8,1536]{2,1,0:T(8,128)(2,1)S(1)} async-done(((bf16[4,8,1536]{2,1,0:T(8,128)(2,1)}), bf16[4,8,1536]{2,1,0:T(8,128)(2,1)S(1)}, u32[]{:S(2)}, u32[]{:S(2)}) %all-to-all-start.2) | async-done | bytes 98336 | tf_op jit(solution)/shard_map/all_to_all | solution.py:407
  67.1 3.4 all-to-all-start.3
  71.0 9.2 %all-to-all-done.3 = bf16[8,8,1536]{2,1,0:T(8,128)(2,1)S(1)} async-done(((bf16[8,8,1536]{2,1,0:T(8,128)(2,1)}), bf16[8,8,1536]{2,1,0:T(8,128)(2,1)S(1)}, u32[]{:S(2)}, u32[]{:S(2)}) %all-to-all-start.3) | async-done | bytes 196640 | tf_op jit(solution)/shard_map/all_to_all | solution.py:410
  87.9 3.0 copy-done.2
  90.9 3.5 joined.2.refs_1_.refs_4_
  103.5 2.6 product.37.refs_4_
  106.1 7.5 %attention.16 = (bf16[128,1536]{1,0:T(8,128)(2,1)S(1)}, bf16[128,1536]{1,0:T(8,128)(2,1)S(1)}) custom-call(bf16[128,4608]{1,0:T(8,128)(2,1)S(1)} %product.33.refs_4_.refs_0_, bf16[128,4608]{1,0:T(8,128)(2,1)S(1)} %product.34.refs_4_.refs_1_, bf16[128,4608]{1,0:T(8,128)(2,1)S(1)} %product.35.refs_4_.refs_2_, bf16[128,4608]{1,0:T(8,128)(2,1)S(1)} %product.36.refs_3_, ...), custom_call_target="tpu_custom_call" | custom-call | flops 2415919104 | bytes 8388608 | tf_op jit(solution)/shard_map/attention/pallas_call | solution.py:310
  116.6 7.5 %attention.17 = (bf16[128,1536]{1,0:T(8,128)(2,1)S(1)}, bf16[128,1536]{1,0:T(8,128)(2,1)S(1)}) custom-call(bf16[128,4608]{1,0:T(8,128)(2,1)S(1)} %product.33.refs_4_.refs_0_, bf16[128,4608]{1,0:T(8,128)(2,1)S(1)} %product.34.refs_4_.refs_1_, bf16[128,4608]{1,0:T(8,128)(2,1)S(1)} %product.35.refs_4_.refs_2_, bf16[128,4608]{1,0:T(8,128)(2,1)S(1)} %product.36.refs_3_, ...), custom_call_target="tpu_custom_call" | custom-call | flops 2415919104 | bytes 8388608 | tf_op jit(solution)/shard_map/attention/pallas_call | solution.py:310
  131.3 2.6 collective-permute-done.10.refs_0_.refs_8_
  140.4 7.5 %attention.18 = (bf16[128,1536]{1,0:T(8,128)(2,1)S(1)}, bf16[128,1536]{1,0:T(8,128)(2,1)S(1)}) custom-call(bf16[128,4608]{1,0:T(8,128)(2,1)S(1)} %product.38.refs_4_.refs_0_, bf16[128,4608]{1,0:T(8,128)(2,1)S(1)} %product.39.refs_4_.refs_1_, bf16[128,4608]{1,0:T(8,128)(2,1)S(1)} %product.40.refs_4_.refs_2_, bf16[128,4608]{1,0:T(8,128)(2,1)S(1)} %product.41.refs_3_, ...), custom_call_target="tpu_custom_call" | custom-call | flops 2415919104 | bytes 8388608 | tf_op jit(solution)/shard_map/attention/pallas_call | solution.py:310
  150.7 7.5 %attention.19 = (bf16[128,1536]{1,0:T(8,128)(2,1)S(1)}, bf16[128,1536]{1,0:T(8,128)(2,1)S(1)}) custom-call(bf16[128,4608]{1,0:T(8,128)(2,1)S(1)} %product.38.refs_4_.refs_0_, bf16[128,4608]{1,0:T(8,128)(2,1)S(1)} %product.39.refs_4_.refs_1_, bf16[128,4608]{1,0:T(8,128)(2,1)S(1)} %product.40.refs_4_.refs_2_, bf16[128,4608]{1,0:T(8,128)(2,1)S(1)} %product.41.refs_3_, ...), custom_call_target="tpu_custom_call" | custom-call | flops 2415919104 | bytes 8388608 | tf_op jit(solution)/shard_map/attention/pallas_call | solution.py:310
  171.3 7.5 %attention.20 = (bf16[128,1536]{1,0:T(8,128)(2,1)S(1)}, bf16[128,1536]{1,0:T(8,128)(2,1)S(1)}) custom-call(bf16[128,4608]{1,0:T(8,128)(2,1)S(1)} %product.42.refs_4_.refs_0_, bf16[128,4608]{1,0:T(8,128)(2,1)S(1)} %product.43.refs_4_.refs_1_, bf16[128,4608]{1,0:T(8,128)(2,1)S(1)} %product.44.refs_4_.refs_2_, bf16[128,4608]{1,0:T(8,128)(2,1)S(1)} %product.45.refs_3_, ...), custom_call_target="tpu_custom_call" | custom-call | flops 2415919104 | bytes 8388608 | tf_op jit(solution)/shard_map/attention/pallas_call | solution.py:310
  180.5 7.5 %attention.21 = (bf16[128,1536]{1,0:T(8,128)(2,1)S(1)}, bf16[128,1536]{1,0:T(8,128)(2,1)S(1)}) custom-call(bf16[128,4608]{1,0:T(8,128)(2,1)S(1)} %product.42.refs_4_.refs_0_, bf16[128,4608]{1,0:T(8,128)(2,1)S(1)} %product.43.refs_4_.refs_1_, bf16[128,4608]{1,0:T(8,128)(2,1)S(1)} %product.44.refs_4_.refs_2_, bf16[128,4608]{1,0:T(8,128)(2,1)S(1)} %product.45.refs_3_, ...), custom_call_target="tpu_custom_call" | custom-call | flops 2415919104 | bytes 8388608 | tf_op jit(solution)/shard_map/attention/pallas_call | solution.py:310
  198.6 7.9 %attention.22 = (bf16[128,1536]{1,0:T(8,128)(2,1)S(1)}, bf16[128,1536]{1,0:T(8,128)(2,1)S(1)}) custom-call(bf16[128,4608]{1,0:T(8,128)(2,1)S(1)} %product.46.refs_4_.refs_0_, bf16[128,4608]{1,0:T(8,128)(2,1)S(1)} %product.47.refs_4_.refs_1_, bf16[128,4608]{1,0:T(8,128)(2,1)S(1)} %product.48.refs_4_.refs_2_, bf16[128,4608]{1,0:T(8,128)(2,1)S(1)} %product.49.refs_3_, ...), custom_call_target="tpu_custom_call" | custom-call | flops 2415919104 | bytes 8388608 | tf_op jit(solution)/shard_map/attention/pallas_call | solution.py:310
  206.5 7.5 %attention.23 = (bf16[128,1536]{1,0:T(8,128)(2,1)S(1)}, bf16[128,1536]{1,0:T(8,128)(2,1)S(1)}) custom-call(bf16[128,4608]{1,0:T(8,128)(2,1)S(1)} %product.46.refs_4_.refs_0_, bf16[128,4608]{1,0:T(8,128)(2,1)S(1)} %product.47.refs_4_.refs_1_, bf16[128,4608]{1,0:T(8,128)(2,1)S(1)} %product.48.refs_4_.refs_2_, bf16[128,4608]{1,0:T(8,128)(2,1)S(1)} %product.49.refs_3_, ...), custom_call_target="tpu_custom_call" | custom-call | flops 2415919104 | bytes 8388608 | tf_op jit(solution)/shard_map/attention/pallas_call | solution.py:310
  226.3 7.5 %attention.24 = (bf16[128,1536]{1,0:T(8,128)(2,1)S(1)}, bf16[128,1536]{1,0:T(8,128)(2,1)S(1)}) custom-call(bf16[128,4608]{1,0:T(8,128)(2,1)S(1)} %product.50.refs_4_.refs_0_, bf16[128,4608]{1,0:T(8,128)(2,1)S(1)} %product.51.refs_4_.refs_1_, bf16[128,4608]{1,0:T(8,128)(2,1)S(1)} %product.52.refs_4_.refs_2_, bf16[128,4608]{1,0:T(8,128)(2,1)S(1)} %product.53.refs_3_, ...), custom_call_target="tpu_custom_call" | custom-call | flops 2415919104 | bytes 8388608 | tf_op jit(solution)/shard_map/attention/pallas_call | solution.py:310
  236.7 7.5 %attention.25 = (bf16[128,1536]{1,0:T(8,128)(2,1)S(1)}, bf16[128,1536]{1,0:T(8,128)(2,1)S(1)}) custom-call(bf16[128,4608]{1,0:T(8,128)(2,1)S(1)} %product.50.refs_4_.refs_0_, bf16[128,4608]{1,0:T(8,128)(2,1)S(1)} %product.51.refs_4_.refs_1_, bf16[128,4608]{1,0:T(8,128)(2,1)S(1)} %product.52.refs_4_.refs_2_, bf16[128,4608]{1,0:T(8,128)(2,1)S(1)} %product.53.refs_3_, ...), custom_call_target="tpu_custom_call" | custom-call | flops 2415919104 | bytes 8388608 | tf_op jit(solution)/shard_map/attention/pallas_call | solution.py:310
  246.8 6.8 %collective-permute-done.21.refs_0_.refs_8_ = bf16[128,1536]{1,0:T(8,128)(2,1)S(1)} collective-permute-done((bf16[128,1536]{1,0:T(8,128)(2,1)S(1)}, bf16[128,1536]{1,0:T(8,128)(2,1)S(1)}, u32[]{:S(2)}, u32[]{:S(2)}) %collective-permute-start.21) | collective-permute-done | bytes 393248 | tf_op jit(solution)/shard_map/ppermute | solution.py:41
  260.1 3.9 %collective-permute-done.23.refs_0_.refs_8_ = bf16[128,1536]{1,0:T(8,128)(2,1)S(1)} collective-permute-done((bf16[128,1536]{1,0:T(8,128)(2,1)S(1)}, bf16[128,1536]{1,0:T(8,128)(2,1)S(1)}, u32[]{:S(2)}, u32[]{:S(2)}) %collective-permute-start.23) | collective-permute-done | bytes 393248 | tf_op jit(solution)/shard_map/ppermute | solution.py:41
  270.5 7.5 %attention.26 = (bf16[128,1536]{1,0:T(8,128)(2,1)S(1)}, bf16[128,1536]{1,0:T(8,128)(2,1)S(1)}) custom-call(bf16[128,4608]{1,0:T(8,128)(2,1)S(1)} %product.54.refs_4_.refs_0_, bf16[128,4608]{1,0:T(8,128)(2,1)S(1)} %product.55.refs_4_.refs_1_, bf16[128,4608]{1,0:T(8,128)(2,1)S(1)} %product.56.refs_4_.refs_2_, bf16[128,4608]{1,0:T(8,128)(2,1)S(1)} %product.57.refs_3_, ...), custom_call_target="tpu_custom_call" | custom-call | flops 2415919104 | bytes 8388608 | tf_op jit(solution)/shard_map/attention/pallas_call | solution.py:310
  281.1 7.5 %attention.27 = (bf16[128,1536]{1,0:T(8,128)(2,1)S(1)}, bf16[128,1536]{1,0:T(8,128)(2,1)S(1)}) custom-call(bf16[128,4608]{1,0:T(8,128)(2,1)S(1)} %product.54.refs_4_.refs_0_, bf16[128,4608]{1,0:T(8,128)(2,1)S(1)} %product.55.refs_4_.refs_1_, bf16[128,4608]{1,0:T(8,128)(2,1)S(1)} %product.56.refs_4_.refs_2_, bf16[128,4608]{1,0:T(8,128)(2,1)S(1)} %product.57.refs_3_, ...), custom_call_target="tpu_custom_call" | custom-call | flops 2415919104 | bytes 8388608 | tf_op jit(solution)/shard_map/attention/pallas_call | solution.py:310
  301.7 7.5 %attention.28 = (bf16[128,1536]{1,0:T(8,128)(2,1)S(1)}, bf16[128,1536]{1,0:T(8,128)(2,1)S(1)}) custom-call(bf16[128,4608]{1,0:T(8,128)(2,1)S(1)} %product.58.refs_4_.refs_0_, bf16[128,4608]{1,0:T(8,128)(2,1)S(1)} %product.59.refs_4_.refs_1_, bf16[128,4608]{1,0:T(8,128)(2,1)S(1)} %product.60.refs_4_.refs_2_, bf16[128,4608]{1,0:T(8,128)(2,1)S(1)} %product.61.refs_3_, ...), custom_call_target="tpu_custom_call" | custom-call | flops 2415919104 | bytes 8388608 | tf_op jit(solution)/shard_map/attention/pallas_call | solution.py:310
  310.8 7.5 %attention.29 = (bf16[128,1536]{1,0:T(8,128)(2,1)S(1)}, bf16[128,1536]{1,0:T(8,128)(2,1)S(1)}) custom-call(bf16[128,4608]{1,0:T(8,128)(2,1)S(1)} %product.58.refs_4_.refs_0_, bf16[128,4608]{1,0:T(8,128)(2,1)S(1)} %product.59.refs_4_.refs_1_, bf16[128,4608]{1,0:T(8,128)(2,1)S(1)} %product.60.refs_4_.refs_2_, bf16[128,4608]{1,0:T(8,128)(2,1)S(1)} %product.61.refs_3_, ...), custom_call_target="tpu_custom_call" | custom-call | flops 2415919104 | bytes 8388608 | tf_op jit(solution)/shard_map/attention/pallas_call | solution.py:310
  328.8 7.7 %attention.30 = (bf16[128,1536]{1,0:T(8,128)(2,1)S(1)}, bf16[128,1536]{1,0:T(8,128)(2,1)S(1)}) custom-call(bf16[128,4608]{1,0:T(8,128)(2,1)S(1)} %product.62.refs_4_.refs_0_, bf16[128,4608]{1,0:T(8,128)(2,1)S(1)} %product.63.refs_4_.refs_1_, bf16[128,4608]{1,0:T(8,128)(2,1)S(1)} %product.64.refs_4_.refs_2_, bf16[128,4608]{1,0:T(8,128)(2,1)S(1)} %product.65.refs_3_, ...), custom_call_target="tpu_custom_call" | custom-call | flops 2415919104 | bytes 8388608 | tf_op jit(solution)/shard_map/attention/pallas_call | solution.py:310
  336.6 7.5 %attention.31 = (bf16[128,1536]{1,0:T(8,128)(2,1)S(1)}, bf16[128,1536]{1,0:T(8,128)(2,1)S(1)}) custom-call(bf16[128,4608]{1,0:T(8,128)(2,1)S(1)} %product.62.refs_4_.refs_0_, bf16[128,4608]{1,0:T(8,128)(2,1)S(1)} %product.63.refs_4_.refs_1_, bf16[128,4608]{1,0:T(8,128)(2,1)S(1)} %product.64.refs_4_.refs_2_, bf16[128,4608]{1,0:T(8,128)(2,1)S(1)} %product.65.refs_3_, ...), custom_call_target="tpu_custom_call" | custom-call | flops 2415919104 | bytes 8388608 | tf_op jit(solution)/shard_map/attention/pallas_call | solution.py:310
  348.1 13.4 %all-to-all-start.4 = ((f32[32,8,128]{2,1,0:T(8,128)}), f32[32,8,128]{2,1,0:T(8,128)S(1)}, u32[]{:S(2)}, u32[]{:S(2)}) async-start(f32[32,8,128]{2,1,0:T(8,128)} %select_bitcast_fusion), calls=%async_computation.4 | async-start | bytes 262144 | tf_op jit(solution)/shard_map/all_to_all | solution.py:467
  361.5 10.5 %all-to-all-done.4 = f32[32,8,128]{2,1,0:T(8,128)S(1)} async-done(((f32[32,8,128]{2,1,0:T(8,128)}), f32[32,8,128]{2,1,0:T(8,128)S(1)}, u32[]{:S(2)}, u32[]{:S(2)}) %all-to-all-start.4) | async-done | bytes 131104 | tf_op jit(solution)/shard_map/all_to_all | solution.py:467
  (157 shorter events, 140.3 us)
Async XLA Ops:
  3.4 84.5 %collective-permute-start.1 = (bf16[768,4608]{1,0:T(8,128)(2,1)}, bf16[768,4608]{1,0:T(8,128)(2,1)}, u32[]{:S(2)}, u32[]{:S(2)}) collective-permute-start(bf16[768,4608]{1,0:T(8,128)(2,1)} %bitcast.32), channel_id=1, source_target_pairs={{1,0},{8,9},{17,16},{24,25},{33,32},{40,41},{49,48},{56,57},{65,64... | collective-permute-start | bytes 21233672 | tf_op jit(solution)/shard_map/ppermute | solution.py:41
  4.8 21.2 %all-to-all-start = ((bf16[4,66,1536]{2,1,0:T(8,128)(2,1)}), bf16[4,66,1536]{2,1,0:T(8,128)(2,1)S(1)}, u32[]{:S(2)}, u32[]{:S(2)}) async-start(bf16[4,66,1536]{2,1,0:T(8,128)(2,1)} %pad_maximum_fusion), calls=%async_computation | async-start | bytes 1769472 | tf_op jit(solution)/shard_map/all_to_all | solution.py:381
  27.0 23.4 %all-to-all-start.1 = ((bf16[8,16,1536]{2,1,0:T(8,128)(2,1)}), bf16[8,16,1536]{2,1,0:T(8,128)(2,1)S(1)}, u32[]{:S(2)}, u32[]{:S(2)}) async-start(bf16[8,16,1536]{2,1,0:T(8,128)(2,1)} %pad_maximum_fusion.1), calls=%async_computation.1 | async-start | bytes 786432 | tf_op jit(solution)/shard_map/all_to_all | solution.py:387
  50.6 10.1 %collective-permute-start = (bf16[256,128]{1,0:T(8,128)(2,1)S(1)}, bf16[256,128]{1,0:T(8,128)(2,1)S(1)}, u32[]{:S(2)}, u32[]{:S(2)}) collective-permute-start(bf16[256,128]{1,0:T(8,128)(2,1)S(1)} %squeeze.32), channel_id=1, source_target_pairs={{80,16},{89,25},{160,32},{169,41},{240,48},{249,57}} | collective-permute-start | bytes 196616 | tf_op jit(solution)/shard_map/ppermute | solution.py:41
  51.4 9.4 %collective-permute-start.2 = (bf16[2,256,128]{2,1,0:T(8,128)(2,1)S(1)}, bf16[2,256,128]{2,1,0:T(8,128)(2,1)S(1)}, u32[]{:S(2)}, u32[]{:S(2)}) collective-permute-start(bf16[2,256,128]{2,1,0:T(8,128)(2,1)S(1)} %reshape.145), channel_id=1, source_target_pairs={{0,192},{9,201},{80,208},{89,217},{160,224},{169,233}} | collective-permute-start | bytes 393224 | tf_op jit(solution)/shard_map/ppermute | solution.py:41
  52.9 12.2 %all-to-all-start.2 = ((bf16[4,8,1536]{2,1,0:T(8,128)(2,1)}), bf16[4,8,1536]{2,1,0:T(8,128)(2,1)S(1)}, u32[]{:S(2)}, u32[]{:S(2)}) async-start(bf16[4,8,1536]{2,1,0:T(8,128)(2,1)} %spread.1), calls=%async_computation.2 | async-start | bytes 196608 | tf_op jit(solution)/shard_map/all_to_all | solution.py:407
  65.8 18.5 %collective-permute-start.7 = (bf16[768,1536]{1,0:T(8,128)(2,1)}, bf16[768,1536]{1,0:T(8,128)(2,1)}, u32[]{:S(2)}, u32[]{:S(2)}) collective-permute-start(bf16[768,1536]{1,0:T(8,128)(2,1)} %bitcast.34), channel_id=1, source_target_pairs={{1,0},{8,9},{17,16},{24,25},{33,32},{40,41},{49,48},{56,57},{65,64... | collective-permute-start | bytes 7077896 | tf_op jit(solution)/shard_map/ppermute | solution.py:41
  67.1 13.2 %all-to-all-start.3 = ((bf16[8,8,1536]{2,1,0:T(8,128)(2,1)}), bf16[8,8,1536]{2,1,0:T(8,128)(2,1)S(1)}, u32[]{:S(2)}, u32[]{:S(2)}) async-start(bf16[8,8,1536]{2,1,0:T(8,128)(2,1)} %twice.1), calls=%async_computation.3 | async-start | bytes 393216 | tf_op jit(solution)/shard_map/all_to_all | solution.py:410
  80.3 23.2 %collective-permute-start.4 = (bf16[64,1536]{1,0:T(8,128)(2,1)S(1)}, bf16[64,1536]{1,0:T(8,128)(2,1)S(1)}, u32[]{:S(2)}, u32[]{:S(2)}) collective-permute-start(bf16[64,1536]{1,0:T(8,128)(2,1)S(1)} %bitcast.36), channel_id=1, source_target_pairs={{2,0},{11,9},{18,16},{27,25},{34,32},{43,41},{50,48},{59,57},{66,6... | collective-permute-start | bytes 589832 | tf_op jit(solution)/shard_map/ppermute | solution.py:41
  81.6 21.9 %collective-permute-start.5 = (bf16[64,1536]{1,0:T(8,128)(2,1)S(1)}, bf16[64,1536]{1,0:T(8,128)(2,1)S(1)}, u32[]{:S(2)}, u32[]{:S(2)}) collective-permute-start(bf16[64,1536]{1,0:T(8,128)(2,1)S(1)} %bitcast.37), channel_id=1, source_target_pairs={{4,0},{13,9},{20,16},{29,25},{36,32},{45,41},{52,48},{61,57},{68,6... | collective-permute-start | bytes 589832 | tf_op jit(solution)/shard_map/ppermute | solution.py:41
  82.9 20.6 %collective-permute-start.6 = (bf16[64,1536]{1,0:T(8,128)(2,1)S(1)}, bf16[64,1536]{1,0:T(8,128)(2,1)S(1)}, u32[]{:S(2)}, u32[]{:S(2)}) collective-permute-start(bf16[64,1536]{1,0:T(8,128)(2,1)S(1)} %bitcast.38), channel_id=1, source_target_pairs={{6,0},{15,9},{22,16},{31,25},{38,32},{47,41},{54,48},{63,57},{70,6... | collective-permute-start | bytes 589832 | tf_op jit(solution)/shard_map/ppermute | solution.py:41
  113.6 13.2 %collective-permute-start.8 = (bf16[128,1536]{1,0:T(8,128)(2,1)S(1)}, bf16[128,1536]{1,0:T(8,128)(2,1)S(1)}, u32[]{:S(2)}, u32[]{:S(2)}) collective-permute-start(bf16[128,1536]{1,0:T(8,128)(2,1)S(1)} %get-tuple-element.60), channel_id=1, source_target_pairs={{0,64},{9,73},{16,80},{25,89},{32,96},{41,105},{48,112},{57,121}} | collective-permute-start | bytes 1179656 | tf_op jit(solution)/shard_map/ppermute | solution.py:41
  114.9 14.1 %collective-permute-start.9 = (bf16[128,1536]{1,0:T(8,128)(2,1)S(1)}, bf16[128,1536]{1,0:T(8,128)(2,1)S(1)}, u32[]{:S(2)}, u32[]{:S(2)}) collective-permute-start(bf16[128,1536]{1,0:T(8,128)(2,1)S(1)} %get-tuple-element.61.refs_10_), channel_id=1, source_target_pairs={{0,64},{9,73},{16,80},{25,89},{32,96},{41,105},{48,112},{57,121}} | collective-permute-start | bytes 1179656 | tf_op jit(solution)/shard_map/ppermute | solution.py:41
  124.2 9.7 %collective-permute-start.10 = (bf16[128,1536]{1,0:T(8,128)(2,1)S(1)}, bf16[128,1536]{1,0:T(8,128)(2,1)S(1)}, u32[]{:S(2)}, u32[]{:S(2)}) collective-permute-start(bf16[128,1536]{1,0:T(8,128)(2,1)S(1)} %get-tuple-element.62), channel_id=1, source_target_pairs={{0,64},{9,73},{16,80},{25,89},{32,96},{41,105},{48,112},{57,121}} | collective-permute-start | bytes 1179656 | tf_op jit(solution)/shard_map/ppermute | solution.py:41
  125.5 12.6 %collective-permute-start.11 = (bf16[128,1536]{1,0:T(8,128)(2,1)S(1)}, bf16[128,1536]{1,0:T(8,128)(2,1)S(1)}, u32[]{:S(2)}, u32[]{:S(2)}) collective-permute-start(bf16[128,1536]{1,0:T(8,128)(2,1)S(1)} %get-tuple-element.63), channel_id=1, source_target_pairs={{0,64},{9,73},{16,80},{25,89},{32,96},{41,105},{48,112},{57,121}} | collective-permute-start | bytes 1179656 | tf_op jit(solution)/shard_map/ppermute | solution.py:41
  147.9 13.0 %collective-permute-start.12 = (bf16[128,1536]{1,0:T(8,128)(2,1)S(1)}, bf16[128,1536]{1,0:T(8,128)(2,1)S(1)}, u32[]{:S(2)}, u32[]{:S(2)}) collective-permute-start(bf16[128,1536]{1,0:T(8,128)(2,1)S(1)} %get-tuple-element.64), channel_id=1, source_target_pairs={{64,128},{73,137},{80,144},{89,153},{96,160},{105,169},{112,176},{... | collective-permute-start | bytes 1179656 | tf_op jit(solution)/shard_map/ppermute | solution.py:41
  149.2 14.0 %collective-permute-start.13 = (bf16[128,1536]{1,0:T(8,128)(2,1)S(1)}, bf16[128,1536]{1,0:T(8,128)(2,1)S(1)}, u32[]{:S(2)}, u32[]{:S(2)}) collective-permute-start(bf16[128,1536]{1,0:T(8,128)(2,1)S(1)} %get-tuple-element.65.refs_10_), channel_id=1, source_target_pairs={{64,128},{73,137},{80,144},{89,153},{96,160},{105,169},{112,176},{... | collective-permute-start | bytes 1179656 | tf_op jit(solution)/shard_map/ppermute | solution.py:41
  159.6 9.5 %collective-permute-start.15 = (bf16[128,1536]{1,0:T(8,128)(2,1)S(1)}, bf16[128,1536]{1,0:T(8,128)(2,1)S(1)}, u32[]{:S(2)}, u32[]{:S(2)}) collective-permute-start(bf16[128,1536]{1,0:T(8,128)(2,1)S(1)} %get-tuple-element.67), channel_id=1, source_target_pairs={{64,128},{73,137},{80,144},{89,153},{96,160},{105,169},{112,176},{... | collective-permute-start | bytes 1179656 | tf_op jit(solution)/shard_map/ppermute | solution.py:41
  178.9 10.6 %collective-permute-start.16 = (bf16[128,1536]{1,0:T(8,128)(2,1)S(1)}, bf16[128,1536]{1,0:T(8,128)(2,1)S(1)}, u32[]{:S(2)}, u32[]{:S(2)}) collective-permute-start(bf16[128,1536]{1,0:T(8,128)(2,1)S(1)} %get-tuple-element.68), channel_id=1, source_target_pairs={{128,192},{137,201},{144,208},{153,217},{160,224},{169,233},{176,2... | collective-permute-start | bytes 1179656 | tf_op jit(solution)/shard_map/ppermute | solution.py:41
  179.6 12.2 %collective-permute-start.17 = (bf16[128,1536]{1,0:T(8,128)(2,1)S(1)}, bf16[128,1536]{1,0:T(8,128)(2,1)S(1)}, u32[]{:S(2)}, u32[]{:S(2)}) collective-permute-start(bf16[128,1536]{1,0:T(8,128)(2,1)S(1)} %get-tuple-element.69.refs_10_), channel_id=1, source_target_pairs={{128,192},{137,201},{144,208},{153,217},{160,224},{169,233},{176,2... | collective-permute-start | bytes 1179656 | tf_op jit(solution)/shard_map/ppermute | solution.py:41
  188.8 7.5 %collective-permute-start.19 = (bf16[128,1536]{1,0:T(8,128)(2,1)S(1)}, bf16[128,1536]{1,0:T(8,128)(2,1)S(1)}, u32[]{:S(2)}, u32[]{:S(2)}) collective-permute-start(bf16[128,1536]{1,0:T(8,128)(2,1)S(1)} %get-tuple-element.71), channel_id=1, source_target_pairs={{128,192},{137,201},{144,208},{153,217},{160,224},{169,233},{176,2... | collective-permute-start | bytes 1179656 | tf_op jit(solution)/shard_map/ppermute | solution.py:41
  233.9 19.7 %collective-permute-start.21 = (bf16[128,1536]{1,0:T(8,128)(2,1)S(1)}, bf16[128,1536]{1,0:T(8,128)(2,1)S(1)}, u32[]{:S(2)}, u32[]{:S(2)}) collective-permute-start(bf16[128,1536]{1,0:T(8,128)(2,1)S(1)} %get-tuple-element.81), channel_id=1, source_target_pairs={{0,64},{9,73},{16,80},{25,89},{32,96},{41,105},{48,112},{57,121}} | collective-permute-start | bytes 1179656 | tf_op jit(solution)/shard_map/ppermute | solution.py:41
  235.2 22.6 %collective-permute-start.22 = (bf16[128,1536]{1,0:T(8,128)(2,1)S(1)}, bf16[128,1536]{1,0:T(8,128)(2,1)S(1)}, u32[]{:S(2)}, u32[]{:S(2)}) collective-permute-start(bf16[128,1536]{1,0:T(8,128)(2,1)S(1)} %get-tuple-element.82.refs_10_), channel_id=1, source_target_pairs={{0,64},{9,73},{16,80},{25,89},{32,96},{41,105},{48,112},{57,121}} | collective-permute-start | bytes 1179656 | tf_op jit(solution)/shard_map/ppermute | solution.py:41
  244.2 19.8 %collective-permute-start.23 = (bf16[128,1536]{1,0:T(8,128)(2,1)S(1)}, bf16[128,1536]{1,0:T(8,128)(2,1)S(1)}, u32[]{:S(2)}, u32[]{:S(2)}) collective-permute-start(bf16[128,1536]{1,0:T(8,128)(2,1)S(1)} %get-tuple-element.83), channel_id=1, source_target_pairs={{0,64},{9,73},{16,80},{25,89},{32,96},{41,105},{48,112},{57,121}} | collective-permute-start | bytes 1179656 | tf_op jit(solution)/shard_map/ppermute | solution.py:41
  245.6 22.7 %collective-permute-start.24 = (bf16[128,1536]{1,0:T(8,128)(2,1)S(1)}, bf16[128,1536]{1,0:T(8,128)(2,1)S(1)}, u32[]{:S(2)}, u32[]{:S(2)}) collective-permute-start(bf16[128,1536]{1,0:T(8,128)(2,1)S(1)} %get-tuple-element.84), channel_id=1, source_target_pairs={{0,64},{9,73},{16,80},{25,89},{32,96},{41,105},{48,112},{57,121}} | collective-permute-start | bytes 1179656 | tf_op jit(solution)/shard_map/ppermute | solution.py:41
  278.0 13.2 %collective-permute-start.25 = (bf16[128,1536]{1,0:T(8,128)(2,1)S(1)}, bf16[128,1536]{1,0:T(8,128)(2,1)S(1)}, u32[]{:S(2)}, u32[]{:S(2)}) collective-permute-start(bf16[128,1536]{1,0:T(8,128)(2,1)S(1)} %get-tuple-element.85), channel_id=1, source_target_pairs={{64,128},{73,137},{80,144},{89,153},{96,160},{105,169},{112,176},{... | collective-permute-start | bytes 1179656 | tf_op jit(solution)/shard_map/ppermute | solution.py:41
  279.4 14.2 %collective-permute-start.26 = (bf16[128,1536]{1,0:T(8,128)(2,1)S(1)}, bf16[128,1536]{1,0:T(8,128)(2,1)S(1)}, u32[]{:S(2)}, u32[]{:S(2)}) collective-permute-start(bf16[128,1536]{1,0:T(8,128)(2,1)S(1)} %get-tuple-element.86.refs_10_), channel_id=1, source_target_pairs={{64,128},{73,137},{80,144},{89,153},{96,160},{105,169},{112,176},{... | collective-permute-start | bytes 1179656 | tf_op jit(solution)/shard_map/ppermute | solution.py:41
  290.0 9.5 %collective-permute-start.28 = (bf16[128,1536]{1,0:T(8,128)(2,1)S(1)}, bf16[128,1536]{1,0:T(8,128)(2,1)S(1)}, u32[]{:S(2)}, u32[]{:S(2)}) collective-permute-start(bf16[128,1536]{1,0:T(8,128)(2,1)S(1)} %get-tuple-element.88), channel_id=1, source_target_pairs={{64,128},{73,137},{80,144},{89,153},{96,160},{105,169},{112,176},{... | collective-permute-start | bytes 1179656 | tf_op jit(solution)/shard_map/ppermute | solution.py:41
  309.2 10.5 %collective-permute-start.29 = (bf16[128,1536]{1,0:T(8,128)(2,1)S(1)}, bf16[128,1536]{1,0:T(8,128)(2,1)S(1)}, u32[]{:S(2)}, u32[]{:S(2)}) collective-permute-start(bf16[128,1536]{1,0:T(8,128)(2,1)S(1)} %get-tuple-element.89), channel_id=1, source_target_pairs={{128,192},{137,201},{144,208},{153,217},{160,224},{169,233},{176,2... | collective-permute-start | bytes 1179656 | tf_op jit(solution)/shard_map/ppermute | solution.py:41
  309.9 12.1 %collective-permute-start.30 = (bf16[128,1536]{1,0:T(8,128)(2,1)S(1)}, bf16[128,1536]{1,0:T(8,128)(2,1)S(1)}, u32[]{:S(2)}, u32[]{:S(2)}) collective-permute-start(bf16[128,1536]{1,0:T(8,128)(2,1)S(1)} %get-tuple-element.90.refs_10_), channel_id=1, source_target_pairs={{128,192},{137,201},{144,208},{153,217},{160,224},{169,233},{176,2... | collective-permute-start | bytes 1179656 | tf_op jit(solution)/shard_map/ppermute | solution.py:41
  319.0 7.5 %collective-permute-start.32 = (bf16[128,1536]{1,0:T(8,128)(2,1)S(1)}, bf16[128,1536]{1,0:T(8,128)(2,1)S(1)}, u32[]{:S(2)}, u32[]{:S(2)}) collective-permute-start(bf16[128,1536]{1,0:T(8,128)(2,1)S(1)} %get-tuple-element.92), channel_id=1, source_target_pairs={{128,192},{137,201},{144,208},{153,217},{160,224},{169,233},{176,2... | collective-permute-start | bytes 1179656 | tf_op jit(solution)/shard_map/ppermute | solution.py:41
  348.1 23.9 %all-to-all-start.4 = ((f32[32,8,128]{2,1,0:T(8,128)}), f32[32,8,128]{2,1,0:T(8,128)S(1)}, u32[]{:S(2)}, u32[]{:S(2)}) async-start(f32[32,8,128]{2,1,0:T(8,128)} %select_bitcast_fusion), calls=%async_computation.4 | async-start | bytes 262144 | tf_op jit(solution)/shard_map/all_to_all | solution.py:467
  (15 other events, 147.2 us)

commit v4 on v3

--- a/solution.py
+++ b/solution.py
@@ -377,13 +377,13 @@
     message = jnp.concatenate(
         [partial.reshape(Y, quarter, width), jnp.broadcast_to(both[None], (Y, 2, width))], 1
     )
-    message, attn_piece = beside(message, attn_mine)
     parts = lax.all_to_all(message, "y", split_axis=0, concat_axis=0, tiled=True)
     summed = jnp.sum(parts[:, :quarter].astype(F32), axis=0).astype(BF)
     both = parts[:, quarter:].reshape(1, 2 * Y, width)
     message = jnp.concatenate(
         [summed.reshape(Z, eighth, width), jnp.broadcast_to(both, (Z, 2 * Y, width))], 1
     )
+    message, attn_piece = beside(message, attn_mine)
     parts = lax.all_to_all(message, "z", split_axis=0, concat_axis=0, tiled=True)
     both = parts[:, eighth:].reshape(patches // rows_here, 2, width)[:, :, : latent.shape[1]]
     both = jnp.transpose(both, (1, 0, 2)).reshape(2, patches * latent_width // 128, 128)

time: 379 us -> 378 us (level)
  blocking collectives: 0 us -> 17.6 us
  waiting for transfers between devices: 69.8 us -> 57.1 us
  starting transfers between devices: 78.7 us -> 74.3 us
    all_to_all x0 -> x1, blocking collectives: none -> 17.6 us  [on_device(): lax.all_to_all(message, 'y', split_axis=0, concat_axis=0, tiled=True)]
    all_to_all x1 -> x0, waiting for transfers between devices: 14 us -> none  [on_device(): lax.all_to_all(message, 'y', split_axis=0, concat_axis=0, tiled=True)]
    all_to_all x1 -> x0, starting transfers between devices: 6.65 us -> none  [on_device(): lax.all_to_all(message, 'y', split_axis=0, concat_axis=0, tiled=True)]
  transfers between devices with their start and end apart: 39 -> 38, of which waited for: 14 -> 13; matrix products, arithmetic and copies ran while one was open for 1% -> 1% of each run, Pallas kernels for 27% -> 27%
where the time goes in v4:
time: 378 us; the launch traced here: 372 us
  Pallas kernels  208 us (55%)
  starting transfers between devices  74.3 us (20%)
  waiting for transfers between devices  57.1 us (15%)
  blocking collectives  17.6 us (5%)
  local copies, waits for them, and re-layouts  7.8 us (2%)
  other arithmetic  4.41 us (1%)
    pallas_call x16, Pallas kernels, attention(): pl.pallas_call(functools.partial(attention_kernel, queries=queries, block...  121 us
    pallas_call x33, Pallas kernels, product(): pl.pallas_call(functools.partial(product_kernel, pieces=len(rows), column...  74.8 us
    ppermute x34, starting transfers between devices, move(): return lax.ppermute(value, AXES, [(flat(*a), flat(*b)) for a, b in pairs])  38.9 us
    ppermute x34, waiting for transfers between devices, move(): return lax.ppermute(value, AXES, [(flat(*a), flat(*b)) for a, b in pairs])  22.2 us
    all_to_all x2, waiting for transfers between devices, on_device(): lax.all_to_all(message, 'z', split_axis=0, concat_axis=0, tiled=True)  20.4 us
    all_to_all x1, blocking collectives, on_device(): lax.all_to_all(message, 'y', split_axis=0, concat_axis=0, tiled=True)  17.6 us
    all_to_all x2, starting transfers between devices, on_device(): lax.all_to_all(message, 'z', split_axis=0, concat_axis=0, tiled=True)  14.2 us
    all_to_all x1, starting transfers between devices, on_device(): lax.all_to_all(latent.reshape(Z * Y, rows_here * latent_width // 128, 128...  13.4 us
  transfers between devices with their start and end apart: 38, of which 13 were waited for; matrix products, arithmetic and copies ran while one was open for 1% of the time, Pallas kernels for 27%

profile of v4, /device:TPU:2, one launch (start us, length us, event | category | flops | bytes accessed | tf_op | source)
XLA Modules:
  0.0 372.5 jit_solution(12258662824820384583)
XLA Ops:
  2.4 17.6 %all_to_all.25 = bf16[4,66,1536]{2,1,0:T(8,128)(2,1)S(1)} all-to-all(bf16[4,66,1536]{2,1,0:T(8,128)(2,1)S(1)} %pad_maximum_fusion), channel_id=1, replica_groups=mesh['x'=4,'z'=8,'y'=4,'c'=2] {'y'}, dimensions={0} | all-to-all | bytes 1622016 | tf_op jit(solution)/shard_map/all_to_all | solution.py:380
  23.1 10.8 %all-to-all-start.1 = ((bf16[8,16,1536]{2,1,0:T(8,128)(2,1)}), bf16[8,16,1536]{2,1,0:T(8,128)(2,1)S(1)}, u32[]{:S(2)}, u32[]{:S(2)}) async-start(bf16[8,16,1536]{2,1,0:T(8,128)(2,1)} %pad_maximum_fusion.1), calls=%async_computation.1 | async-start | bytes 786432 | tf_op jit(solution)/shard_map/all_to_all | solution.py:387
  38.8 11.2 %all-to-all-done.1.parts_ref = bf16[8,16,1536]{2,1,0:T(8,128)(2,1)S(1)} async-done(((bf16[8,16,1536]{2,1,0:T(8,128)(2,1)}), bf16[8,16,1536]{2,1,0:T(8,128)(2,1)S(1)}, u32[]{:S(2)}, u32[]{:S(2)}) %all-to-all-start.1) | async-done | bytes 393248 | tf_op jit(solution)/shard_map/all_to_all | solution.py:387
  52.5 7.8 %all-to-all-start.2 = ((bf16[4,8,1536]{2,1,0:T(8,128)(2,1)}), bf16[4,8,1536]{2,1,0:T(8,128)(2,1)S(1)}, u32[]{:S(2)}, u32[]{:S(2)}) async-start(bf16[4,8,1536]{2,1,0:T(8,128)(2,1)} %spread.1), calls=%async_computation.2 | async-start | bytes 196608 | tf_op jit(solution)/shard_map/all_to_all | solution.py:407
  60.6 4.1 %all-to-all-done.2.rows_ref = bf16[4,8,1536]{2,1,0:T(8,128)(2,1)S(1)} async-done(((bf16[4,8,1536]{2,1,0:T(8,128)(2,1)}), bf16[4,8,1536]{2,1,0:T(8,128)(2,1)S(1)}, u32[]{:S(2)}, u32[]{:S(2)}) %all-to-all-start.2) | async-done | bytes 98336 | tf_op jit(solution)/shard_map/all_to_all | solution.py:407
  66.7 3.4 all-to-all-start.3
  70.6 9.2 %all-to-all-done.3 = bf16[8,8,1536]{2,1,0:T(8,128)(2,1)S(1)} async-done(((bf16[8,8,1536]{2,1,0:T(8,128)(2,1)}), bf16[8,8,1536]{2,1,0:T(8,128)(2,1)S(1)}, u32[]{:S(2)}, u32[]{:S(2)}) %all-to-all-start.3) | async-done | bytes 196640 | tf_op jit(solution)/shard_map/all_to_all | solution.py:410
  87.5 3.0 copy-done.2
  90.5 3.5 joined.2.refs_1_.refs_4_
  103.1 2.6 product.37.refs_4_
  105.7 7.5 %attention.16 = (bf16[128,1536]{1,0:T(8,128)(2,1)S(1)}, bf16[128,1536]{1,0:T(8,128)(2,1)S(1)}) custom-call(bf16[128,4608]{1,0:T(8,128)(2,1)S(1)} %product.33.refs_4_.refs_0_, bf16[128,4608]{1,0:T(8,128)(2,1)S(1)} %product.34.refs_4_.refs_1_, bf16[128,4608]{1,0:T(8,128)(2,1)S(1)} %product.35.refs_4_.refs_2_, bf16[128,4608]{1,0:T(8,128)(2,1)S(1)} %product.36.refs_3_, ...), custom_call_target="tpu_custom_call" | custom-call | flops 2415919104 | bytes 8388608 | tf_op jit(solution)/shard_map/attention/pallas_call | solution.py:310
  116.2 7.5 %attention.17 = (bf16[128,1536]{1,0:T(8,128)(2,1)S(1)}, bf16[128,1536]{1,0:T(8,128)(2,1)S(1)}) custom-call(bf16[128,4608]{1,0:T(8,128)(2,1)S(1)} %product.33.refs_4_.refs_0_, bf16[128,4608]{1,0:T(8,128)(2,1)S(1)} %product.34.refs_4_.refs_1_, bf16[128,4608]{1,0:T(8,128)(2,1)S(1)} %product.35.refs_4_.refs_2_, bf16[128,4608]{1,0:T(8,128)(2,1)S(1)} %product.36.refs_3_, ...), custom_call_target="tpu_custom_call" | custom-call | flops 2415919104 | bytes 8388608 | tf_op jit(solution)/shard_map/attention/pallas_call | solution.py:310
  130.9 2.6 collective-permute-done.10.refs_0_.refs_8_
  139.9 7.5 %attention.18 = (bf16[128,1536]{1,0:T(8,128)(2,1)S(1)}, bf16[128,1536]{1,0:T(8,128)(2,1)S(1)}) custom-call(bf16[128,4608]{1,0:T(8,128)(2,1)S(1)} %product.38.refs_4_.refs_0_, bf16[128,4608]{1,0:T(8,128)(2,1)S(1)} %product.39.refs_4_.refs_1_, bf16[128,4608]{1,0:T(8,128)(2,1)S(1)} %product.40.refs_4_.refs_2_, bf16[128,4608]{1,0:T(8,128)(2,1)S(1)} %product.41.refs_3_, ...), custom_call_target="tpu_custom_call" | custom-call | flops 2415919104 | bytes 8388608 | tf_op jit(solution)/shard_map/attention/pallas_call | solution.py:310
  150.3 7.5 %attention.19 = (bf16[128,1536]{1,0:T(8,128)(2,1)S(1)}, bf16[128,1536]{1,0:T(8,128)(2,1)S(1)}) custom-call(bf16[128,4608]{1,0:T(8,128)(2,1)S(1)} %product.38.refs_4_.refs_0_, bf16[128,4608]{1,0:T(8,128)(2,1)S(1)} %product.39.refs_4_.refs_1_, bf16[128,4608]{1,0:T(8,128)(2,1)S(1)} %product.40.refs_4_.refs_2_, bf16[128,4608]{1,0:T(8,128)(2,1)S(1)} %product.41.refs_3_, ...), custom_call_target="tpu_custom_call" | custom-call | flops 2415919104 | bytes 8388608 | tf_op jit(solution)/shard_map/attention/pallas_call | solution.py:310
  170.9 7.5 %attention.20 = (bf16[128,1536]{1,0:T(8,128)(2,1)S(1)}, bf16[128,1536]{1,0:T(8,128)(2,1)S(1)}) custom-call(bf16[128,4608]{1,0:T(8,128)(2,1)S(1)} %product.42.refs_4_.refs_0_, bf16[128,4608]{1,0:T(8,128)(2,1)S(1)} %product.43.refs_4_.refs_1_, bf16[128,4608]{1,0:T(8,128)(2,1)S(1)} %product.44.refs_4_.refs_2_, bf16[128,4608]{1,0:T(8,128)(2,1)S(1)} %product.45.refs_3_, ...), custom_call_target="tpu_custom_call" | custom-call | flops 2415919104 | bytes 8388608 | tf_op jit(solution)/shard_map/attention/pallas_call | solution.py:310
  180.0 7.5 %attention.21 = (bf16[128,1536]{1,0:T(8,128)(2,1)S(1)}, bf16[128,1536]{1,0:T(8,128)(2,1)S(1)}) custom-call(bf16[128,4608]{1,0:T(8,128)(2,1)S(1)} %product.42.refs_4_.refs_0_, bf16[128,4608]{1,0:T(8,128)(2,1)S(1)} %product.43.refs_4_.refs_1_, bf16[128,4608]{1,0:T(8,128)(2,1)S(1)} %product.44.refs_4_.refs_2_, bf16[128,4608]{1,0:T(8,128)(2,1)S(1)} %product.45.refs_3_, ...), custom_call_target="tpu_custom_call" | custom-call | flops 2415919104 | bytes 8388608 | tf_op jit(solution)/shard_map/attention/pallas_call | solution.py:310
  198.1 7.9 %attention.22 = (bf16[128,1536]{1,0:T(8,128)(2,1)S(1)}, bf16[128,1536]{1,0:T(8,128)(2,1)S(1)}) custom-call(bf16[128,4608]{1,0:T(8,128)(2,1)S(1)} %product.46.refs_4_.refs_0_, bf16[128,4608]{1,0:T(8,128)(2,1)S(1)} %product.47.refs_4_.refs_1_, bf16[128,4608]{1,0:T(8,128)(2,1)S(1)} %product.48.refs_4_.refs_2_, bf16[128,4608]{1,0:T(8,128)(2,1)S(1)} %product.49.refs_3_, ...), custom_call_target="tpu_custom_call" | custom-call | flops 2415919104 | bytes 8388608 | tf_op jit(solution)/shard_map/attention/pallas_call | solution.py:310
  206.1 7.5 %attention.23 = (bf16[128,1536]{1,0:T(8,128)(2,1)S(1)}, bf16[128,1536]{1,0:T(8,128)(2,1)S(1)}) custom-call(bf16[128,4608]{1,0:T(8,128)(2,1)S(1)} %product.46.refs_4_.refs_0_, bf16[128,4608]{1,0:T(8,128)(2,1)S(1)} %product.47.refs_4_.refs_1_, bf16[128,4608]{1,0:T(8,128)(2,1)S(1)} %product.48.refs_4_.refs_2_, bf16[128,4608]{1,0:T(8,128)(2,1)S(1)} %product.49.refs_3_, ...), custom_call_target="tpu_custom_call" | custom-call | flops 2415919104 | bytes 8388608 | tf_op jit(solution)/shard_map/attention/pallas_call | solution.py:310
  225.9 7.5 %attention.24 = (bf16[128,1536]{1,0:T(8,128)(2,1)S(1)}, bf16[128,1536]{1,0:T(8,128)(2,1)S(1)}) custom-call(bf16[128,4608]{1,0:T(8,128)(2,1)S(1)} %product.50.refs_4_.refs_0_, bf16[128,4608]{1,0:T(8,128)(2,1)S(1)} %product.51.refs_4_.refs_1_, bf16[128,4608]{1,0:T(8,128)(2,1)S(1)} %product.52.refs_4_.refs_2_, bf16[128,4608]{1,0:T(8,128)(2,1)S(1)} %product.53.refs_3_, ...), custom_call_target="tpu_custom_call" | custom-call | flops 2415919104 | bytes 8388608 | tf_op jit(solution)/shard_map/attention/pallas_call | solution.py:310
  236.3 7.5 %attention.25 = (bf16[128,1536]{1,0:T(8,128)(2,1)S(1)}, bf16[128,1536]{1,0:T(8,128)(2,1)S(1)}) custom-call(bf16[128,4608]{1,0:T(8,128)(2,1)S(1)} %product.50.refs_4_.refs_0_, bf16[128,4608]{1,0:T(8,128)(2,1)S(1)} %product.51.refs_4_.refs_1_, bf16[128,4608]{1,0:T(8,128)(2,1)S(1)} %product.52.refs_4_.refs_2_, bf16[128,4608]{1,0:T(8,128)(2,1)S(1)} %product.53.refs_3_, ...), custom_call_target="tpu_custom_call" | custom-call | flops 2415919104 | bytes 8388608 | tf_op jit(solution)/shard_map/attention/pallas_call | solution.py:310
  246.4 6.8 %collective-permute-done.21.refs_0_.refs_8_ = bf16[128,1536]{1,0:T(8,128)(2,1)S(1)} collective-permute-done((bf16[128,1536]{1,0:T(8,128)(2,1)S(1)}, bf16[128,1536]{1,0:T(8,128)(2,1)S(1)}, u32[]{:S(2)}, u32[]{:S(2)}) %collective-permute-start.21) | collective-permute-done | bytes 393248 | tf_op jit(solution)/shard_map/ppermute | solution.py:41
  259.7 3.9 %collective-permute-done.23.refs_0_.refs_8_ = bf16[128,1536]{1,0:T(8,128)(2,1)S(1)} collective-permute-done((bf16[128,1536]{1,0:T(8,128)(2,1)S(1)}, bf16[128,1536]{1,0:T(8,128)(2,1)S(1)}, u32[]{:S(2)}, u32[]{:S(2)}) %collective-permute-start.23) | collective-permute-done | bytes 393248 | tf_op jit(solution)/shard_map/ppermute | solution.py:41
  270.1 7.5 %attention.26 = (bf16[128,1536]{1,0:T(8,128)(2,1)S(1)}, bf16[128,1536]{1,0:T(8,128)(2,1)S(1)}) custom-call(bf16[128,4608]{1,0:T(8,128)(2,1)S(1)} %product.54.refs_4_.refs_0_, bf16[128,4608]{1,0:T(8,128)(2,1)S(1)} %product.55.refs_4_.refs_1_, bf16[128,4608]{1,0:T(8,128)(2,1)S(1)} %product.56.refs_4_.refs_2_, bf16[128,4608]{1,0:T(8,128)(2,1)S(1)} %product.57.refs_3_, ...), custom_call_target="tpu_custom_call" | custom-call | flops 2415919104 | bytes 8388608 | tf_op jit(solution)/shard_map/attention/pallas_call | solution.py:310
  280.7 7.5 %attention.27 = (bf16[128,1536]{1,0:T(8,128)(2,1)S(1)}, bf16[128,1536]{1,0:T(8,128)(2,1)S(1)}) custom-call(bf16[128,4608]{1,0:T(8,128)(2,1)S(1)} %product.54.refs_4_.refs_0_, bf16[128,4608]{1,0:T(8,128)(2,1)S(1)} %product.55.refs_4_.refs_1_, bf16[128,4608]{1,0:T(8,128)(2,1)S(1)} %product.56.refs_4_.refs_2_, bf16[128,4608]{1,0:T(8,128)(2,1)S(1)} %product.57.refs_3_, ...), custom_call_target="tpu_custom_call" | custom-call | flops 2415919104 | bytes 8388608 | tf_op jit(solution)/shard_map/attention/pallas_call | solution.py:310
  301.3 7.5 %attention.28 = (bf16[128,1536]{1,0:T(8,128)(2,1)S(1)}, bf16[128,1536]{1,0:T(8,128)(2,1)S(1)}) custom-call(bf16[128,4608]{1,0:T(8,128)(2,1)S(1)} %product.58.refs_4_.refs_0_, bf16[128,4608]{1,0:T(8,128)(2,1)S(1)} %product.59.refs_4_.refs_1_, bf16[128,4608]{1,0:T(8,128)(2,1)S(1)} %product.60.refs_4_.refs_2_, bf16[128,4608]{1,0:T(8,128)(2,1)S(1)} %product.61.refs_3_, ...), custom_call_target="tpu_custom_call" | custom-call | flops 2415919104 | bytes 8388608 | tf_op jit(solution)/shard_map/attention/pallas_call | solution.py:310
  310.4 7.5 %attention.29 = (bf16[128,1536]{1,0:T(8,128)(2,1)S(1)}, bf16[128,1536]{1,0:T(8,128)(2,1)S(1)}) custom-call(bf16[128,4608]{1,0:T(8,128)(2,1)S(1)} %product.58.refs_4_.refs_0_, bf16[128,4608]{1,0:T(8,128)(2,1)S(1)} %product.59.refs_4_.refs_1_, bf16[128,4608]{1,0:T(8,128)(2,1)S(1)} %product.60.refs_4_.refs_2_, bf16[128,4608]{1,0:T(8,128)(2,1)S(1)} %product.61.refs_3_, ...), custom_call_target="tpu_custom_call" | custom-call | flops 2415919104 | bytes 8388608 | tf_op jit(solution)/shard_map/attention/pallas_call | solution.py:310
  328.4 7.7 %attention.30 = (bf16[128,1536]{1,0:T(8,128)(2,1)S(1)}, bf16[128,1536]{1,0:T(8,128)(2,1)S(1)}) custom-call(bf16[128,4608]{1,0:T(8,128)(2,1)S(1)} %product.62.refs_4_.refs_0_, bf16[128,4608]{1,0:T(8,128)(2,1)S(1)} %product.63.refs_4_.refs_1_, bf16[128,4608]{1,0:T(8,128)(2,1)S(1)} %product.64.refs_4_.refs_2_, bf16[128,4608]{1,0:T(8,128)(2,1)S(1)} %product.65.refs_3_, ...), custom_call_target="tpu_custom_call" | custom-call | flops 2415919104 | bytes 8388608 | tf_op jit(solution)/shard_map/attention/pallas_call | solution.py:310
  336.2 7.5 %attention.31 = (bf16[128,1536]{1,0:T(8,128)(2,1)S(1)}, bf16[128,1536]{1,0:T(8,128)(2,1)S(1)}) custom-call(bf16[128,4608]{1,0:T(8,128)(2,1)S(1)} %product.62.refs_4_.refs_0_, bf16[128,4608]{1,0:T(8,128)(2,1)S(1)} %product.63.refs_4_.refs_1_, bf16[128,4608]{1,0:T(8,128)(2,1)S(1)} %product.64.refs_4_.refs_2_, bf16[128,4608]{1,0:T(8,128)(2,1)S(1)} %product.65.refs_3_, ...), custom_call_target="tpu_custom_call" | custom-call | flops 2415919104 | bytes 8388608 | tf_op jit(solution)/shard_map/attention/pallas_call | solution.py:310
  343.7 2.5 finish.3
  347.7 13.4 %all-to-all-start.4 = ((f32[32,8,128]{2,1,0:T(8,128)}), f32[32,8,128]{2,1,0:T(8,128)S(1)}, u32[]{:S(2)}, u32[]{:S(2)}) async-start(f32[32,8,128]{2,1,0:T(8,128)} %select_bitcast_fusion), calls=%async_computation.4 | async-start | bytes 262144 | tf_op jit(solution)/shard_map/all_to_all | solution.py:467
  361.1 10.5 %all-to-all-done.4 = f32[32,8,128]{2,1,0:T(8,128)S(1)} async-done(((f32[32,8,128]{2,1,0:T(8,128)}), f32[32,8,128]{2,1,0:T(8,128)S(1)}, u32[]{:S(2)}, u32[]{:S(2)}) %all-to-all-start.4) | async-done | bytes 131104 | tf_op jit(solution)/shard_map/all_to_all | solution.py:467
  (156 shorter events, 137.1 us)
Async XLA Ops:
  21.0 66.5 %collective-permute-start.1 = (bf16[768,4608]{1,0:T(8,128)(2,1)}, bf16[768,4608]{1,0:T(8,128)(2,1)}, u32[]{:S(2)}, u32[]{:S(2)}) collective-permute-start(bf16[768,4608]{1,0:T(8,128)(2,1)} %bitcast.32), channel_id=1, source_target_pairs={{1,0},{8,9},{17,16},{24,25},{33,32},{40,41},{49,48},{56,57},{65,64... | collective-permute-start | bytes 21233672 | tf_op jit(solution)/shard_map/ppermute | solution.py:41
  23.1 26.9 %all-to-all-start.1 = ((bf16[8,16,1536]{2,1,0:T(8,128)(2,1)}), bf16[8,16,1536]{2,1,0:T(8,128)(2,1)S(1)}, u32[]{:S(2)}, u32[]{:S(2)}) async-start(bf16[8,16,1536]{2,1,0:T(8,128)(2,1)} %pad_maximum_fusion.1), calls=%async_computation.1 | async-start | bytes 786432 | tf_op jit(solution)/shard_map/all_to_all | solution.py:387
  50.3 10.1 %collective-permute-start = (bf16[256,128]{1,0:T(8,128)(2,1)S(1)}, bf16[256,128]{1,0:T(8,128)(2,1)S(1)}, u32[]{:S(2)}, u32[]{:S(2)}) collective-permute-start(bf16[256,128]{1,0:T(8,128)(2,1)S(1)} %squeeze.32), channel_id=1, source_target_pairs={{80,16},{89,25},{160,32},{169,41},{240,48},{249,57}} | collective-permute-start | bytes 196616 | tf_op jit(solution)/shard_map/ppermute | solution.py:41
  51.1 9.4 %collective-permute-start.2 = (bf16[2,256,128]{2,1,0:T(8,128)(2,1)S(1)}, bf16[2,256,128]{2,1,0:T(8,128)(2,1)S(1)}, u32[]{:S(2)}, u32[]{:S(2)}) collective-permute-start(bf16[2,256,128]{2,1,0:T(8,128)(2,1)S(1)} %reshape.145), channel_id=1, source_target_pairs={{0,192},{9,201},{80,208},{89,217},{160,224},{169,233}} | collective-permute-start | bytes 393224 | tf_op jit(solution)/shard_map/ppermute | solution.py:41
  52.5 12.2 %all-to-all-start.2 = ((bf16[4,8,1536]{2,1,0:T(8,128)(2,1)}), bf16[4,8,1536]{2,1,0:T(8,128)(2,1)S(1)}, u32[]{:S(2)}, u32[]{:S(2)}) async-start(bf16[4,8,1536]{2,1,0:T(8,128)(2,1)} %spread.1), calls=%async_computation.2 | async-start | bytes 196608 | tf_op jit(solution)/shard_map/all_to_all | solution.py:407
  65.4 18.5 %collective-permute-start.7 = (bf16[768,1536]{1,0:T(8,128)(2,1)}, bf16[768,1536]{1,0:T(8,128)(2,1)}, u32[]{:S(2)}, u32[]{:S(2)}) collective-permute-start(bf16[768,1536]{1,0:T(8,128)(2,1)} %bitcast.34), channel_id=1, source_target_pairs={{1,0},{8,9},{17,16},{24,25},{33,32},{40,41},{49,48},{56,57},{65,64... | collective-permute-start | bytes 7077896 | tf_op jit(solution)/shard_map/ppermute | solution.py:41
  66.7 13.2 %all-to-all-start.3 = ((bf16[8,8,1536]{2,1,0:T(8,128)(2,1)}), bf16[8,8,1536]{2,1,0:T(8,128)(2,1)S(1)}, u32[]{:S(2)}, u32[]{:S(2)}) async-start(bf16[8,8,1536]{2,1,0:T(8,128)(2,1)} %twice.1), calls=%async_computation.3 | async-start | bytes 393216 | tf_op jit(solution)/shard_map/all_to_all | solution.py:410
  79.9 23.2 %collective-permute-start.4 = (bf16[64,1536]{1,0:T(8,128)(2,1)S(1)}, bf16[64,1536]{1,0:T(8,128)(2,1)S(1)}, u32[]{:S(2)}, u32[]{:S(2)}) collective-permute-start(bf16[64,1536]{1,0:T(8,128)(2,1)S(1)} %bitcast.36), channel_id=1, source_target_pairs={{2,0},{11,9},{18,16},{27,25},{34,32},{43,41},{50,48},{59,57},{66,6... | collective-permute-start | bytes 589832 | tf_op jit(solution)/shard_map/ppermute | solution.py:41
  81.2 21.9 %collective-permute-start.5 = (bf16[64,1536]{1,0:T(8,128)(2,1)S(1)}, bf16[64,1536]{1,0:T(8,128)(2,1)S(1)}, u32[]{:S(2)}, u32[]{:S(2)}) collective-permute-start(bf16[64,1536]{1,0:T(8,128)(2,1)S(1)} %bitcast.37), channel_id=1, source_target_pairs={{4,0},{13,9},{20,16},{29,25},{36,32},{45,41},{52,48},{61,57},{68,6... | collective-permute-start | bytes 589832 | tf_op jit(solution)/shard_map/ppermute | solution.py:41
  82.5 20.6 %collective-permute-start.6 = (bf16[64,1536]{1,0:T(8,128)(2,1)S(1)}, bf16[64,1536]{1,0:T(8,128)(2,1)S(1)}, u32[]{:S(2)}, u32[]{:S(2)}) collective-permute-start(bf16[64,1536]{1,0:T(8,128)(2,1)S(1)} %bitcast.38), channel_id=1, source_target_pairs={{6,0},{15,9},{22,16},{31,25},{38,32},{47,41},{54,48},{63,57},{70,6... | collective-permute-start | bytes 589832 | tf_op jit(solution)/shard_map/ppermute | solution.py:41
  113.2 13.2 %collective-permute-start.8 = (bf16[128,1536]{1,0:T(8,128)(2,1)S(1)}, bf16[128,1536]{1,0:T(8,128)(2,1)S(1)}, u32[]{:S(2)}, u32[]{:S(2)}) collective-permute-start(bf16[128,1536]{1,0:T(8,128)(2,1)S(1)} %get-tuple-element.60), channel_id=1, source_target_pairs={{0,64},{9,73},{16,80},{25,89},{32,96},{41,105},{48,112},{57,121}} | collective-permute-start | bytes 1179656 | tf_op jit(solution)/shard_map/ppermute | solution.py:41
  114.5 14.1 %collective-permute-start.9 = (bf16[128,1536]{1,0:T(8,128)(2,1)S(1)}, bf16[128,1536]{1,0:T(8,128)(2,1)S(1)}, u32[]{:S(2)}, u32[]{:S(2)}) collective-permute-start(bf16[128,1536]{1,0:T(8,128)(2,1)S(1)} %get-tuple-element.61.refs_10_), channel_id=1, source_target_pairs={{0,64},{9,73},{16,80},{25,89},{32,96},{41,105},{48,112},{57,121}} | collective-permute-start | bytes 1179656 | tf_op jit(solution)/shard_map/ppermute | solution.py:41
  123.8 9.7 %collective-permute-start.10 = (bf16[128,1536]{1,0:T(8,128)(2,1)S(1)}, bf16[128,1536]{1,0:T(8,128)(2,1)S(1)}, u32[]{:S(2)}, u32[]{:S(2)}) collective-permute-start(bf16[128,1536]{1,0:T(8,128)(2,1)S(1)} %get-tuple-element.62), channel_id=1, source_target_pairs={{0,64},{9,73},{16,80},{25,89},{32,96},{41,105},{48,112},{57,121}} | collective-permute-start | bytes 1179656 | tf_op jit(solution)/shard_map/ppermute | solution.py:41
  125.1 12.6 %collective-permute-start.11 = (bf16[128,1536]{1,0:T(8,128)(2,1)S(1)}, bf16[128,1536]{1,0:T(8,128)(2,1)S(1)}, u32[]{:S(2)}, u32[]{:S(2)}) collective-permute-start(bf16[128,1536]{1,0:T(8,128)(2,1)S(1)} %get-tuple-element.63), channel_id=1, source_target_pairs={{0,64},{9,73},{16,80},{25,89},{32,96},{41,105},{48,112},{57,121}} | collective-permute-start | bytes 1179656 | tf_op jit(solution)/shard_map/ppermute | solution.py:41
  147.5 13.0 %collective-permute-start.12 = (bf16[128,1536]{1,0:T(8,128)(2,1)S(1)}, bf16[128,1536]{1,0:T(8,128)(2,1)S(1)}, u32[]{:S(2)}, u32[]{:S(2)}) collective-permute-start(bf16[128,1536]{1,0:T(8,128)(2,1)S(1)} %get-tuple-element.64), channel_id=1, source_target_pairs={{64,128},{73,137},{80,144},{89,153},{96,160},{105,169},{112,176},{... | collective-permute-start | bytes 1179656 | tf_op jit(solution)/shard_map/ppermute | solution.py:41
  148.8 14.0 %collective-permute-start.13 = (bf16[128,1536]{1,0:T(8,128)(2,1)S(1)}, bf16[128,1536]{1,0:T(8,128)(2,1)S(1)}, u32[]{:S(2)}, u32[]{:S(2)}) collective-permute-start(bf16[128,1536]{1,0:T(8,128)(2,1)S(1)} %get-tuple-element.65.refs_10_), channel_id=1, source_target_pairs={{64,128},{73,137},{80,144},{89,153},{96,160},{105,169},{112,176},{... | collective-permute-start | bytes 1179656 | tf_op jit(solution)/shard_map/ppermute | solution.py:41
  157.8 7.2 %collective-permute-start.14 = (bf16[128,1536]{1,0:T(8,128)(2,1)S(1)}, bf16[128,1536]{1,0:T(8,128)(2,1)S(1)}, u32[]{:S(2)}, u32[]{:S(2)}) collective-permute-start(bf16[128,1536]{1,0:T(8,128)(2,1)S(1)} %get-tuple-element.66), channel_id=1, source_target_pairs={{64,128},{73,137},{80,144},{89,153},{96,160},{105,169},{112,176},{... | collective-permute-start | bytes 1179656 | tf_op jit(solution)/shard_map/ppermute | solution.py:41
  159.2 9.5 %collective-permute-start.15 = (bf16[128,1536]{1,0:T(8,128)(2,1)S(1)}, bf16[128,1536]{1,0:T(8,128)(2,1)S(1)}, u32[]{:S(2)}, u32[]{:S(2)}) collective-permute-start(bf16[128,1536]{1,0:T(8,128)(2,1)S(1)} %get-tuple-element.67), channel_id=1, source_target_pairs={{64,128},{73,137},{80,144},{89,153},{96,160},{105,169},{112,176},{... | collective-permute-start | bytes 1179656 | tf_op jit(solution)/shard_map/ppermute | solution.py:41
  178.4 10.6 %collective-permute-start.16 = (bf16[128,1536]{1,0:T(8,128)(2,1)S(1)}, bf16[128,1536]{1,0:T(8,128)(2,1)S(1)}, u32[]{:S(2)}, u32[]{:S(2)}) collective-permute-start(bf16[128,1536]{1,0:T(8,128)(2,1)S(1)} %get-tuple-element.68), channel_id=1, source_target_pairs={{128,192},{137,201},{144,208},{153,217},{160,224},{169,233},{176,2... | collective-permute-start | bytes 1179656 | tf_op jit(solution)/shard_map/ppermute | solution.py:41
  179.1 12.2 %collective-permute-start.17 = (bf16[128,1536]{1,0:T(8,128)(2,1)S(1)}, bf16[128,1536]{1,0:T(8,128)(2,1)S(1)}, u32[]{:S(2)}, u32[]{:S(2)}) collective-permute-start(bf16[128,1536]{1,0:T(8,128)(2,1)S(1)} %get-tuple-element.69.refs_10_), channel_id=1, source_target_pairs={{128,192},{137,201},{144,208},{153,217},{160,224},{169,233},{176,2... | collective-permute-start | bytes 1179656 | tf_op jit(solution)/shard_map/ppermute | solution.py:41
  188.4 7.5 %collective-permute-start.19 = (bf16[128,1536]{1,0:T(8,128)(2,1)S(1)}, bf16[128,1536]{1,0:T(8,128)(2,1)S(1)}, u32[]{:S(2)}, u32[]{:S(2)}) collective-permute-start(bf16[128,1536]{1,0:T(8,128)(2,1)S(1)} %get-tuple-element.71), channel_id=1, source_target_pairs={{128,192},{137,201},{144,208},{153,217},{160,224},{169,233},{176,2... | collective-permute-start | bytes 1179656 | tf_op jit(solution)/shard_map/ppermute | solution.py:41
  233.5 19.7 %collective-permute-start.21 = (bf16[128,1536]{1,0:T(8,128)(2,1)S(1)}, bf16[128,1536]{1,0:T(8,128)(2,1)S(1)}, u32[]{:S(2)}, u32[]{:S(2)}) collective-permute-start(bf16[128,1536]{1,0:T(8,128)(2,1)S(1)} %get-tuple-element.81), channel_id=1, source_target_pairs={{0,64},{9,73},{16,80},{25,89},{32,96},{41,105},{48,112},{57,121}} | collective-permute-start | bytes 1179656 | tf_op jit(solution)/shard_map/ppermute | solution.py:41
  234.8 22.6 %collective-permute-start.22 = (bf16[128,1536]{1,0:T(8,128)(2,1)S(1)}, bf16[128,1536]{1,0:T(8,128)(2,1)S(1)}, u32[]{:S(2)}, u32[]{:S(2)}) collective-permute-start(bf16[128,1536]{1,0:T(8,128)(2,1)S(1)} %get-tuple-element.82.refs_10_), channel_id=1, source_target_pairs={{0,64},{9,73},{16,80},{25,89},{32,96},{41,105},{48,112},{57,121}} | collective-permute-start | bytes 1179656 | tf_op jit(solution)/shard_map/ppermute | solution.py:41
  243.8 19.8 %collective-permute-start.23 = (bf16[128,1536]{1,0:T(8,128)(2,1)S(1)}, bf16[128,1536]{1,0:T(8,128)(2,1)S(1)}, u32[]{:S(2)}, u32[]{:S(2)}) collective-permute-start(bf16[128,1536]{1,0:T(8,128)(2,1)S(1)} %get-tuple-element.83), channel_id=1, source_target_pairs={{0,64},{9,73},{16,80},{25,89},{32,96},{41,105},{48,112},{57,121}} | collective-permute-start | bytes 1179656 | tf_op jit(solution)/shard_map/ppermute | solution.py:41
  245.1 22.7 %collective-permute-start.24 = (bf16[128,1536]{1,0:T(8,128)(2,1)S(1)}, bf16[128,1536]{1,0:T(8,128)(2,1)S(1)}, u32[]{:S(2)}, u32[]{:S(2)}) collective-permute-start(bf16[128,1536]{1,0:T(8,128)(2,1)S(1)} %get-tuple-element.84), channel_id=1, source_target_pairs={{0,64},{9,73},{16,80},{25,89},{32,96},{41,105},{48,112},{57,121}} | collective-permute-start | bytes 1179656 | tf_op jit(solution)/shard_map/ppermute | solution.py:41
  277.6 13.2 %collective-permute-start.25 = (bf16[128,1536]{1,0:T(8,128)(2,1)S(1)}, bf16[128,1536]{1,0:T(8,128)(2,1)S(1)}, u32[]{:S(2)}, u32[]{:S(2)}) collective-permute-start(bf16[128,1536]{1,0:T(8,128)(2,1)S(1)} %get-tuple-element.85), channel_id=1, source_target_pairs={{64,128},{73,137},{80,144},{89,153},{96,160},{105,169},{112,176},{... | collective-permute-start | bytes 1179656 | tf_op jit(solution)/shard_map/ppermute | solution.py:41
  279.0 14.2 %collective-permute-start.26 = (bf16[128,1536]{1,0:T(8,128)(2,1)S(1)}, bf16[128,1536]{1,0:T(8,128)(2,1)S(1)}, u32[]{:S(2)}, u32[]{:S(2)}) collective-permute-start(bf16[128,1536]{1,0:T(8,128)(2,1)S(1)} %get-tuple-element.86.refs_10_), channel_id=1, source_target_pairs={{64,128},{73,137},{80,144},{89,153},{96,160},{105,169},{112,176},{... | collective-permute-start | bytes 1179656 | tf_op jit(solution)/shard_map/ppermute | solution.py:41
  289.5 9.5 %collective-permute-start.28 = (bf16[128,1536]{1,0:T(8,128)(2,1)S(1)}, bf16[128,1536]{1,0:T(8,128)(2,1)S(1)}, u32[]{:S(2)}, u32[]{:S(2)}) collective-permute-start(bf16[128,1536]{1,0:T(8,128)(2,1)S(1)} %get-tuple-element.88), channel_id=1, source_target_pairs={{64,128},{73,137},{80,144},{89,153},{96,160},{105,169},{112,176},{... | collective-permute-start | bytes 1179656 | tf_op jit(solution)/shard_map/ppermute | solution.py:41
  308.8 10.5 %collective-permute-start.29 = (bf16[128,1536]{1,0:T(8,128)(2,1)S(1)}, bf16[128,1536]{1,0:T(8,128)(2,1)S(1)}, u32[]{:S(2)}, u32[]{:S(2)}) collective-permute-start(bf16[128,1536]{1,0:T(8,128)(2,1)S(1)} %get-tuple-element.89), channel_id=1, source_target_pairs={{128,192},{137,201},{144,208},{153,217},{160,224},{169,233},{176,2... | collective-permute-start | bytes 1179656 | tf_op jit(solution)/shard_map/ppermute | solution.py:41
  309.5 12.1 %collective-permute-start.30 = (bf16[128,1536]{1,0:T(8,128)(2,1)S(1)}, bf16[128,1536]{1,0:T(8,128)(2,1)S(1)}, u32[]{:S(2)}, u32[]{:S(2)}) collective-permute-start(bf16[128,1536]{1,0:T(8,128)(2,1)S(1)} %get-tuple-element.90.refs_10_), channel_id=1, source_target_pairs={{128,192},{137,201},{144,208},{153,217},{160,224},{169,233},{176,2... | collective-permute-start | bytes 1179656 | tf_op jit(solution)/shard_map/ppermute | solution.py:41
  318.6 7.5 %collective-permute-start.32 = (bf16[128,1536]{1,0:T(8,128)(2,1)S(1)}, bf16[128,1536]{1,0:T(8,128)(2,1)S(1)}, u32[]{:S(2)}, u32[]{:S(2)}) collective-permute-start(bf16[128,1536]{1,0:T(8,128)(2,1)S(1)} %get-tuple-element.92), channel_id=1, source_target_pairs={{128,192},{137,201},{144,208},{153,217},{160,224},{169,233},{176,2... | collective-permute-start | bytes 1179656 | tf_op jit(solution)/shard_map/ppermute | solution.py:41
  347.7 23.9 %all-to-all-start.4 = ((f32[32,8,128]{2,1,0:T(8,128)}), f32[32,8,128]{2,1,0:T(8,128)S(1)}, u32[]{:S(2)}, u32[]{:S(2)}) async-start(f32[32,8,128]{2,1,0:T(8,128)} %select_bitcast_fusion), calls=%async_computation.4 | async-start | bytes 262144 | tf_op jit(solution)/shard_map/all_to_all | solution.py:467
  (14 other events, 141.5 us)

commit v5 on v4

--- a/solution.py
+++ b/solution.py
@@ -18,7 +18,7 @@
 F32 = jnp.float32
 VMEM = 20 * 1024 * 1024
 SPAN = 768
-CALLS = ((128, 128), (128, 128))
+CALLS = ((256,), (128, 128))
 CHUNKS = sum(CALLS, ())
 
 epsilon = 1e-06

time: 378 us -> 369 us (0.976)
  starting transfers between devices: 74.3 us -> 67.8 us
    ppermute x34 -> x28, starting transfers between devices: 38.9 us -> 32.9 us  [move(): return lax.ppermute(value, AXES, [(flat(*a), flat(*b)) for a, b in pairs])]
    pallas_call x33 -> x25, Pallas kernels: 74.8 us -> 72.4 us  [product(): pl.pallas_call(functools.partial(product_kernel, pieces=len(rows), column...]
    ppermute x34 -> x28, waiting for transfers between devices: 22.2 us -> 22.9 us  [move(): return lax.ppermute(value, AXES, [(flat(*a), flat(*b)) for a, b in pairs])]
  transfers between devices with their start and end apart: 38 -> 32, of which waited for: 13 -> 13; matrix products, arithmetic and copies ran while one was open for 1% -> 1% of each run, Pallas kernels for 27% -> 28%
where the time goes in v5:
time: 369 us; the launch traced here: 364 us
  Pallas kernels  205 us (56%)
  starting transfers between devices  67.8 us (18%)
  waiting for transfers between devices  57.8 us (16%)
  blocking collectives  17.6 us (5%)
  local copies, waits for them, and re-layouts  7.71 us (2%)
  other arithmetic  4.28 us (1%)
    pallas_call x16, Pallas kernels, attention(): pl.pallas_call(functools.partial(attention_kernel, queries=queries, block...  121 us
    pallas_call x25, Pallas kernels, product(): pl.pallas_call(functools.partial(product_kernel, pieces=len(rows), column...  72.4 us
    ppermute x28, starting transfers between devices, move(): return lax.ppermute(value, AXES, [(flat(*a), flat(*b)) for a, b in pairs])  32.9 us
    ppermute x28, waiting for transfers between devices, move(): return lax.ppermute(value, AXES, [(flat(*a), flat(*b)) for a, b in pairs])  22.9 us
    all_to_all x2, waiting for transfers between devices, on_device(): lax.all_to_all(message, 'z', split_axis=0, concat_axis=0, tiled=True)  20.4 us
    all_to_all x1, blocking collectives, on_device(): lax.all_to_all(message, 'y', split_axis=0, concat_axis=0, tiled=True)  17.6 us
    all_to_all x2, starting transfers between devices, on_device(): lax.all_to_all(message, 'z', split_axis=0, concat_axis=0, tiled=True)  14.2 us
    all_to_all x1, starting transfers between devices, on_device(): lax.all_to_all(latent.reshape(Z * Y, rows_here * latent_width // 128, 128...  12.9 us
  transfers between devices with their start and end apart: 32, of which 13 were waited for; matrix products, arithmetic and copies ran while one was open for 1% of the time, Pallas kernels for 28%

profile of v5, /device:TPU:2, one launch (start us, length us, event | category | flops | bytes accessed | tf_op | source)
XLA Modules:
  0.0 363.6 jit_solution(8628348107862555205)
XLA Ops:
  2.4 17.6 %all_to_all.25 = bf16[4,66,1536]{2,1,0:T(8,128)(2,1)S(1)} all-to-all(bf16[4,66,1536]{2,1,0:T(8,128)(2,1)S(1)} %pad_maximum_fusion), channel_id=1, replica_groups=mesh['x'=4,'z'=8,'y'=4,'c'=2] {'y'}, dimensions={0} | all-to-all | bytes 1622016 | tf_op jit(solution)/shard_map/all_to_all | solution.py:380
  23.0 10.8 %all-to-all-start.1 = ((bf16[8,16,1536]{2,1,0:T(8,128)(2,1)}), bf16[8,16,1536]{2,1,0:T(8,128)(2,1)S(1)}, u32[]{:S(2)}, u32[]{:S(2)}) async-start(bf16[8,16,1536]{2,1,0:T(8,128)(2,1)} %pad_maximum_fusion.1), calls=%async_computation.1 | async-start | bytes 786432 | tf_op jit(solution)/shard_map/all_to_all | solution.py:387
  38.7 11.1 %all-to-all-done.1.parts_ref = bf16[8,16,1536]{2,1,0:T(8,128)(2,1)S(1)} async-done(((bf16[8,16,1536]{2,1,0:T(8,128)(2,1)}), bf16[8,16,1536]{2,1,0:T(8,128)(2,1)S(1)}, u32[]{:S(2)}, u32[]{:S(2)}) %all-to-all-start.1) | async-done | bytes 393248 | tf_op jit(solution)/shard_map/all_to_all | solution.py:387
  52.4 7.8 %all-to-all-start.2 = ((bf16[4,8,1536]{2,1,0:T(8,128)(2,1)}), bf16[4,8,1536]{2,1,0:T(8,128)(2,1)S(1)}, u32[]{:S(2)}, u32[]{:S(2)}) async-start(bf16[4,8,1536]{2,1,0:T(8,128)(2,1)} %spread.1), calls=%async_computation.2 | async-start | bytes 196608 | tf_op jit(solution)/shard_map/all_to_all | solution.py:407
  70.5 9.2 %all-to-all-done.3 = bf16[8,8,1536]{2,1,0:T(8,128)(2,1)S(1)} async-done(((bf16[8,8,1536]{2,1,0:T(8,128)(2,1)}), bf16[8,8,1536]{2,1,0:T(8,128)(2,1)S(1)}, u32[]{:S(2)}, u32[]{:S(2)}) %all-to-all-start.3) | async-done | bytes 196640 | tf_op jit(solution)/shard_map/all_to_all | solution.py:410
  94.0 4.2 %product.25.refs_4_.refs_0_ = bf16[256,4608]{1,0:T(8,128)(2,1)S(1)} custom-call(bf16[256,1536]{1,0:T(8,128)(2,1)S(1)} %get-tuple-element.35.refs_0_.refs_7_, bf16[1536,4608]{1,0:T(8,128)(2,1)S(1)} %joined.2.refs_1_.refs_4_, f32[1,1536]{1,0:T(1,128)S(1)} %get-tuple-element.68.refs_6_.refs_2_.refs_5_, f32[1,1536]{1,0:T(1,128)S(1)} %get-tuple-element.66.refs_8_.refs_3_.refs_7_), custom_call_target="tpu_custom_call" | custom-call | flops 3623878656 | bytes 2097152 | tf_op jit(solution)/shard_map/product/pallas_call | solution.py:131
  105.4 7.6 %attention.16.refs_9_ = bf16[256,1536]{1,0:T(8,128)(2,1)S(1)} custom-call(bf16[256,4608]{1,0:T(8,128)(2,1)S(1)} %product.25.refs_4_.refs_0_, bf16[128,4608]{1,0:T(8,128)(2,1)S(1)} %product.26.refs_4_.refs_1_, bf16[128,4608]{1,0:T(8,128)(2,1)S(1)} %product.27.refs_2_, bf16[256,3072]{1,0:T(8,128)(2,1)S(1)} %product.28.refs_3_, ...), custom_call_target="tpu_custom_call" | custom-call | flops 2415919104 | bytes 8388608 | tf_op jit(solution)/shard_map/attention/pallas_call | solution.py:310
  114.8 7.5 %attention.17 = (bf16[128,1536]{1,0:T(8,128)(2,1)S(1)}, bf16[128,1536]{1,0:T(8,128)(2,1)S(1)}) custom-call(bf16[256,4608]{1,0:T(8,128)(2,1)S(1)} %product.25.refs_4_.refs_0_, bf16[128,4608]{1,0:T(8,128)(2,1)S(1)} %product.26.refs_4_.refs_1_, bf16[128,4608]{1,0:T(8,128)(2,1)S(1)} %product.27.refs_2_, bf16[256,3072]{1,0:T(8,128)(2,1)S(1)} %product.28.refs_3_, ...), custom_call_target="tpu_custom_call" | custom-call | flops 2415919104 | bytes 8388608 | tf_op jit(solution)/shard_map/attention/pallas_call | solution.py:310
  126.8 4.2 %product.29.refs_4_.refs_0_ = bf16[256,4608]{1,0:T(8,128)(2,1)S(1)} custom-call(bf16[256,1536]{1,0:T(8,128)(2,1)S(1)} %collective-permute-done.8.refs_0_.refs_7_, bf16[1536,4608]{1,0:T(8,128)(2,1)S(1)} %joined.2.refs_1_.refs_4_, f32[1,1536]{1,0:T(1,128)S(1)} %get-tuple-element.68.refs_6_.refs_2_.refs_5_, f32[1,1536]{1,0:T(1,128)S(1)} %get-tuple-element.66.refs_8_.refs_3_.refs_7_), custom_call_target="tpu_custom_call" | custom-call | flops 3623878656 | bytes 2097152 | tf_op jit(solution)/shard_map/product/pallas_call | solution.py:131
  138.5 7.6 %attention.18.refs_9_ = bf16[256,1536]{1,0:T(8,128)(2,1)S(1)} custom-call(bf16[256,4608]{1,0:T(8,128)(2,1)S(1)} %product.29.refs_4_.refs_0_, bf16[128,4608]{1,0:T(8,128)(2,1)S(1)} %product.30.refs_4_.refs_1_, bf16[128,4608]{1,0:T(8,128)(2,1)S(1)} %product.31.refs_2_, bf16[256,3072]{1,0:T(8,128)(2,1)S(1)} %product.28.refs_3_, ...), custom_call_target="tpu_custom_call" | custom-call | flops 2415919104 | bytes 8388608 | tf_op jit(solution)/shard_map/attention/pallas_call | solution.py:310
  147.6 7.5 %attention.19 = (bf16[128,1536]{1,0:T(8,128)(2,1)S(1)}, bf16[128,1536]{1,0:T(8,128)(2,1)S(1)}) custom-call(bf16[256,4608]{1,0:T(8,128)(2,1)S(1)} %product.29.refs_4_.refs_0_, bf16[128,4608]{1,0:T(8,128)(2,1)S(1)} %product.30.refs_4_.refs_1_, bf16[128,4608]{1,0:T(8,128)(2,1)S(1)} %product.31.refs_2_, bf16[256,3072]{1,0:T(8,128)(2,1)S(1)} %product.28.refs_3_, ...), custom_call_target="tpu_custom_call" | custom-call | flops 2415919104 | bytes 8388608 | tf_op jit(solution)/shard_map/attention/pallas_call | solution.py:310
  157.8 4.2 %product.32.refs_4_.refs_0_ = bf16[256,4608]{1,0:T(8,128)(2,1)S(1)} custom-call(bf16[256,1536]{1,0:T(8,128)(2,1)S(1)} %collective-permute-done.11.refs_0_.refs_7_, bf16[1536,4608]{1,0:T(8,128)(2,1)S(1)} %joined.2.refs_1_.refs_4_, f32[1,1536]{1,0:T(1,128)S(1)} %get-tuple-element.68.refs_6_.refs_2_.refs_5_, f32[1,1536]{1,0:T(1,128)S(1)} %get-tuple-element.66.refs_8_.refs_3_.refs_7_), custom_call_target="tpu_custom_call" | custom-call | flops 3623878656 | bytes 2097152 | tf_op jit(solution)/shard_map/product/pallas_call | solution.py:131
  168.2 7.6 %attention.20.refs_9_ = bf16[256,1536]{1,0:T(8,128)(2,1)S(1)} custom-call(bf16[256,4608]{1,0:T(8,128)(2,1)S(1)} %product.32.refs_4_.refs_0_, bf16[128,4608]{1,0:T(8,128)(2,1)S(1)} %product.33.refs_4_.refs_1_, bf16[128,4608]{1,0:T(8,128)(2,1)S(1)} %product.34.refs_2_, bf16[256,3072]{1,0:T(8,128)(2,1)S(1)} %product.28.refs_3_, ...), custom_call_target="tpu_custom_call" | custom-call | flops 2415919104 | bytes 8388608 | tf_op jit(solution)/shard_map/attention/pallas_call | solution.py:310
  176.9 7.5 %attention.21 = (bf16[128,1536]{1,0:T(8,128)(2,1)S(1)}, bf16[128,1536]{1,0:T(8,128)(2,1)S(1)}) custom-call(bf16[256,4608]{1,0:T(8,128)(2,1)S(1)} %product.32.refs_4_.refs_0_, bf16[128,4608]{1,0:T(8,128)(2,1)S(1)} %product.33.refs_4_.refs_1_, bf16[128,4608]{1,0:T(8,128)(2,1)S(1)} %product.34.refs_2_, bf16[256,3072]{1,0:T(8,128)(2,1)S(1)} %product.28.refs_3_, ...), custom_call_target="tpu_custom_call" | custom-call | flops 2415919104 | bytes 8388608 | tf_op jit(solution)/shard_map/attention/pallas_call | solution.py:310
  185.9 4.2 %product.35.refs_4_.refs_0_ = bf16[256,4608]{1,0:T(8,128)(2,1)S(1)} custom-call(bf16[256,1536]{1,0:T(8,128)(2,1)S(1)} %collective-permute-done.14.refs_0_.refs_7_, bf16[1536,4608]{1,0:T(8,128)(2,1)S(1)} %joined.2.refs_1_.refs_4_, f32[1,1536]{1,0:T(1,128)S(1)} %get-tuple-element.68.refs_6_.refs_2_.refs_5_, f32[1,1536]{1,0:T(1,128)S(1)} %get-tuple-element.66.refs_8_.refs_3_.refs_7_), custom_call_target="tpu_custom_call" | custom-call | flops 3623878656 | bytes 2097152 | tf_op jit(solution)/shard_map/product/pallas_call | solution.py:131
  194.7 7.6 %attention.22.refs_9_.refs_0_ = bf16[256,1536]{1,0:T(8,128)(2,1)S(1)} custom-call(bf16[256,4608]{1,0:T(8,128)(2,1)S(1)} %product.35.refs_4_.refs_0_, bf16[128,4608]{1,0:T(8,128)(2,1)S(1)} %product.36.refs_4_.refs_1_, bf16[128,4608]{1,0:T(8,128)(2,1)S(1)} %product.37.refs_2_, bf16[256,3072]{1,0:T(8,128)(2,1)S(1)} %product.28.refs_3_, ...), custom_call_target="tpu_custom_call" | custom-call | flops 2415919104 | bytes 8388608 | tf_op jit(solution)/shard_map/attention/pallas_call | solution.py:310
  202.2 7.5 %attention.23 = (bf16[128,1536]{1,0:T(8,128)(2,1)S(1)}, bf16[128,1536]{1,0:T(8,128)(2,1)S(1)}) custom-call(bf16[256,4608]{1,0:T(8,128)(2,1)S(1)} %product.35.refs_4_.refs_0_, bf16[128,4608]{1,0:T(8,128)(2,1)S(1)} %product.36.refs_4_.refs_1_, bf16[128,4608]{1,0:T(8,128)(2,1)S(1)} %product.37.refs_2_, bf16[256,3072]{1,0:T(8,128)(2,1)S(1)} %product.28.refs_3_, ...), custom_call_target="tpu_custom_call" | custom-call | flops 2415919104 | bytes 8388608 | tf_op jit(solution)/shard_map/attention/pallas_call | solution.py:310
  213.0 4.2 %product.38.refs_4_.refs_0_ = bf16[256,4608]{1,0:T(8,128)(2,1)S(1)} custom-call(bf16[256,1536]{1,0:T(8,128)(2,1)S(1)} %get-tuple-element.50.refs_0_.refs_7_, bf16[1536,4608]{1,0:T(8,128)(2,1)S(1)} %joined.2.refs_1_.refs_4_, f32[1,1536]{1,0:T(1,128)S(1)} %get-tuple-element.67.refs_7_.refs_6_.refs_2_, f32[1,1536]{1,0:T(1,128)S(1)} %get-tuple-element.65.refs_9_.refs_8_.refs_3_), custom_call_target="tpu_custom_call" | custom-call | flops 3623878656 | bytes 2097152 | tf_op jit(solution)/shard_map/product/pallas_call | solution.py:131
  221.7 7.6 %attention.24.refs_9_ = bf16[256,1536]{1,0:T(8,128)(2,1)S(1)} custom-call(bf16[256,4608]{1,0:T(8,128)(2,1)S(1)} %product.38.refs_4_.refs_0_, bf16[128,4608]{1,0:T(8,128)(2,1)S(1)} %product.39.refs_4_.refs_1_, bf16[128,4608]{1,0:T(8,128)(2,1)S(1)} %product.40.refs_2_, bf16[256,3072]{1,0:T(8,128)(2,1)S(1)} %product.28.refs_3_, ...), custom_call_target="tpu_custom_call" | custom-call | flops 2415919104 | bytes 8388608 | tf_op jit(solution)/shard_map/attention/pallas_call | solution.py:310
  230.6 7.6 %attention.25 = (bf16[128,1536]{1,0:T(8,128)(2,1)S(1)}, bf16[128,1536]{1,0:T(8,128)(2,1)S(1)}) custom-call(bf16[256,4608]{1,0:T(8,128)(2,1)S(1)} %product.38.refs_4_.refs_0_, bf16[128,4608]{1,0:T(8,128)(2,1)S(1)} %product.39.refs_4_.refs_1_, bf16[128,4608]{1,0:T(8,128)(2,1)S(1)} %product.40.refs_2_, bf16[256,3072]{1,0:T(8,128)(2,1)S(1)} %product.28.refs_3_, ...), custom_call_target="tpu_custom_call" | custom-call | flops 2415919104 | bytes 8388608 | tf_op jit(solution)/shard_map/attention/pallas_call | solution.py:310
  241.0 11.9 %collective-permute-done.18.refs_0_.refs_7_ = bf16[256,1536]{1,0:T(8,128)(2,1)S(1)} collective-permute-done((bf16[256,1536]{1,0:T(8,128)(2,1)S(1)}, bf16[256,1536]{1,0:T(8,128)(2,1)S(1)}, u32[]{:S(2)}, u32[]{:S(2)}) %collective-permute-start.18) | collective-permute-done | bytes 786464 | tf_op jit(solution)/shard_map/ppermute | solution.py:41
  252.9 4.2 %product.41.refs_4_.refs_0_ = bf16[256,4608]{1,0:T(8,128)(2,1)S(1)} custom-call(bf16[256,1536]{1,0:T(8,128)(2,1)S(1)} %collective-permute-done.18.refs_0_.refs_7_, bf16[1536,4608]{1,0:T(8,128)(2,1)S(1)} %joined.2.refs_1_.refs_4_, f32[1,1536]{1,0:T(1,128)S(1)} %get-tuple-element.67.refs_7_.refs_6_.refs_2_, f32[1,1536]{1,0:T(1,128)S(1)} %get-tuple-element.65.refs_9_.refs_8_.refs_3_), custom_call_target="tpu_custom_call" | custom-call | flops 3623878656 | bytes 2097152 | tf_op jit(solution)/shard_map/product/pallas_call | solution.py:131
  264.3 7.6 %attention.26.refs_9_ = bf16[256,1536]{1,0:T(8,128)(2,1)S(1)} custom-call(bf16[256,4608]{1,0:T(8,128)(2,1)S(1)} %product.41.refs_4_.refs_0_, bf16[128,4608]{1,0:T(8,128)(2,1)S(1)} %product.42.refs_4_.refs_1_, bf16[128,4608]{1,0:T(8,128)(2,1)S(1)} %product.43.refs_2_, bf16[256,3072]{1,0:T(8,128)(2,1)S(1)} %product.28.refs_3_, ...), custom_call_target="tpu_custom_call" | custom-call | flops 2415919104 | bytes 8388608 | tf_op jit(solution)/shard_map/attention/pallas_call | solution.py:310
  273.2 7.6 %attention.27 = (bf16[128,1536]{1,0:T(8,128)(2,1)S(1)}, bf16[128,1536]{1,0:T(8,128)(2,1)S(1)}) custom-call(bf16[256,4608]{1,0:T(8,128)(2,1)S(1)} %product.41.refs_4_.refs_0_, bf16[128,4608]{1,0:T(8,128)(2,1)S(1)} %product.42.refs_4_.refs_1_, bf16[128,4608]{1,0:T(8,128)(2,1)S(1)} %product.43.refs_2_, bf16[256,3072]{1,0:T(8,128)(2,1)S(1)} %product.28.refs_3_, ...), custom_call_target="tpu_custom_call" | custom-call | flops 2415919104 | bytes 8388608 | tf_op jit(solution)/shard_map/attention/pallas_call | solution.py:310
  283.9 4.2 %product.44.refs_4_.refs_0_ = bf16[256,4608]{1,0:T(8,128)(2,1)S(1)} custom-call(bf16[256,1536]{1,0:T(8,128)(2,1)S(1)} %collective-permute-done.21.refs_0_.refs_7_, bf16[1536,4608]{1,0:T(8,128)(2,1)S(1)} %joined.2.refs_1_.refs_4_, f32[1,1536]{1,0:T(1,128)S(1)} %get-tuple-element.67.refs_7_.refs_6_.refs_2_, f32[1,1536]{1,0:T(1,128)S(1)} %get-tuple-element.65.refs_9_.refs_8_.refs_3_), custom_call_target="tpu_custom_call" | custom-call | flops 3623878656 | bytes 2097152 | tf_op jit(solution)/shard_map/product/pallas_call | solution.py:131
  293.8 7.6 %attention.28.refs_9_ = bf16[256,1536]{1,0:T(8,128)(2,1)S(1)} custom-call(bf16[256,4608]{1,0:T(8,128)(2,1)S(1)} %product.44.refs_4_.refs_0_, bf16[128,4608]{1,0:T(8,128)(2,1)S(1)} %product.45.refs_4_.refs_1_, bf16[128,4608]{1,0:T(8,128)(2,1)S(1)} %product.46.refs_2_, bf16[256,3072]{1,0:T(8,128)(2,1)S(1)} %product.28.refs_3_, ...), custom_call_target="tpu_custom_call" | custom-call | flops 2415919104 | bytes 8388608 | tf_op jit(solution)/shard_map/attention/pallas_call | solution.py:310
  302.1 7.6 %attention.29 = (bf16[128,1536]{1,0:T(8,128)(2,1)S(1)}, bf16[128,1536]{1,0:T(8,128)(2,1)S(1)}) custom-call(bf16[256,4608]{1,0:T(8,128)(2,1)S(1)} %product.44.refs_4_.refs_0_, bf16[128,4608]{1,0:T(8,128)(2,1)S(1)} %product.45.refs_4_.refs_1_, bf16[128,4608]{1,0:T(8,128)(2,1)S(1)} %product.46.refs_2_, bf16[256,3072]{1,0:T(8,128)(2,1)S(1)} %product.28.refs_3_, ...), custom_call_target="tpu_custom_call" | custom-call | flops 2415919104 | bytes 8388608 | tf_op jit(solution)/shard_map/attention/pallas_call | solution.py:310
  311.3 4.2 %product.47.refs_4_.refs_0_ = bf16[256,4608]{1,0:T(8,128)(2,1)S(1)} custom-call(bf16[256,1536]{1,0:T(8,128)(2,1)S(1)} %collective-permute-done.24.refs_0_.refs_7_, bf16[1536,4608]{1,0:T(8,128)(2,1)S(1)} %joined.2.refs_1_.refs_4_, f32[1,1536]{1,0:T(1,128)S(1)} %get-tuple-element.67.refs_7_.refs_6_.refs_2_, f32[1,1536]{1,0:T(1,128)S(1)} %get-tuple-element.65.refs_9_.refs_8_.refs_3_), custom_call_target="tpu_custom_call" | custom-call | flops 3623878656 | bytes 2097152 | tf_op jit(solution)/shard_map/product/pallas_call | solution.py:131
  320.1 7.8 %attention.30.refs_9_.refs_0_ = bf16[256,1536]{1,0:T(8,128)(2,1)S(1)} custom-call(bf16[256,4608]{1,0:T(8,128)(2,1)S(1)} %product.47.refs_4_.refs_0_, bf16[128,4608]{1,0:T(8,128)(2,1)S(1)} %product.48.refs_4_.refs_1_, bf16[128,4608]{1,0:T(8,128)(2,1)S(1)} %product.49.refs_2_, bf16[256,3072]{1,0:T(8,128)(2,1)S(1)} %product.28.refs_3_, ...), custom_call_target="tpu_custom_call" | custom-call | flops 2415919104 | bytes 8388608 | tf_op jit(solution)/shard_map/attention/pallas_call | solution.py:310
  327.8 7.5 %attention.31 = (bf16[128,1536]{1,0:T(8,128)(2,1)S(1)}, bf16[128,1536]{1,0:T(8,128)(2,1)S(1)}) custom-call(bf16[256,4608]{1,0:T(8,128)(2,1)S(1)} %product.47.refs_4_.refs_0_, bf16[128,4608]{1,0:T(8,128)(2,1)S(1)} %product.48.refs_4_.refs_1_, bf16[128,4608]{1,0:T(8,128)(2,1)S(1)} %product.49.refs_2_, bf16[256,3072]{1,0:T(8,128)(2,1)S(1)} %product.28.refs_3_, ...), custom_call_target="tpu_custom_call" | custom-call | flops 2415919104 | bytes 8388608 | tf_op jit(solution)/shard_map/attention/pallas_call | solution.py:310
  339.3 12.9 %all-to-all-start.4 = ((f32[32,8,128]{2,1,0:T(8,128)}), f32[32,8,128]{2,1,0:T(8,128)S(1)}, u32[]{:S(2)}, u32[]{:S(2)}) async-start(f32[32,8,128]{2,1,0:T(8,128)} %select_bitcast_fusion), calls=%async_computation.4 | async-start | bytes 262144 | tf_op jit(solution)/shard_map/all_to_all | solution.py:467
  352.2 10.5 %all-to-all-done.4 = f32[32,8,128]{2,1,0:T(8,128)S(1)} async-done(((f32[32,8,128]{2,1,0:T(8,128)}), f32[32,8,128]{2,1,0:T(8,128)S(1)}, u32[]{:S(2)}, u32[]{:S(2)}) %all-to-all-start.4) | async-done | bytes 131104 | tf_op jit(solution)/shard_map/all_to_all | solution.py:467
  (136 shorter events, 115.7 us)
Async XLA Ops:
  21.0 66.5 %collective-permute-start.1 = (bf16[768,4608]{1,0:T(8,128)(2,1)}, bf16[768,4608]{1,0:T(8,128)(2,1)}, u32[]{:S(2)}, u32[]{:S(2)}) collective-permute-start(bf16[768,4608]{1,0:T(8,128)(2,1)} %bitcast.32), channel_id=1, source_target_pairs={{1,0},{8,9},{17,16},{24,25},{33,32},{40,41},{49,48},{56,57},{65,64... | collective-permute-start | bytes 21233672 | tf_op jit(solution)/shard_map/ppermute | solution.py:41
  23.0 26.9 %all-to-all-start.1 = ((bf16[8,16,1536]{2,1,0:T(8,128)(2,1)}), bf16[8,16,1536]{2,1,0:T(8,128)(2,1)S(1)}, u32[]{:S(2)}, u32[]{:S(2)}) async-start(bf16[8,16,1536]{2,1,0:T(8,128)(2,1)} %pad_maximum_fusion.1), calls=%async_computation.1 | async-start | bytes 786432 | tf_op jit(solution)/shard_map/all_to_all | solution.py:387
  35.4 3.3 collective-permute-start.3
  50.2 10.1 %collective-permute-start = (bf16[256,128]{1,0:T(8,128)(2,1)S(1)}, bf16[256,128]{1,0:T(8,128)(2,1)S(1)}, u32[]{:S(2)}, u32[]{:S(2)}) collective-permute-start(bf16[256,128]{1,0:T(8,128)(2,1)S(1)} %squeeze.32), channel_id=1, source_target_pairs={{80,16},{89,25},{160,32},{169,41},{240,48},{249,57}} | collective-permute-start | bytes 196616 | tf_op jit(solution)/shard_map/ppermute | solution.py:41
  51.0 9.4 %collective-permute-start.2 = (bf16[2,256,128]{2,1,0:T(8,128)(2,1)S(1)}, bf16[2,256,128]{2,1,0:T(8,128)(2,1)S(1)}, u32[]{:S(2)}, u32[]{:S(2)}) collective-permute-start(bf16[2,256,128]{2,1,0:T(8,128)(2,1)S(1)} %reshape.145), channel_id=1, source_target_pairs={{0,192},{9,201},{80,208},{89,217},{160,224},{169,233}} | collective-permute-start | bytes 393224 | tf_op jit(solution)/shard_map/ppermute | solution.py:41
  52.4 12.2 %all-to-all-start.2 = ((bf16[4,8,1536]{2,1,0:T(8,128)(2,1)}), bf16[4,8,1536]{2,1,0:T(8,128)(2,1)S(1)}, u32[]{:S(2)}, u32[]{:S(2)}) async-start(bf16[4,8,1536]{2,1,0:T(8,128)(2,1)} %spread.1), calls=%async_computation.2 | async-start | bytes 196608 | tf_op jit(solution)/shard_map/all_to_all | solution.py:407
  65.3 18.7 %collective-permute-start.7 = (bf16[768,1536]{1,0:T(8,128)(2,1)}, bf16[768,1536]{1,0:T(8,128)(2,1)}, u32[]{:S(2)}, u32[]{:S(2)}) collective-permute-start(bf16[768,1536]{1,0:T(8,128)(2,1)} %bitcast.34), channel_id=1, source_target_pairs={{1,0},{8,9},{17,16},{24,25},{33,32},{40,41},{49,48},{56,57},{65,64... | collective-permute-start | bytes 7077896 | tf_op jit(solution)/shard_map/ppermute | solution.py:41
  66.6 13.2 %all-to-all-start.3 = ((bf16[8,8,1536]{2,1,0:T(8,128)(2,1)}), bf16[8,8,1536]{2,1,0:T(8,128)(2,1)S(1)}, u32[]{:S(2)}, u32[]{:S(2)}) async-start(bf16[8,8,1536]{2,1,0:T(8,128)(2,1)} %twice.1), calls=%async_computation.3 | async-start | bytes 393216 | tf_op jit(solution)/shard_map/all_to_all | solution.py:410
  79.7 23.0 %collective-permute-start.4 = (bf16[64,1536]{1,0:T(8,128)(2,1)S(1)}, bf16[64,1536]{1,0:T(8,128)(2,1)S(1)}, u32[]{:S(2)}, u32[]{:S(2)}) collective-permute-start(bf16[64,1536]{1,0:T(8,128)(2,1)S(1)} %bitcast.36), channel_id=1, source_target_pairs={{2,0},{11,9},{18,16},{27,25},{34,32},{43,41},{50,48},{59,57},{66,6... | collective-permute-start | bytes 589832 | tf_op jit(solution)/shard_map/ppermute | solution.py:41
  81.0 21.7 %collective-permute-start.5 = (bf16[64,1536]{1,0:T(8,128)(2,1)S(1)}, bf16[64,1536]{1,0:T(8,128)(2,1)S(1)}, u32[]{:S(2)}, u32[]{:S(2)}) collective-permute-start(bf16[64,1536]{1,0:T(8,128)(2,1)S(1)} %bitcast.37), channel_id=1, source_target_pairs={{4,0},{13,9},{20,16},{29,25},{36,32},{45,41},{52,48},{61,57},{68,6... | collective-permute-start | bytes 589832 | tf_op jit(solution)/shard_map/ppermute | solution.py:41
  82.3 20.4 %collective-permute-start.6 = (bf16[64,1536]{1,0:T(8,128)(2,1)S(1)}, bf16[64,1536]{1,0:T(8,128)(2,1)S(1)}, u32[]{:S(2)}, u32[]{:S(2)}) collective-permute-start(bf16[64,1536]{1,0:T(8,128)(2,1)S(1)} %bitcast.38), channel_id=1, source_target_pairs={{6,0},{15,9},{22,16},{31,25},{38,32},{47,41},{54,48},{63,57},{70,6... | collective-permute-start | bytes 589832 | tf_op jit(solution)/shard_map/ppermute | solution.py:41
  112.9 13.9 %collective-permute-start.8 = (bf16[256,1536]{1,0:T(8,128)(2,1)S(1)}, bf16[256,1536]{1,0:T(8,128)(2,1)S(1)}, u32[]{:S(2)}, u32[]{:S(2)}) collective-permute-start(bf16[256,1536]{1,0:T(8,128)(2,1)S(1)} %attention.16.refs_9_), channel_id=1, source_target_pairs={{0,64},{9,73},{16,80},{25,89},{32,96},{41,105},{48,112},{57,121}} | collective-permute-start | bytes 2359304 | tf_op jit(solution)/shard_map/ppermute | solution.py:41
  122.3 9.7 %collective-permute-start.9 = (bf16[128,1536]{1,0:T(8,128)(2,1)S(1)}, bf16[128,1536]{1,0:T(8,128)(2,1)S(1)}, u32[]{:S(2)}, u32[]{:S(2)}) collective-permute-start(bf16[128,1536]{1,0:T(8,128)(2,1)S(1)} %get-tuple-element.41), channel_id=1, source_target_pairs={{0,64},{9,73},{16,80},{25,89},{32,96},{41,105},{48,112},{57,121}} | collective-permute-start | bytes 1179656 | tf_op jit(solution)/shard_map/ppermute | solution.py:41
  123.6 12.6 %collective-permute-start.10 = (bf16[128,1536]{1,0:T(8,128)(2,1)S(1)}, bf16[128,1536]{1,0:T(8,128)(2,1)S(1)}, u32[]{:S(2)}, u32[]{:S(2)}) collective-permute-start(bf16[128,1536]{1,0:T(8,128)(2,1)S(1)} %get-tuple-element.42), channel_id=1, source_target_pairs={{0,64},{9,73},{16,80},{25,89},{32,96},{41,105},{48,112},{57,121}} | collective-permute-start | bytes 1179656 | tf_op jit(solution)/shard_map/ppermute | solution.py:41
  146.1 11.7 %collective-permute-start.11 = (bf16[256,1536]{1,0:T(8,128)(2,1)S(1)}, bf16[256,1536]{1,0:T(8,128)(2,1)S(1)}, u32[]{:S(2)}, u32[]{:S(2)}) collective-permute-start(bf16[256,1536]{1,0:T(8,128)(2,1)S(1)} %attention.18.refs_9_), channel_id=1, source_target_pairs={{64,128},{73,137},{80,144},{89,153},{96,160},{105,169},{112,176},{... | collective-permute-start | bytes 2359304 | tf_op jit(solution)/shard_map/ppermute | solution.py:41
  155.1 6.9 %collective-permute-start.12 = (bf16[128,1536]{1,0:T(8,128)(2,1)S(1)}, bf16[128,1536]{1,0:T(8,128)(2,1)S(1)}, u32[]{:S(2)}, u32[]{:S(2)}) collective-permute-start(bf16[128,1536]{1,0:T(8,128)(2,1)S(1)} %get-tuple-element.43), channel_id=1, source_target_pairs={{64,128},{73,137},{80,144},{89,153},{96,160},{105,169},{112,176},{... | collective-permute-start | bytes 1179656 | tf_op jit(solution)/shard_map/ppermute | solution.py:41
  156.5 9.5 %collective-permute-start.13 = (bf16[128,1536]{1,0:T(8,128)(2,1)S(1)}, bf16[128,1536]{1,0:T(8,128)(2,1)S(1)}, u32[]{:S(2)}, u32[]{:S(2)}) collective-permute-start(bf16[128,1536]{1,0:T(8,128)(2,1)S(1)} %get-tuple-element.44), channel_id=1, source_target_pairs={{64,128},{73,137},{80,144},{89,153},{96,160},{105,169},{112,176},{... | collective-permute-start | bytes 1179656 | tf_op jit(solution)/shard_map/ppermute | solution.py:41
  175.7 10.1 %collective-permute-start.14 = (bf16[256,1536]{1,0:T(8,128)(2,1)S(1)}, bf16[256,1536]{1,0:T(8,128)(2,1)S(1)}, u32[]{:S(2)}, u32[]{:S(2)}) collective-permute-start(bf16[256,1536]{1,0:T(8,128)(2,1)S(1)} %attention.20.refs_9_), channel_id=1, source_target_pairs={{128,192},{137,201},{144,208},{153,217},{160,224},{169,233},{176,2... | collective-permute-start | bytes 2359304 | tf_op jit(solution)/shard_map/ppermute | solution.py:41
  184.4 5.7 %collective-permute-start.15 = (bf16[128,1536]{1,0:T(8,128)(2,1)S(1)}, bf16[128,1536]{1,0:T(8,128)(2,1)S(1)}, u32[]{:S(2)}, u32[]{:S(2)}) collective-permute-start(bf16[128,1536]{1,0:T(8,128)(2,1)S(1)} %get-tuple-element.45), channel_id=1, source_target_pairs={{128,192},{137,201},{144,208},{153,217},{160,224},{169,233},{176,2... | collective-permute-start | bytes 1179656 | tf_op jit(solution)/shard_map/ppermute | solution.py:41
  185.2 7.2 %collective-permute-start.16 = (bf16[128,1536]{1,0:T(8,128)(2,1)S(1)}, bf16[128,1536]{1,0:T(8,128)(2,1)S(1)}, u32[]{:S(2)}, u32[]{:S(2)}) collective-permute-start(bf16[128,1536]{1,0:T(8,128)(2,1)S(1)} %get-tuple-element.46), channel_id=1, source_target_pairs={{128,192},{137,201},{144,208},{153,217},{160,224},{169,233},{176,2... | collective-permute-start | bytes 1179656 | tf_op jit(solution)/shard_map/ppermute | solution.py:41
  211.6 0.9 collective-permute-start.17
  229.3 23.6 %collective-permute-start.18 = (bf16[256,1536]{1,0:T(8,128)(2,1)S(1)}, bf16[256,1536]{1,0:T(8,128)(2,1)S(1)}, u32[]{:S(2)}, u32[]{:S(2)}) collective-permute-start(bf16[256,1536]{1,0:T(8,128)(2,1)S(1)} %attention.24.refs_9_), channel_id=1, source_target_pairs={{0,64},{9,73},{16,80},{25,89},{32,96},{41,105},{48,112},{57,121}} | collective-permute-start | bytes 2359304 | tf_op jit(solution)/shard_map/ppermute | solution.py:41
  238.1 19.7 %collective-permute-start.19 = (bf16[128,1536]{1,0:T(8,128)(2,1)S(1)}, bf16[128,1536]{1,0:T(8,128)(2,1)S(1)}, u32[]{:S(2)}, u32[]{:S(2)}) collective-permute-start(bf16[128,1536]{1,0:T(8,128)(2,1)S(1)} %get-tuple-element.53), channel_id=1, source_target_pairs={{0,64},{9,73},{16,80},{25,89},{32,96},{41,105},{48,112},{57,121}} | collective-permute-start | bytes 1179656 | tf_op jit(solution)/shard_map/ppermute | solution.py:41
  239.7 22.4 %collective-permute-start.20 = (bf16[128,1536]{1,0:T(8,128)(2,1)S(1)}, bf16[128,1536]{1,0:T(8,128)(2,1)S(1)}, u32[]{:S(2)}, u32[]{:S(2)}) collective-permute-start(bf16[128,1536]{1,0:T(8,128)(2,1)S(1)} %get-tuple-element.54), channel_id=1, source_target_pairs={{0,64},{9,73},{16,80},{25,89},{32,96},{41,105},{48,112},{57,121}} | collective-permute-start | bytes 1179656 | tf_op jit(solution)/shard_map/ppermute | solution.py:41
  271.9 12.0 %collective-permute-start.21 = (bf16[256,1536]{1,0:T(8,128)(2,1)S(1)}, bf16[256,1536]{1,0:T(8,128)(2,1)S(1)}, u32[]{:S(2)}, u32[]{:S(2)}) collective-permute-start(bf16[256,1536]{1,0:T(8,128)(2,1)S(1)} %attention.26.refs_9_), channel_id=1, source_target_pairs={{64,128},{73,137},{80,144},{89,153},{96,160},{105,169},{112,176},{... | collective-permute-start | bytes 2359304 | tf_op jit(solution)/shard_map/ppermute | solution.py:41
  280.8 7.3 %collective-permute-start.22 = (bf16[128,1536]{1,0:T(8,128)(2,1)S(1)}, bf16[128,1536]{1,0:T(8,128)(2,1)S(1)}, u32[]{:S(2)}, u32[]{:S(2)}) collective-permute-start(bf16[128,1536]{1,0:T(8,128)(2,1)S(1)} %get-tuple-element.55), channel_id=1, source_target_pairs={{64,128},{73,137},{80,144},{89,153},{96,160},{105,169},{112,176},{... | collective-permute-start | bytes 1179656 | tf_op jit(solution)/shard_map/ppermute | solution.py:41
  282.1 9.5 %collective-permute-start.23 = (bf16[128,1536]{1,0:T(8,128)(2,1)S(1)}, bf16[128,1536]{1,0:T(8,128)(2,1)S(1)}, u32[]{:S(2)}, u32[]{:S(2)}) collective-permute-start(bf16[128,1536]{1,0:T(8,128)(2,1)S(1)} %get-tuple-element.56), channel_id=1, source_target_pairs={{64,128},{73,137},{80,144},{89,153},{96,160},{105,169},{112,176},{... | collective-permute-start | bytes 1179656 | tf_op jit(solution)/shard_map/ppermute | solution.py:41
  301.4 9.8 %collective-permute-start.24 = (bf16[256,1536]{1,0:T(8,128)(2,1)S(1)}, bf16[256,1536]{1,0:T(8,128)(2,1)S(1)}, u32[]{:S(2)}, u32[]{:S(2)}) collective-permute-start(bf16[256,1536]{1,0:T(8,128)(2,1)S(1)} %attention.28.refs_9_), channel_id=1, source_target_pairs={{128,192},{137,201},{144,208},{153,217},{160,224},{169,233},{176,2... | collective-permute-start | bytes 2359304 | tf_op jit(solution)/shard_map/ppermute | solution.py:41
  309.7 5.8 %collective-permute-start.25 = (bf16[128,1536]{1,0:T(8,128)(2,1)S(1)}, bf16[128,1536]{1,0:T(8,128)(2,1)S(1)}, u32[]{:S(2)}, u32[]{:S(2)}) collective-permute-start(bf16[128,1536]{1,0:T(8,128)(2,1)S(1)} %get-tuple-element.57), channel_id=1, source_target_pairs={{128,192},{137,201},{144,208},{153,217},{160,224},{169,233},{176,2... | collective-permute-start | bytes 1179656 | tf_op jit(solution)/shard_map/ppermute | solution.py:41
  310.4 7.4 %collective-permute-start.26 = (bf16[128,1536]{1,0:T(8,128)(2,1)S(1)}, bf16[128,1536]{1,0:T(8,128)(2,1)S(1)}, u32[]{:S(2)}, u32[]{:S(2)}) collective-permute-start(bf16[128,1536]{1,0:T(8,128)(2,1)S(1)} %get-tuple-element.58), channel_id=1, source_target_pairs={{128,192},{137,201},{144,208},{153,217},{160,224},{169,233},{176,2... | collective-permute-start | bytes 1179656 | tf_op jit(solution)/shard_map/ppermute | solution.py:41
  337.9 0.7 collective-permute-start.27
  339.3 23.4 %all-to-all-start.4 = ((f32[32,8,128]{2,1,0:T(8,128)}), f32[32,8,128]{2,1,0:T(8,128)S(1)}, u32[]{:S(2)}, u32[]{:S(2)}) async-start(f32[32,8,128]{2,1,0:T(8,128)} %select_bitcast_fusion), calls=%async_computation.4 | async-start | bytes 262144 | tf_op jit(solution)/shard_map/all_to_all | solution.py:467
  (8 other events, 116.7 us)
